TPU v7x, 32 devices: a whole 2x2x4 slice. The times are simulated.
32 devices in a mesh: ctx: 16 (over z, y, x), head: 2 (over core).
Axes of the slice: x: 2, y: 2, z: 4, core: 2. Of those that a mesh axis runs over, the one named last changes fastest.
Arguments:
- queries: bfloat16 [16384, 4096], P(('ctx', 'head')), may hold values from -400 to 400
- key_states: bfloat16 [16384, 1024], P(('ctx', 'head')), may hold values from -5 to 5
- value_states: bfloat16 [16384, 1024], P(('ctx', 'head')), may hold values from -6 to 6
- selection: int32 [32, 8, 4], replicated, may hold values from -1 to 31, as said below
Outputs:
- attended: bfloat16 [16384, 4096], P(('ctx', 'head'))
Inputs may be any that keep to these rules, and one draw needn't show every extreme that they name: `selection`: column 0 of row b is b. Columns 1 to 3 name distinct blocks below b, or -1 where none is named. Take the rows of the 2 blocks of one ctx index c (rows c * 2 to c * 2 + 1) and the 4 key-value heads of one head index (heads h * 4 to h * 4 + 3): the named blocks among them that belong to other ctx indices (block // 2 != c) lie on distinct ctx indices, so at most one block is named from any other ctx index; in every draw some ctx index names one block from each of several others.
All inputs are finite; a program needn't handle non-finite values.
Results may differ from a plain program's by a relative error of at most 0.004.
Values may be sent and summed in bfloat16 or wider, within the bound.
No kernel may reach another device: no remote copies, remote signals or barrier semaphores. Data moves between devices by JAX's collectives and lax.ppermute only.
A program may use at most 128 MiB of HBM per device.

v0:
```python
import functools
import math

import jax
import jax.numpy as jnp
import numpy as np
from jax import lax
from jax.experimental import pallas as pl
from jax.experimental.pallas import tpu as pltpu
from jax.sharding import PartitionSpec as P

QH = 32
KVH = 8
HD = 128
BLK = 512
TOPK = 3
GROUP = QH // KVH
KVG = KVH // 2
WIDE = GROUP * HD
ROWS = GROUP * BLK
SCALE = math.log2(math.e) / math.sqrt(HD)
TILE = 128
VMEM = pltpu.VMEM
ANY = pl.ANY


def patterns(peers):
    fast = 4 if peers % 4 == 0 else 1
    slow = peers // fast
    if (fast, slow) == (4, 4):
        order = [(2, 0), (1, 0), (3, 0), (2, 1), (1, 1), (3, 1), (2, 2), (0, 1), (1, 2), (0, 2), (3, 2), (2, 3), (0, 3)]
        order += [(1, 3), (3, 3)]
        edges = [0, 3, 6, 10, 13, 15]
    else:
        far = sorted(range(1, slow), key=lambda d: -min(d, slow - d))
        order = [(d, m) for m in range(fast) for d in far] + [(0, m) for m in range(1, fast)]
        edges = [round(i * len(order) / 5) for i in range(6)]
    return fast, slow, order, list(zip(edges[:-1], edges[1:]))


def pairs_of(fast, slow, step, flip):
    pairs = []
    for s in range(slow - step):
        for f in range(fast):
            source, target = s * fast + f, (s + step) * fast + (f ^ flip)
            if target > source:
                pairs.append((source, target))
    return pairs


def scores_of(k, q):
    return lax.dot_general(k, q, (((1,), (1,)), ((), ())), preferred_element_type=jnp.float32)


def total_of(vt, weights):
    return jnp.dot(vt, weights.astype(jnp.bfloat16), preferred_element_type=jnp.float32)


def cut_kernel(fast, slow, order, meta, key, value, okey, ovalue, *rest):
    outs, sems = rest[:-1], rest[-1]
    me, side = meta[0], meta[1]
    s_me, f_me = me // fast, me % fast

    def each(act):
        for j, (step, flip) in enumerate(order):
            f_to = f_me ^ flip
            target = (s_me + step) * fast + f_to
            fine = jnp.logical_and(s_me + step < slow, target > me)
            code = jnp.where(fine, meta[2 + jnp.where(fine, target, 0)], 0) - 1
            block, head = code // KVH, code % KVH
            col = pl.multiple_of(jnp.maximum(head, 0) * HD, HD)
            for t, (here, there) in enumerate(((key, okey), (value, ovalue))):
                to = outs[j].at[pl.ds(t * BLK, BLK), :]
                mine = pltpu.make_async_copy(here.at[:, pl.ds(col, HD)], to, sems.at[j, t])
                other = pltpu.make_async_copy(there.at[:, pl.ds(col, HD)], to, sems.at[j, t])
                act(jnp.logical_and(code >= 0, block == side), mine)
                act(jnp.logical_and(code >= 0, block != side), other)

    def start(flag, copy):
        pl.when(flag)(copy.start)

    def wait(flag, copy):
        pl.when(flag)(copy.wait)

    each(start)
    each(wait)


def own_kernel(local_at, meta, q, k, v, ok, ov, acc_out, stat_out, out, vt):
    g = pl.program_id(0)
    vt[...] = v[...].T
    for r in range(BLK // TILE):
        keys, at = (r + 1) * TILE, slice(r * TILE, (r + 1) * TILE)
        row = lax.broadcasted_iota(jnp.int32, (keys, TILE), 1) + r * TILE
        mask = row >= lax.broadcasted_iota(jnp.int32, (keys, TILE), 0)
        for j in range(GROUP):
            scores = scores_of(k[:keys, :], q[at, j * HD : (j + 1) * HD])
            scores = jnp.where(mask, scores, -1e30)
            m = jnp.max(scores, axis=0, keepdims=True)
            weights = jnp.exp2((scores - m) * SCALE)
            stat_out[0, j : j + 1, at] = m
            stat_out[0, GROUP + j : GROUP + j + 1, at] = jnp.sum(weights, axis=0, keepdims=True)
            acc_out[0, j, :, at] = total_of(vt[:, :keys], weights)

    @pl.when(meta[local_at + g] > 0)
    def _():
        vt[...] = ov[...].T
        fold(ok, lambda at, col: q[at, col], vt, acc_out.at[0], stat_out.at[0])

    for j in range(GROUP):
        total = stat_out[0, GROUP + j : GROUP + j + 1, :]
        out[:, j * HD : (j + 1) * HD] = (acc_out[0, j] / total).T.astype(jnp.bfloat16)


def fold(k, q_of, vt, acc, stat):
    for j in range(GROUP):
        for r in range(BLK // TILE):
            at = slice(r * TILE, (r + 1) * TILE)
            scores = scores_of(k[...], q_of(at, slice(j * HD, (j + 1) * HD)))
            m_old = stat[j : j + 1, at]
            m = jnp.maximum(m_old, jnp.max(scores, axis=0, keepdims=True))
            weights = jnp.exp2((scores - m) * SCALE)
            alpha = jnp.exp2((m_old - m) * SCALE)
            total = GROUP + j
            stat[j : j + 1, at] = m
            stat[total : total + 1, at] = stat[total : total + 1, at] * alpha + jnp.sum(weights, axis=0, keepdims=True)
            acc[j, :, at] = acc[j, :, at] * alpha + total_of(vt[...], weights)


def far_kernel(n_here, n_swap, n_pass, here_at, here_later, swap_at, swap_later, meta, *refs):
    arrived, refs = refs[:n_here], refs[n_here:]
    swapped, refs = refs[:n_swap], refs[n_swap:]
    q_hbm, acc_hbm, stat_hbm = refs[:3]
    refs = refs[4 + n_pass :]
    acc_new, stat_new, out_new = refs[:3]
    qs, accs, stats, outs, kv, vt, seen, here, later, kv_sem, in_sem, out_sem = refs[3 + n_pass :]
    each = n_swap and swapped[0].shape[0] // (2 * BLK)
    pieces = n_here + n_swap * each

    def wide(g):
        return pl.ds(pl.multiple_of(g * WIDE, WIDE), WIDE)

    def loads(g):
        return (
            pltpu.make_async_copy(q_hbm.at[:, wide(g)], qs.at[g], in_sem.at[g, 0]),
            pltpu.make_async_copy(acc_hbm.at[g], accs.at[g], in_sem.at[g, 1]),
            pltpu.make_async_copy(stat_hbm.at[g], stats.at[g], in_sem.at[g, 2]),
        )

    def stores(g):
        return (
            pltpu.make_async_copy(accs.at[g], acc_new.at[g], out_sem.at[g, 0]),
            pltpu.make_async_copy(stats.at[g], stat_new.at[g], out_sem.at[g, 1]),
        )

    def finish(g):
        return pltpu.make_async_copy(outs.at[g], out_new.at[:, wide(g)], out_sem.at[g, 2])

    def head_of(i):
        return meta[jnp.where(i < n_here, here_at + i, swap_at + i - n_here)]

    for g in range(KVH):
        seen[g] = 0
        here[g] = 0
        later[g] = 0

    for i in range(pieces):
        g = meta[here_at + i] if i < n_here else meta[swap_at + i - n_here]
        block = arrived[i] if i < n_here else swapped[0].at[pl.ds((i - n_here) * 2 * BLK, 2 * BLK), :]

        @pl.when(g >= 0)
        def _():
            pltpu.make_async_copy(block, kv.at[i], kv_sem.at[i]).start()

            @pl.when(here[g] == 0)
            def _():
                for copy in loads(g):
                    copy.start()

            here[g] = here[g] + 1

    def count(i, carry):
        g = meta[i]

        @pl.when(g >= 0)
        def _():
            later[g] = later[g] + 1

        return carry

    lax.fori_loop(*here_later, count, 0)
    lax.fori_loop(*swap_later, count, 0)

    def piece(i, carry):
        g = head_of(i)

        @pl.when(g >= 0)
        def _():
            @pl.when(seen[g] == 0)
            def _():
                for copy in loads(g):
                    copy.wait()

            pltpu.make_async_copy(kv.at[i], kv.at[i], kv_sem.at[i]).wait()
            vt[...] = kv[i, BLK:, :].T
            fold(
                kv.at[i, pl.ds(0, BLK), :], lambda at, col: qs[g, at, col], vt, accs.at[g], stats.at[g]
            )
            seen[g] = seen[g] + 1
            done = seen[g] == here[g]

            @pl.when(jnp.logical_and(done, later[g] > 0))
            def _():
                for copy in stores(g):
                    copy.start()

            @pl.when(jnp.logical_and(done, later[g] == 0))
            def _():
                for j in range(GROUP):
                    outs[g, :, j * HD : (j + 1) * HD] = (
                        (accs[g, j] / stats[g, GROUP + j : GROUP + j + 1, :]).T.astype(jnp.bfloat16)
                    )
                finish(g).start()

        return carry

    lax.fori_loop(0, pieces, piece, 0)

    for g in range(KVH):
        used = here[g] > 0

        @pl.when(jnp.logical_and(used, later[g] > 0))
        def _():
            for copy in stores(g):
                copy.wait()

        @pl.when(jnp.logical_and(used, later[g] == 0))
        def _():
            finish(g).wait()


def pack_kernel(*refs):
    arrived, joined = refs[: (len(refs) - 3)], refs[-2]
    for i, x in enumerate(arrived):
        joined[i * 2 * BLK : (i + 1) * 2 * BLK, :] = x[...]


def body(queries, key, value, selection):
    me, side = lax.axis_index("ctx"), lax.axis_index("head")
    peers = lax.axis_size("ctx")
    fast, slow, order, groups = patterns(peers)
    steps = np.array([s for s, _ in order], np.int32)
    flips = np.array([f for _, f in order], np.int32)
    swap = [(0, 1), (1, 0)]
    okey, ovalue = lax.ppermute(key, "head", swap), lax.ppermute(value, "head", swap)

    picks = selection[:, :, 1:]
    asked = lax.dynamic_slice_in_dim(picks, side * KVG, KVG, 1)
    codes = (asked - 2 * me) * KVH + (side * KVG + jnp.arange(KVG, dtype=jnp.int32))[None, :, None] + 1
    wanted = jnp.max(
        jnp.where((asked >> 1) == me, codes, 0).reshape(peers, 2 * KVG * TOPK), axis=1
    )
    mine = lax.dynamic_slice_in_dim(picks, 2 * me + side, 1, 0)[0]
    owners = jnp.where(mine >= 0, mine >> 1, -1)
    local = jnp.any(owners == me, axis=1).astype(jnp.int32)
    s_from = me // fast - steps
    source = jnp.where(s_from >= 0, s_from * fast + ((me % fast) ^ flips), me)
    source = jnp.where(source < me, source, -2)
    heads = jnp.arange(KVH, dtype=jnp.int32)
    hit = jnp.any(owners[None, :, :] == source[:, None, None], axis=2)
    near = (heads // KVG) == side
    work_here = jnp.max(jnp.where(hit & near, heads, -1), axis=1)
    work_swap = jnp.max(jnp.where(hit & ~near, heads, -1), axis=1)
    meta = jnp.concatenate([jnp.stack([me, side]).astype(jnp.int32), wanted, local, work_here, work_swap])
    local_at = 2 + peers
    here_at = local_at + KVH
    swap_at = here_at + len(order)
    end = swap_at + len(order)

    piece_shape = jax.ShapeDtypeStruct((2 * BLK, HD), jnp.bfloat16)
    any_spec, vmem_spec = pl.BlockSpec(memory_space=ANY), pl.BlockSpec(memory_space=VMEM)
    sent = pl.pallas_call(
        functools.partial(cut_kernel, fast, slow, order),
        grid_spec=pltpu.PrefetchScalarGridSpec(
            num_scalar_prefetch=1,
            grid=(),
            in_specs=[vmem_spec] * 4,
            out_specs=[any_spec] * len(order),
            scratch_shapes=[pltpu.SemaphoreType.DMA((len(order), 2))],
        ),
        out_shape=[piece_shape] * len(order),
        cost_estimate=pl.CostEstimate(flops=0, bytes_accessed=len(order) << 19, transcendentals=0),
        name="cut",
    )(meta, key, value, okey, ovalue)
    sent = list(sent)

    state = (
        jax.ShapeDtypeStruct((KVH, GROUP, HD, BLK), jnp.float32),
        jax.ShapeDtypeStruct((KVH, 2 * GROUP, BLK), jnp.float32),
        jax.ShapeDtypeStruct((BLK, QH * HD), jnp.bfloat16),
    )
    kv_spec = pl.BlockSpec((BLK, HD), lambda g, _: (0, g))
    q_spec = pl.BlockSpec((BLK, WIDE), lambda g, _: (0, g))
    piece_flops = 4 * ROWS * BLK * HD
    acc, stat, out = pl.pallas_call(
        functools.partial(own_kernel, local_at),
        grid_spec=pltpu.PrefetchScalarGridSpec(
            num_scalar_prefetch=1,
            grid=(KVH,),
            in_specs=[q_spec] + [kv_spec] * 4,
            out_specs=[
                pl.BlockSpec((1, GROUP, HD, BLK), lambda g, _: (g, 0, 0, 0)),
                pl.BlockSpec((1, 2 * GROUP, BLK), lambda g, _: (g, 0, 0)),
                q_spec,
            ],
            scratch_shapes=[VMEM((HD, BLK), jnp.bfloat16)],
        ),
        out_shape=state,
        compiler_params=pltpu.CompilerParams(vmem_limit_bytes=52 << 20),
        cost_estimate=pl.CostEstimate(
            flops=32 * piece_flops, bytes_accessed=28 << 20, transcendentals=12 * ROWS * BLK
        ),
        name="own",
    )(meta, queries, key, value, okey, ovalue)

    landed = [None] * len(order)
    swapped = []

    def send(n):
        a, b = groups[n]
        for j in range(a, b):
            landed[j] = lax.ppermute(sent[j], "ctx", pairs_of(fast, slow, *order[j]))

    send(0)
    send(1)
    count = len(groups)
    for n in range(count + 1):
        a, b = groups[n] if n < count else (len(order), len(order))
        a0, b0 = groups[n - 1] if n else (0, 0)
        late = range(*groups[n + 2]) if n + 2 < count else range(0)
        n_here, n_pass = b - a, len(late)
        pieces = n_here + b0 - a0
        if n < count:
            parts = landed[a:b]
            joined, stat = pl.pallas_call(
                pack_kernel,
                in_specs=[vmem_spec] * n_here + [any_spec],
                out_specs=[vmem_spec, any_spec],
                out_shape=(jax.ShapeDtypeStruct((n_here * 2 * BLK, HD), jnp.bfloat16), state[1]),
                input_output_aliases={n_here: 1},
                compiler_params=pltpu.CompilerParams(vmem_limit_bytes=52 << 20),
                cost_estimate=pl.CostEstimate(flops=0, bytes_accessed=n_here << 19, transcendentals=0),
                name="pack",
            )(*parts, stat)
            swapped.append(lax.ppermute(joined, "head", swap))
        others = [swapped[n - 1]] if n else []
        base = 1 + n_here + len(others)
        result = pl.pallas_call(
            functools.partial(
                far_kernel, n_here, len(others), n_pass,
                here_at + a, (here_at + b, swap_at), swap_at + a0, (swap_at + b0, end),
            ),
            grid_spec=pltpu.PrefetchScalarGridSpec(
                num_scalar_prefetch=1,
                grid=(),
                in_specs=[any_spec] * (base - 1 + 4 + n_pass),
                out_specs=[any_spec] * (3 + n_pass),
                scratch_shapes=[
                    VMEM((KVH, BLK, WIDE), jnp.bfloat16),
                    VMEM((KVH, GROUP, HD, BLK), jnp.float32),
                    VMEM((KVH, 2 * GROUP, BLK), jnp.float32),
                    VMEM((KVH, BLK, WIDE), jnp.bfloat16),
                    VMEM((pieces, 2 * BLK, HD), jnp.bfloat16),
                    VMEM((HD, BLK), jnp.bfloat16),
                    pltpu.SMEM((KVH,), jnp.int32),
                    pltpu.SMEM((KVH,), jnp.int32),
                    pltpu.SMEM((KVH,), jnp.int32),
                    pltpu.SemaphoreType.DMA((pieces,)),
                    pltpu.SemaphoreType.DMA((KVH, 3)),
                    pltpu.SemaphoreType.DMA((KVH, 3)),
                ],
            ),
            out_shape=(*state, *[piece_shape] * n_pass),
            input_output_aliases={base + 1 + i: i for i in range(3 + n_pass)},
            compiler_params=pltpu.CompilerParams(vmem_limit_bytes=52 << 20),
            cost_estimate=pl.CostEstimate(
                flops=8 * pieces * piece_flops, bytes_accessed=pieces << 21, transcendentals=pieces * ROWS * BLK
            ),
            name="far",
        )(meta, *landed[a:b], *others, queries, acc, stat, out, *[sent[j] for j in late])
        acc, stat, out = result[:3]
        for j, x in zip(late, result[3:]):
            sent[j] = x
        if late:
            send(n + 2)
    return out


def solution(mesh):
    placed = (P(("ctx", "head"), None), P(("ctx", "head"), None), P(("ctx", "head"), None), P())
    return jax.shard_map(
        body, mesh=mesh, in_specs=placed, out_specs=P(("ctx", "head"), None), check_vma=False
    )
```

profile of v0, /device:TPU:30, one launch (start us, length us, event | category | flops | bytes accessed | tf_op | source)
XLA Modules:
  0.0 131.9 jit_solution(4340530644810695913)
XLA Ops:
  0.0 0.0 collective-permute-start
  0.0 0.5 collective-permute-start.1
  0.5 0.7 slice.3
  1.2 0.3 compare_reduce_fusion
  1.6 0.1 copy.43
  1.7 0.1 select_reduce_fusion
  1.8 0.1 reduce_max.35
  1.8 0.1 reduce_max.36
  2.0 0.7 compare_select_fusion
  2.7 0.1 compare_reduce_fusion.1
  2.8 0.1 select_reduce_fusion.1
  2.8 0.7 concatenate.3.meta
  3.5 0.0 collective-permute-done.okey.ok
  3.5 0.9 collective-permute-done.1.ovalue.ov
  4.4 0.2 copy-done.11
  4.5 1.0 copy-done.12
  5.5 3.1 %cut.1 = (bf16[1024,128]{1,0:T(8,128)(2,1)}, bf16[1024,128]{1,0:T(8,128)(2,1)}, bf16[1024,128]{1,0:T(8,128)(2,1)}, bf16[1024,128]{1,0:T(8,128)(2,1)}, bf16[1024,...) custom-call(s32[56]{0:T(128)} %concatenate.3.meta, ...), custom_call_target="tpu_custom_call" | custom-call | bytes 7864320 | tf_op jit(solution)/shard_map/cut/pallas_call | solution.py:282
  8.6 1.3 collective-permute-start.2
  9.9 1.3 collective-permute-start.3
  11.2 1.3 collective-permute-start.4
  12.5 1.3 collective-permute-start.9
  13.9 1.4 %collective-permute-start.10 = (bf16[1024,128]{1,0:T(8,128)(2,1)}, bf16[1024,128]{1,0:T(8,128)(2,1)S(1)}, u32[]{:S(2)}, u32[]{:S(2)}) collective-permute-start(bf16[1024,128]{1,0:T(8,128)(2,1)} %get-tuple-element.74), channel_id=1, source_target_pairs={{0,10},{2,8},{4,14},{6,12},{8,18},{10,16},{12,22},{14,20},{16,26},... | collective-permute-start | bytes 786440 | tf_op jit(solution)/shard_map/ppermute | solution.py:332
  15.3 21.5 %own.1 = (f32[8,4,128,512]{3,2,1,0:T(8,128)}, f32[8,8,512]{2,1,0:T(8,128)S(1)}, bf16[512,4096]{1,0:T(8,128)(2,1)}) custom-call(s32[56]{0:T(128)S(1)} %copy-done.1, bf16[512,4096]{1,0:T(8,128)(2,1)} %refs_1_.1, bf16[512,1024]{1,0:T(8,128)(2,1)S(1)} %copy-done, bf16[512,1024]{1,0:T(8,128)(2,1)} %v.1, bf16[512,1024]{1,0:T(8,128)(2,1)} %copy-done.11, ...), custom_call_target="tpu_custom_call" | custom-call | flops 17179869184 | bytes 29360128 | tf_op jit(solution)/shard_map/own/pallas_call | solution.py:305
  36.9 0.0 collective-permute-done.2.refs_0_
  36.9 1.3 collective-permute-start.11
  38.2 0.0 collective-permute-done.3.refs_1_
  38.2 0.0 collective-permute-done.4.refs_2_
  38.2 0.1 pack.5
  38.3 14.0 %collective-permute-start.13 = (bf16[3072,128]{1,0:T(8,128)(2,1)S(1)}, bf16[3072,128]{1,0:T(8,128)(2,1)S(1)}, u32[]{:S(2)}, u32[]{:S(2)}) collective-permute-start(bf16[3072,128]{1,0:T(8,128)(2,1)S(1)} %get-tuple-element.78), channel_id=1, source_target_pairs={{0,1},{1,0},{2,3},{3,2},{4,5},{5,4},{6,7},{7,6},{8,9},{9,8},{10,11... | collective-permute-start | bytes 2359304 | tf_op jit(solution)/shard_map/ppermute | solution.py:355
  52.3 7.2 %far.6 = (f32[8,4,128,512]{3,2,1,0:T(8,128)}, f32[8,8,512]{2,1,0:T(8,128)S(1)}, bf16[512,4096]{1,0:T(8,128)(2,1)}, bf16[1024,128]{1,0:T(8,128)(2,1)S(1)}, bf16[1...) custom-call(s32[56]{0:T(128)S(1)} %copy-done.1, ...), custom_call_target="tpu_custom_call", output_to_operand_aliasing={{0}: (5, {}), {1}: (6, {}), {2}: (7, {}), {3}: (8, {}), {4}... | custom-call | flops 12884901888 | bytes 6291456 | tf_op jit(solution)/shard_map/far/pallas_call | solution.py:358
  59.5 1.3 collective-permute-start.5
  60.8 0.0 collective-permute-done.9.refs_0_
  60.8 1.3 collective-permute-start.6
  62.1 1.3 collective-permute-start.7
  63.4 1.3 collective-permute-start.8
  64.7 0.1 pack.6
  64.8 0.0 collective-permute-done.13.refs_3_
  64.8 0.9 collective-permute-start.12
  65.7 0.0 copy-done.13
  65.8 13.1 %far.7 = (f32[8,4,128,512]{3,2,1,0:T(8,128)}, f32[8,8,512]{2,1,0:T(8,128)S(1)}, bf16[512,4096]{1,0:T(8,128)(2,1)}, bf16[1024,128]{1,0:T(8,128)(2,1)S(1)}, bf16[1...) custom-call(s32[56]{0:T(128)S(1)} %copy-done.1, ...), custom_call_target="tpu_custom_call", output_to_operand_aliasing={{0}: (6, {}), {1}: (7, {}), {2}: (8, {}), {3}: (9, {}), {4}... | custom-call | flops 25769803776 | bytes 12582912 | tf_op jit(solution)/shard_map/far/pallas_call | solution.py:358
  78.9 0.0 collective-permute-done.5.refs_0_
  78.9 1.3 collective-permute-start.16
  80.2 1.3 collective-permute-start.17
  81.5 0.0 collective-permute-done.7.refs_2_
  81.5 1.3 collective-permute-start.18
  82.8 0.2 collective-permute-done.8.refs_3_
  83.0 1.1 pack.7
  84.1 0.1 collective-permute-start.19
  84.2 0.9 copy-done.14
  85.1 7.5 %far.8 = (f32[8,4,128,512]{3,2,1,0:T(8,128)}, f32[8,8,512]{2,1,0:T(8,128)S(1)}, bf16[512,4096]{1,0:T(8,128)(2,1)}, bf16[1024,128]{1,0:T(8,128)(2,1)S(1)}, bf16[1024,128]{1,0:T(8,128)(2,1)S(1)}) custom-call(s32[56]{0:T(128)S(1)} %copy-done.1, ...), custom_call_target="tpu_custom_call", output_to_operand_aliasing={{0}: (7, {}), {1}: (8, {}), {2}: (9, {}), {3}: (10, {}), {4... | custom-call | flops 30064771072 | bytes 14680064 | tf_op jit(solution)/shard_map/far/pallas_call | solution.py:358
  92.6 1.3 collective-permute-start.14
  93.9 0.0 collective-permute-done.16.refs_0_
  93.9 1.3 collective-permute-start.15
  95.2 5.9 %collective-permute-done.17.refs_1_ = bf16[1024,128]{1,0:T(8,128)(2,1)S(1)} collective-permute-done((bf16[1024,128]{1,0:T(8,128)(2,1)S(1)}, bf16[1024,128]{1,0:T(8,128)(2,1)S(1)}, u32[]{:S(2)}, u32[]{:S(2)}) %collective-permute-start.17) | collective-permute-done | bytes 262176 | tf_op jit(solution)/shard_map/ppermute | solution.py:332
  101.0 0.0 collective-permute-done.18.refs_2_
  101.0 0.1 pack.8
  101.1 0.1 collective-permute-start.21
  101.2 0.0 collective-permute-done.19.refs_3_
  101.2 9.4 %far.9 = (f32[8,4,128,512]{3,2,1,0:T(8,128)}, f32[8,8,512]{2,1,0:T(8,128)S(1)}, bf16[512,4096]{1,0:T(8,128)(2,1)}) custom-call(s32[56]{0:T(128)S(1)} %copy-done.1, bf16[1024,128]{1,0:T(8,128)(2,1)S(1)} %collective-permute-done.16.refs_0_, ...), custom_call_target="tpu_custom_call", output_to_operand_aliasing={{0}: (6, {}), {1}: (7, {}), {2}: (8, {})} | custom-call | flops 30064771072 | bytes 14680064 | tf_op jit(solution)/shard_map/far/pallas_call | solution.py:358
  110.6 2.9 %collective-permute-done.15.refs_1_ = bf16[1024,128]{1,0:T(8,128)(2,1)S(1)} collective-permute-done((bf16[1024,128]{1,0:T(8,128)(2,1)S(1)}, bf16[1024,128]{1,0:T(8,128)(2,1)S(1)}, u32[]{:S(2)}, u32[]{:S(2)}) %collective-permute-start.15) | collective-permute-done | bytes 262176 | tf_op jit(solution)/shard_map/ppermute | solution.py:332
  113.5 1.2 collective-permute-start.20
  114.8 0.0 collective-permute-done.21.refs_2_
  114.8 9.5 %far.10 = (f32[8,4,128,512]{3,2,1,0:T(8,128)}, f32[8,8,512]{2,1,0:T(8,128)S(1)}, bf16[512,4096]{1,0:T(8,128)(2,1)}) custom-call(s32[56]{0:T(128)S(1)} %copy-done.1, bf16[1024,128]{1,0:T(8,128)(2,1)S(1)} %collective-permute-done.14.refs_0_, ...), custom_call_target="tpu_custom_call", output_to_operand_aliasing={{0}: (5, {}), {1}: (6, {}), {2}: (7, {})} | custom-call | flops 21474836480 | bytes 10485760 | tf_op jit(solution)/shard_map/far/pallas_call | solution.py:358
  124.3 7.4 %far.11 = (f32[8,4,128,512]{3,2,1,0:T(8,128)}, f32[8,8,512]{2,1,0:T(8,128)S(1)}, bf16[512,4096]{1,0:T(8,128)(2,1)}) custom-call(s32[56]{0:T(128)S(1)} %copy-done.1, bf16[2048,128]{1,0:T(8,128)(2,1)S(1)} %collective-permute-done.20.refs_0_, bf16[512,4096]{1,0:T(8,128)(2,1)} %refs_1_.1, ...), custom_call_target="tpu_custom_call", output_to_operand_aliasing={{0}: (3, {}), {1}: (4, {}), {2}: (5, {})} | custom-call | flops 8589934592 | bytes 4194304 | tf_op jit(solution)/shard_map/far/pallas_call | solution.py:358
  (38 shorter events, 0.1 us)
Async XLA Ops:
  0.0 15.3 %copy-start = (bf16[512,1024]{1,0:T(8,128)(2,1)S(1)}, bf16[512,1024]{1,0:T(8,128)(2,1)}, u32[]{:S(2)}) copy-start(bf16[512,1024]{1,0:T(8,128)(2,1)} %k.1) | copy-start | bytes 3145732
  0.0 3.5 %collective-permute-start = (bf16[512,1024]{1,0:T(8,128)(2,1)}, bf16[512,1024]{1,0:T(8,128)(2,1)S(1)}, u32[]{:S(2)}, u32[]{:S(2)}) collective-permute-start(bf16[512,1024]{1,0:T(8,128)(2,1)} %k.1), channel_id=1, source_target_pairs={{0,1},{1,0},{2,3},{3,2},{4,5},{5,4},{6,7},{7,6},{8,9},{9,8},{10,11... | collective-permute-start | bytes 3145736 | tf_op jit(solution)/shard_map/ppermute | solution.py:255
  0.0 4.4 %collective-permute-start.1 = (bf16[512,1024]{1,0:T(8,128)(2,1)}, bf16[512,1024]{1,0:T(8,128)(2,1)S(1)}, u32[]{:S(2)}, u32[]{:S(2)}) collective-permute-start(bf16[512,1024]{1,0:T(8,128)(2,1)} %v.1), channel_id=1, source_target_pairs={{0,1},{1,0},{2,3},{3,2},{4,5},{5,4},{6,7},{7,6},{8,9},{9,8},{10,11... | collective-permute-start | bytes 3145736 | tf_op jit(solution)/shard_map/ppermute | solution.py:255
  3.5 11.8 %copy-start.1 = (s32[56]{0:T(128)S(1)}, s32[56]{0:T(128)}, u32[]{:S(2)}) copy-start(s32[56]{0:T(128)} %concatenate.3.meta) | copy-start | bytes 676
  3.5 1.0 copy-start.11
  4.5 1.0 copy-start.12
  8.6 28.2 %collective-permute-start.2 = (bf16[1024,128]{1,0:T(8,128)(2,1)}, bf16[1024,128]{1,0:T(8,128)(2,1)S(1)}, u32[]{:S(2)}, u32[]{:S(2)}) collective-permute-start(bf16[1024,128]{1,0:T(8,128)(2,1)} %get-tuple-element.58), channel_id=1, source_target_pairs={{0,16},{2,18},{4,20},{6,22},{8,24},{10,26},{12,28},{14,30},{1,17},... | collective-permute-start | bytes 786440 | tf_op jit(solution)/shard_map/ppermute | solution.py:332
  9.9 28.2 %collective-permute-start.3 = (bf16[1024,128]{1,0:T(8,128)(2,1)}, bf16[1024,128]{1,0:T(8,128)(2,1)S(1)}, u32[]{:S(2)}, u32[]{:S(2)}) collective-permute-start(bf16[1024,128]{1,0:T(8,128)(2,1)} %get-tuple-element.59), channel_id=1, source_target_pairs={{0,8},{2,10},{4,12},{6,14},{8,16},{10,18},{12,20},{14,22},{16,24},... | collective-permute-start | bytes 786440 | tf_op jit(solution)/shard_map/ppermute | solution.py:332
  11.2 26.9 %collective-permute-start.4 = (bf16[1024,128]{1,0:T(8,128)(2,1)}, bf16[1024,128]{1,0:T(8,128)(2,1)S(1)}, u32[]{:S(2)}, u32[]{:S(2)}) collective-permute-start(bf16[1024,128]{1,0:T(8,128)(2,1)} %get-tuple-element.60), channel_id=1, source_target_pairs={{0,24},{2,26},{4,28},{6,30},{1,25},{3,27},{5,29},{7,31}} | collective-permute-start | bytes 786440 | tf_op jit(solution)/shard_map/ppermute | solution.py:332
  12.5 48.2 %collective-permute-start.9 = (bf16[1024,128]{1,0:T(8,128)(2,1)}, bf16[1024,128]{1,0:T(8,128)(2,1)S(1)}, u32[]{:S(2)}, u32[]{:S(2)}) collective-permute-start(bf16[1024,128]{1,0:T(8,128)(2,1)} %get-tuple-element.73), channel_id=1, source_target_pairs={{0,18},{2,16},{4,22},{6,20},{8,26},{10,24},{12,30},{14,28},{1,19},... | collective-permute-start | bytes 786440 | tf_op jit(solution)/shard_map/ppermute | solution.py:332
  13.8 23.0 %copy-start.15 = (bf16[1024,128]{1,0:T(8,128)(2,1)S(1)}, bf16[1024,128]{1,0:T(8,128)(2,1)}, u32[]{:S(2)}) copy-start(bf16[1024,128]{1,0:T(8,128)(2,1)} %get-tuple-element.75) | copy-start | bytes 786436
  13.9 38.4 %copy-start.7 = (bf16[1024,128]{1,0:T(8,128)(2,1)S(1)}, bf16[1024,128]{1,0:T(8,128)(2,1)}, u32[]{:S(2)}) copy-start(bf16[1024,128]{1,0:T(8,128)(2,1)} %get-tuple-element.65.refs_7_) | copy-start | bytes 786436
  13.9 38.4 %copy-start.8 = (bf16[1024,128]{1,0:T(8,128)(2,1)S(1)}, bf16[1024,128]{1,0:T(8,128)(2,1)}, u32[]{:S(2)}) copy-start(bf16[1024,128]{1,0:T(8,128)(2,1)} %get-tuple-element.66.refs_8_) | copy-start | bytes 786436
  13.9 38.4 %copy-start.9 = (bf16[1024,128]{1,0:T(8,128)(2,1)S(1)}, bf16[1024,128]{1,0:T(8,128)(2,1)}, u32[]{:S(2)}) copy-start(bf16[1024,128]{1,0:T(8,128)(2,1)} %get-tuple-element.67.refs_9_) | copy-start | bytes 786436
  13.9 38.4 %copy-start.10 = (bf16[1024,128]{1,0:T(8,128)(2,1)S(1)}, bf16[1024,128]{1,0:T(8,128)(2,1)}, u32[]{:S(2)}) copy-start(bf16[1024,128]{1,0:T(8,128)(2,1)} %get-tuple-element.68.refs_10_) | copy-start | bytes 786436
  13.9 48.2 %collective-permute-start.10 = (bf16[1024,128]{1,0:T(8,128)(2,1)}, bf16[1024,128]{1,0:T(8,128)(2,1)S(1)}, u32[]{:S(2)}, u32[]{:S(2)}) collective-permute-start(bf16[1024,128]{1,0:T(8,128)(2,1)} %get-tuple-element.74), channel_id=1, source_target_pairs={{0,10},{2,8},{4,14},{6,12},{8,18},{10,16},{12,22},{14,20},{16,26},... | collective-permute-start | bytes 786440 | tf_op jit(solution)/shard_map/ppermute | solution.py:332
  36.9 26.5 %collective-permute-start.11 = (bf16[1024,128]{1,0:T(8,128)(2,1)S(1)}, bf16[1024,128]{1,0:T(8,128)(2,1)S(1)}, u32[]{:S(2)}, u32[]{:S(2)}) collective-permute-start(bf16[1024,128]{1,0:T(8,128)(2,1)S(1)} %copy-done.15), channel_id=1, source_target_pairs={{0,26},{2,24},{4,30},{6,28},{1,27},{3,25},{5,31},{7,29}} | collective-permute-start | bytes 786440 | tf_op jit(solution)/shard_map/ppermute | solution.py:332
  38.3 26.5 %collective-permute-start.13 = (bf16[3072,128]{1,0:T(8,128)(2,1)S(1)}, bf16[3072,128]{1,0:T(8,128)(2,1)S(1)}, u32[]{:S(2)}, u32[]{:S(2)}) collective-permute-start(bf16[3072,128]{1,0:T(8,128)(2,1)S(1)} %get-tuple-element.78), channel_id=1, source_target_pairs={{0,1},{1,0},{2,3},{3,2},{4,5},{5,4},{6,7},{7,6},{8,9},{9,8},{10,11... | collective-permute-start | bytes 2359304 | tf_op jit(solution)/shard_map/ppermute | solution.py:355
  52.3 13.5 %copy-start.4 = (bf16[1024,128]{1,0:T(8,128)(2,1)S(1)}, bf16[1024,128]{1,0:T(8,128)(2,1)}, u32[]{:S(2)}) copy-start(bf16[1024,128]{1,0:T(8,128)(2,1)} %get-tuple-element.82.refs_8_) | copy-start | bytes 786436
  52.3 13.5 %copy-start.5 = (bf16[1024,128]{1,0:T(8,128)(2,1)S(1)}, bf16[1024,128]{1,0:T(8,128)(2,1)}, u32[]{:S(2)}) copy-start(bf16[1024,128]{1,0:T(8,128)(2,1)} %get-tuple-element.83.refs_9_) | copy-start | bytes 786436
  52.3 13.5 %copy-start.6 = (bf16[1024,128]{1,0:T(8,128)(2,1)S(1)}, bf16[1024,128]{1,0:T(8,128)(2,1)}, u32[]{:S(2)}) copy-start(bf16[1024,128]{1,0:T(8,128)(2,1)} %get-tuple-element.84.refs_10_) | copy-start | bytes 786436
  59.5 19.4 %collective-permute-start.5 = (bf16[1024,128]{1,0:T(8,128)(2,1)S(1)}, bf16[1024,128]{1,0:T(8,128)(2,1)S(1)}, u32[]{:S(2)}, u32[]{:S(2)}) collective-permute-start(bf16[1024,128]{1,0:T(8,128)(2,1)S(1)} %get-tuple-element.69), channel_id=1, source_target_pairs={{0,20},{2,22},{4,16},{6,18},{8,28},{10,30},{12,24},{14,26},{1,21},... | collective-permute-start | bytes 786440 | tf_op jit(solution)/shard_map/ppermute | solution.py:332
  60.8 19.4 %collective-permute-start.6 = (bf16[1024,128]{1,0:T(8,128)(2,1)S(1)}, bf16[1024,128]{1,0:T(8,128)(2,1)S(1)}, u32[]{:S(2)}, u32[]{:S(2)}) collective-permute-start(bf16[1024,128]{1,0:T(8,128)(2,1)S(1)} %get-tuple-element.70), channel_id=1, source_target_pairs={{0,2},{4,6},{8,10},{12,14},{16,18},{20,22},{24,26},{28,30},{1,3},{... | collective-permute-start | bytes 786440 | tf_op jit(solution)/shard_map/ppermute | solution.py:332
  62.1 19.4 %collective-permute-start.7 = (bf16[1024,128]{1,0:T(8,128)(2,1)S(1)}, bf16[1024,128]{1,0:T(8,128)(2,1)S(1)}, u32[]{:S(2)}, u32[]{:S(2)}) collective-permute-start(bf16[1024,128]{1,0:T(8,128)(2,1)S(1)} %get-tuple-element.71), channel_id=1, source_target_pairs={{0,12},{2,14},{4,8},{6,10},{8,20},{10,22},{12,16},{14,18},{16,28},... | collective-permute-start | bytes 786440 | tf_op jit(solution)/shard_map/ppermute | solution.py:332
  63.4 19.6 %collective-permute-start.8 = (bf16[1024,128]{1,0:T(8,128)(2,1)S(1)}, bf16[1024,128]{1,0:T(8,128)(2,1)S(1)}, u32[]{:S(2)}, u32[]{:S(2)}) collective-permute-start(bf16[1024,128]{1,0:T(8,128)(2,1)S(1)} %get-tuple-element.72), channel_id=1, source_target_pairs={{0,4},{2,6},{8,12},{10,14},{16,20},{18,22},{24,28},{26,30},{1,5},{... | collective-permute-start | bytes 786440 | tf_op jit(solution)/shard_map/ppermute | solution.py:332
  64.8 0.9 copy-start.13
  64.8 19.4 %collective-permute-start.12 = (bf16[3072,128]{1,0:T(8,128)(2,1)S(1)}, bf16[3072,128]{1,0:T(8,128)(2,1)S(1)}, u32[]{:S(2)}, u32[]{:S(2)}) collective-permute-start(bf16[3072,128]{1,0:T(8,128)(2,1)S(1)} %get-tuple-element.77), channel_id=1, source_target_pairs={{0,1},{1,0},{2,3},{3,2},{4,5},{5,4},{6,7},{7,6},{8,9},{9,8},{10,11... | collective-permute-start | bytes 2359304 | tf_op jit(solution)/shard_map/ppermute | solution.py:355
  65.7 19.4 %copy-start.2 = (bf16[1024,128]{1,0:T(8,128)(2,1)S(1)}, bf16[1024,128]{1,0:T(8,128)(2,1)}, u32[]{:S(2)}) copy-start(bf16[1024,128]{1,0:T(8,128)(2,1)} %get-tuple-element.89.refs_9_) | copy-start | bytes 786436
  65.7 19.4 %copy-start.3 = (bf16[1024,128]{1,0:T(8,128)(2,1)S(1)}, bf16[1024,128]{1,0:T(8,128)(2,1)}, u32[]{:S(2)}) copy-start(bf16[1024,128]{1,0:T(8,128)(2,1)} %get-tuple-element.90.refs_10_) | copy-start | bytes 786436
  78.9 15.0 %collective-permute-start.16 = (bf16[1024,128]{1,0:T(8,128)(2,1)S(1)}, bf16[1024,128]{1,0:T(8,128)(2,1)S(1)}, u32[]{:S(2)}, u32[]{:S(2)}) collective-permute-start(bf16[1024,128]{1,0:T(8,128)(2,1)S(1)} %get-tuple-element.93), channel_id=1, source_target_pairs={{0,28},{2,30},{4,24},{6,26},{1,29},{3,31},{5,25},{7,27}} | collective-permute-start | bytes 786440 | tf_op jit(solution)/shard_map/ppermute | solution.py:332
  80.2 20.8 %collective-permute-start.17 = (bf16[1024,128]{1,0:T(8,128)(2,1)S(1)}, bf16[1024,128]{1,0:T(8,128)(2,1)S(1)}, u32[]{:S(2)}, u32[]{:S(2)}) collective-permute-start(bf16[1024,128]{1,0:T(8,128)(2,1)S(1)} %get-tuple-element.94), channel_id=1, source_target_pairs={{0,22},{2,20},{4,18},{6,16},{8,30},{10,28},{12,26},{14,24},{1,23},... | collective-permute-start | bytes 786440 | tf_op jit(solution)/shard_map/ppermute | solution.py:332
  81.5 19.5 %collective-permute-start.18 = (bf16[1024,128]{1,0:T(8,128)(2,1)S(1)}, bf16[1024,128]{1,0:T(8,128)(2,1)S(1)}, u32[]{:S(2)}, u32[]{:S(2)}) collective-permute-start(bf16[1024,128]{1,0:T(8,128)(2,1)S(1)} %get-tuple-element.95), channel_id=1, source_target_pairs={{0,6},{2,4},{8,14},{10,12},{16,22},{18,20},{24,30},{26,28},{1,7},{... | collective-permute-start | bytes 786440 | tf_op jit(solution)/shard_map/ppermute | solution.py:332
  84.1 17.1 %collective-permute-start.19 = (bf16[4096,128]{1,0:T(8,128)(2,1)}, bf16[4096,128]{1,0:T(8,128)(2,1)S(1)}, u32[]{:S(2)}, u32[]{:S(2)}) collective-permute-start(bf16[4096,128]{1,0:T(8,128)(2,1)} %get-tuple-element.96), channel_id=1, source_target_pairs={{0,1},{1,0},{2,3},{3,2},{4,5},{5,4},{6,7},{7,6},{8,9},{9,8},{10,11... | collective-permute-start | bytes 3145736 | tf_op jit(solution)/shard_map/ppermute | solution.py:355
  84.2 0.9 copy-start.14
  92.6 18.1 %collective-permute-start.14 = (bf16[1024,128]{1,0:T(8,128)(2,1)S(1)}, bf16[1024,128]{1,0:T(8,128)(2,1)S(1)}, u32[]{:S(2)}, u32[]{:S(2)}) collective-permute-start(bf16[1024,128]{1,0:T(8,128)(2,1)S(1)} %get-tuple-element.91), channel_id=1, source_target_pairs={{0,14},{2,12},{4,10},{6,8},{8,22},{10,20},{12,18},{14,16},{16,30},... | collective-permute-start | bytes 786440 | tf_op jit(solution)/shard_map/ppermute | solution.py:332
  93.9 19.6 %collective-permute-start.15 = (bf16[1024,128]{1,0:T(8,128)(2,1)S(1)}, bf16[1024,128]{1,0:T(8,128)(2,1)S(1)}, u32[]{:S(2)}, u32[]{:S(2)}) collective-permute-start(bf16[1024,128]{1,0:T(8,128)(2,1)S(1)} %get-tuple-element.92), channel_id=1, source_target_pairs={{0,30},{2,28},{4,26},{6,24},{1,31},{3,29},{5,27},{7,25}} | collective-permute-start | bytes 786440 | tf_op jit(solution)/shard_map/ppermute | solution.py:332
  101.1 13.7 %collective-permute-start.21 = (bf16[3072,128]{1,0:T(8,128)(2,1)S(1)}, bf16[3072,128]{1,0:T(8,128)(2,1)S(1)}, u32[]{:S(2)}, u32[]{:S(2)}) collective-permute-start(bf16[3072,128]{1,0:T(8,128)(2,1)S(1)} %get-tuple-element.103), channel_id=1, source_target_pairs={{0,1},{1,0},{2,3},{3,2},{4,5},{5,4},{6,7},{7,6},{8,9},{9,8},{10,11... | collective-permute-start | bytes 2359304 | tf_op jit(solution)/shard_map/ppermute | solution.py:355
  113.5 10.8 %collective-permute-start.20 = (bf16[2048,128]{1,0:T(8,128)(2,1)S(1)}, bf16[2048,128]{1,0:T(8,128)(2,1)S(1)}, u32[]{:S(2)}, u32[]{:S(2)}) collective-permute-start(bf16[2048,128]{1,0:T(8,128)(2,1)S(1)} %get-tuple-element.102), channel_id=1, source_target_pairs={{0,1},{1,0},{2,3},{3,2},{4,5},{5,4},{6,7},{7,6},{8,9},{9,8},{10,11... | collective-permute-start | bytes 1572872 | tf_op jit(solution)/shard_map/ppermute | solution.py:355
where the time goes:
time: 134 us; the launch traced here: 132 us
  Pallas kernels  80.1 us (60%)
  starting transfers between devices  36.3 us (27%)
  waiting for transfers between devices  9.78 us (7%)
  local copies, waits for them, and re-layouts  3.7 us (3%)
  other arithmetic  1.4 us (1%)
    pallas_call x6, Pallas kernels, body(): pl.pallas_call(functools.partial(far_kernel, n_here, len(others), n_pass,...  54.2 us
    pallas_call x1, Pallas kernels, body(): pl.pallas_call(functools.partial(own_kernel, local_at), grid_spec=pltpu.P...  21.5 us
    ppermute x15, starting transfers between devices, send(): landed[j] = lax.ppermute(sent[j], 'ctx', pairs_of(fast, slow, *order[j]))  19.5 us
    ppermute x5, starting transfers between devices, body(): swapped.append(lax.ppermute(joined, 'head', swap))  16.3 us
    ppermute x15, waiting for transfers between devices, send(): landed[j] = lax.ppermute(sent[j], 'ctx', pairs_of(fast, slow, *order[j]))  8.91 us
    pallas_call x1, Pallas kernels, body(): pl.pallas_call(functools.partial(cut_kernel, fast, slow, order), grid_spe...  3.11 us
  transfers between devices with their start and end apart: 22, of which 4 were waited for; matrix products, arithmetic and copies ran while one was open for 2% of the time, Pallas kernels for 53%

commit v1 on v0

v1 whole, which is shorter than its diff:
```python
import functools
import math

import jax
import jax.numpy as jnp
import numpy as np
from jax import lax
from jax.experimental import pallas as pl
from jax.experimental.pallas import tpu as pltpu
from jax.sharding import PartitionSpec as P

QH = 32
KVH = 8
HD = 128
BLK = 512
TOPK = 3
GROUP = QH // KVH
KVG = KVH // 2
WIDE = GROUP * HD
ROWS = GROUP * BLK
SCALE = math.log2(math.e) / math.sqrt(HD)
TILE = 128
VMEM = pltpu.VMEM
ANY = pl.ANY


def patterns(peers):
    fast = 4 if peers % 4 == 0 else 1
    slow = peers // fast

    def permute(moves, flip):
        pairs = [(a * fast + f, b * fast + (f ^ flip)) for a, b in moves for f in range(fast)]
        return [(a, b) for a, b in pairs if a < b]

    level = [(a, a) for a in range(slow)]
    if (fast, slow) == (4, 4):
        two, one, zero = [(0, 2), (1, 3)], [(0, 3), (1, 2)], [(0, 1), (2, 3)]
        order = []
        for m in range(3):
            order += [permute(two, m), permute(one, m), permute(zero, m)]
        order += [permute(level, 1), permute(two, 3), permute(level, 2), permute(level, 3), permute(zero, 3)]
        order += [permute(one, 3)]
        edges = [0, 3, 6, 10, 14, 15]
    else:
        order = []
        for m in range(fast):
            order += [permute([(a, a + d) for a in range(slow - d)], m) for d in range(1, slow)]
        order += [permute(level, m) for m in range(1, fast)]
        edges = [round(i * len(order) / 5) for i in range(6)]
    table = np.full((peers, 2 * len(order)), -2, np.int32)
    for n, pairs in enumerate(order):
        for a, b in pairs:
            table[a, n] = b
            table[b, len(order) + n] = a
    return order, table, list(zip(edges[:-1], edges[1:]))


def scores_of(k, q):
    return lax.dot_general(k, q, (((1,), (1,)), ((), ())), preferred_element_type=jnp.float32)


def total_of(vt, weights):
    return jnp.dot(vt, weights.astype(jnp.bfloat16), preferred_element_type=jnp.float32)


def cut_kernel(first, count, n_pass, meta, key, value, okey, ovalue, *rest):
    outs, sems = rest[n_pass : n_pass + count], rest[-1]
    side = meta[0]

    def each(act):
        for j in range(count):
            code = meta[1 + first + j] - 1
            block, head = code // KVH, code % KVH
            col = pl.multiple_of(jnp.maximum(head, 0) * HD, HD)
            for t, (here, there) in enumerate(((key, okey), (value, ovalue))):
                to = outs[j].at[pl.ds(t * BLK, BLK), :]
                mine = pltpu.make_async_copy(here.at[:, pl.ds(col, HD)], to, sems.at[j, t])
                other = pltpu.make_async_copy(there.at[:, pl.ds(col, HD)], to, sems.at[j, t])
                act(jnp.logical_and(code >= 0, block == side), mine)
                act(jnp.logical_and(code >= 0, block != side), other)

    def start(flag, copy):
        pl.when(flag)(copy.start)

    def wait(flag, copy):
        pl.when(flag)(copy.wait)

    each(start)
    each(wait)


def own_kernel(local_at, work, meta, q, k, v, ok, ov, acc_out, stat_out, out, vt, outs, uses, sem):
    g = pl.program_id(0)
    cols = pl.ds(pl.multiple_of(g * HD, HD), HD)
    vt[...] = v[:, cols].T
    low = lax.broadcasted_iota(jnp.int32, (TILE, TILE), 1) >= lax.broadcasted_iota(jnp.int32, (TILE, TILE), 0)
    for r in reversed(range(BLK // TILE)):
        keys, at = (r + 1) * TILE, slice(r * TILE, (r + 1) * TILE)
        for j in range(GROUP):
            scores = scores_of(k[:keys, cols], q[at, j * HD : (j + 1) * HD])
            last = jnp.where(low, scores[r * TILE :], -1e30)
            scores = jnp.concatenate([scores[: r * TILE], last], axis=0) if r else last
            m = jnp.max(scores, axis=0, keepdims=True)
            weights = jnp.exp2((scores - m) * SCALE)
            stat_out[0, j : j + 1, at] = m
            stat_out[0, GROUP + j : GROUP + j + 1, at] = jnp.sum(weights, axis=0, keepdims=True)
            acc_out[0, j, :, at] = total_of(vt[:, :keys], weights)

    @pl.when(meta[local_at + g] > 0)
    def _():
        vt[...] = ov[:, cols].T
        fold(ok.at[:, cols], lambda at, col: q[at, col], vt, acc_out.at[0], stat_out.at[0])

    uses[0] = 0

    def count(i, carry):
        uses[0] = uses[0] + jnp.where(meta[i] == g, 1, 0)
        return carry

    lax.fori_loop(*work, count, 0)

    @pl.when(uses[0] == 0)
    def _():
        for j in range(GROUP):
            total = stat_out[0, GROUP + j : GROUP + j + 1, :]
            outs[:, j * HD : (j + 1) * HD] = (acc_out[0, j] / total).astype(jnp.bfloat16).T
        copy = pltpu.make_async_copy(outs, out.at[:, pl.ds(pl.multiple_of(g * WIDE, WIDE), WIDE)], sem)
        copy.start()
        copy.wait()


def fold(k, q_of, vt, acc, stat):
    for j in range(GROUP):
        for r in range(BLK // TILE):
            at = slice(r * TILE, (r + 1) * TILE)
            scores = scores_of(k[...], q_of(at, slice(j * HD, (j + 1) * HD)))
            m_old = stat[j : j + 1, at]
            m = jnp.maximum(m_old, jnp.max(scores, axis=0, keepdims=True))
            weights = jnp.exp2((scores - m) * SCALE)
            alpha = jnp.exp2((m_old - m) * SCALE)
            total = GROUP + j
            stat[j : j + 1, at] = m
            stat[total : total + 1, at] = stat[total : total + 1, at] * alpha + jnp.sum(weights, axis=0, keepdims=True)
            acc[j, :, at] = acc[j, :, at] * alpha + total_of(vt[...], weights)


def far_kernel(n_here, n_swap, here_at, here_later, swap_at, swap_later, meta, *refs):
    arrived, refs = refs[:n_here], refs[n_here:]
    swapped, refs = refs[:n_swap], refs[n_swap:]
    q_hbm, acc_hbm, stat_hbm = refs[:3]
    refs = refs[4:]
    acc_new, stat_new, out_new = refs[:3]
    qs, accs, stats, outs, kv, vt, seen, here, later, kv_sem, in_sem, out_sem = refs[3:]
    each = n_swap and swapped[0].shape[0] // (2 * BLK)
    pieces = n_here + n_swap * each

    def wide(g):
        return pl.ds(pl.multiple_of(g * WIDE, WIDE), WIDE)

    def loads(g):
        return (
            pltpu.make_async_copy(q_hbm.at[:, wide(g)], qs.at[g], in_sem.at[g, 0]),
            pltpu.make_async_copy(acc_hbm.at[g], accs.at[g], in_sem.at[g, 1]),
            pltpu.make_async_copy(stat_hbm.at[g], stats.at[g], in_sem.at[g, 2]),
        )

    def stores(g):
        return (
            pltpu.make_async_copy(accs.at[g], acc_new.at[g], out_sem.at[g, 0]),
            pltpu.make_async_copy(stats.at[g], stat_new.at[g], out_sem.at[g, 1]),
        )

    def finish(g):
        return pltpu.make_async_copy(outs.at[g], out_new.at[:, wide(g)], out_sem.at[g, 2])

    def head_of(i):
        return meta[jnp.where(i < n_here, here_at + i, swap_at + i - n_here)]

    for g in range(KVH):
        seen[g] = 0
        here[g] = 0
        later[g] = 0

    for i in range(pieces):
        g = meta[here_at + i] if i < n_here else meta[swap_at + i - n_here]
        block = arrived[i] if i < n_here else swapped[0].at[pl.ds((i - n_here) * 2 * BLK, 2 * BLK), :]

        @pl.when(g >= 0)
        def _():
            pltpu.make_async_copy(block, kv.at[i], kv_sem.at[i]).start()

            @pl.when(here[g] == 0)
            def _():
                for copy in loads(g):
                    copy.start()

            here[g] = here[g] + 1

    def count(i, carry):
        g = meta[i]

        @pl.when(g >= 0)
        def _():
            later[g] = later[g] + 1

        return carry

    lax.fori_loop(*here_later, count, 0)
    lax.fori_loop(*swap_later, count, 0)

    def piece(i, carry):
        g = head_of(i)

        @pl.when(g >= 0)
        def _():
            @pl.when(seen[g] == 0)
            def _():
                for copy in loads(g):
                    copy.wait()

            pltpu.make_async_copy(kv.at[i], kv.at[i], kv_sem.at[i]).wait()
            vt[...] = kv[i, BLK:, :].T
            fold(
                kv.at[i, pl.ds(0, BLK), :], lambda at, col: qs[g, at, col], vt, accs.at[g], stats.at[g]
            )
            seen[g] = seen[g] + 1
            done = seen[g] == here[g]

            @pl.when(jnp.logical_and(done, later[g] > 0))
            def _():
                for copy in stores(g):
                    copy.start()

            @pl.when(jnp.logical_and(done, later[g] == 0))
            def _():
                for j in range(GROUP):
                    outs[g, :, j * HD : (j + 1) * HD] = (
                        (accs[g, j] / stats[g, GROUP + j : GROUP + j + 1, :]).astype(jnp.bfloat16).T
                    )
                finish(g).start()

        return carry

    lax.fori_loop(0, pieces, piece, 0)

    for g in range(KVH):
        used = here[g] > 0

        @pl.when(jnp.logical_and(used, later[g] > 0))
        def _():
            for copy in stores(g):
                copy.wait()

        @pl.when(jnp.logical_and(used, later[g] == 0))
        def _():
            finish(g).wait()


def pack_kernel(count, n_pass, *refs):
    joined = refs[count + 1 + n_pass]
    for i in range(count):
        joined[i * 2 * BLK : (i + 1) * 2 * BLK, :] = refs[i][...]


def body(queries, key, value, selection):
    me, side = lax.axis_index("ctx"), lax.axis_index("head")
    peers = lax.axis_size("ctx")
    order, table, groups = patterns(peers)
    total = len(order)
    swap = [(0, 1), (1, 0)]
    okey, ovalue = lax.ppermute(key, "head", swap), lax.ppermute(value, "head", swap)

    ends = lax.dynamic_index_in_dim(jnp.asarray(table), me, 0, keepdims=False)
    targets, sources = ends[:total], ends[total:]
    picks = selection[:, :, 1:]
    asked = lax.dynamic_slice_in_dim(picks, side * KVG, KVG, 1)
    codes = (asked - 2 * me) * KVH + (side * KVG + jnp.arange(KVG, dtype=jnp.int32))[None, :, None] + 1
    wanted = jnp.max(
        jnp.where((asked >> 1) == me, codes, 0).reshape(peers, 2 * KVG * TOPK), axis=1
    )
    cuts = jnp.max(
        jnp.where(targets[:, None] == jnp.arange(peers, dtype=jnp.int32)[None, :], wanted[None, :], 0), axis=1
    )
    mine = lax.dynamic_slice_in_dim(picks, 2 * me + side, 1, 0)[0]
    owners = jnp.where(mine >= 0, mine >> 1, -1)
    local = jnp.any(owners == me, axis=1).astype(jnp.int32)
    heads = jnp.arange(KVH, dtype=jnp.int32)
    hit = jnp.any(owners[None, :, :] == sources[:, None, None], axis=2)
    near = (heads // KVG) == side
    work_here = jnp.max(jnp.where(hit & near, heads, -1), axis=1)
    work_swap = jnp.max(jnp.where(hit & ~near, heads, -1), axis=1)
    meta = jnp.concatenate([side[None].astype(jnp.int32), cuts, local, work_here, work_swap])
    local_at = 1 + total
    here_at = local_at + KVH
    swap_at = here_at + total
    end = swap_at + total

    piece_shape = jax.ShapeDtypeStruct((2 * BLK, HD), jnp.bfloat16)
    any_spec, vmem_spec = pl.BlockSpec(memory_space=ANY), pl.BlockSpec(memory_space=VMEM)
    state = (
        jax.ShapeDtypeStruct((KVH, GROUP, HD, BLK), jnp.float32),
        jax.ShapeDtypeStruct((KVH, 2 * GROUP, BLK), jnp.float32),
        jax.ShapeDtypeStruct((BLK, QH * HD), jnp.bfloat16),
    )
    params = pltpu.CompilerParams(vmem_limit_bytes=48 << 20)

    def cut(first, last, *through):
        count = last - first
        return pl.pallas_call(
            functools.partial(cut_kernel, first, count, len(through)),
            grid_spec=pltpu.PrefetchScalarGridSpec(
                num_scalar_prefetch=1,
                grid=(),
                in_specs=[vmem_spec] * 4 + [any_spec] * len(through),
                out_specs=[any_spec] * (count + len(through)),
                scratch_shapes=[pltpu.SemaphoreType.DMA((count, 2))],
            ),
            out_shape=[piece_shape] * count + [jax.ShapeDtypeStruct(x.shape, x.dtype) for x in through],
            input_output_aliases={5 + i: count + i for i in range(len(through))},
            cost_estimate=pl.CostEstimate(flops=0, bytes_accessed=count << 19, transcendentals=0),
            name="cut",
        )(meta, key, value, okey, ovalue, *through)

    early = min(5, groups[1][1])
    sent = list(cut(0, early))

    q_spec = pl.BlockSpec((BLK, WIDE), lambda g, _: (0, g))
    piece_flops = 4 * ROWS * BLK * HD
    acc, stat, out = pl.pallas_call(
        functools.partial(own_kernel, local_at, (here_at, end)),
        grid_spec=pltpu.PrefetchScalarGridSpec(
            num_scalar_prefetch=1,
            grid=(KVH,),
            in_specs=[q_spec] + [vmem_spec] * 4,
            out_specs=[
                pl.BlockSpec((1, GROUP, HD, BLK), lambda g, _: (g, 0, 0, 0)),
                pl.BlockSpec((1, 2 * GROUP, BLK), lambda g, _: (g, 0, 0)),
                any_spec,
            ],
            scratch_shapes=[
                VMEM((HD, BLK), jnp.bfloat16),
                VMEM((BLK, WIDE), jnp.bfloat16),
                pltpu.SMEM((1,), jnp.int32),
                pltpu.SemaphoreType.DMA,
            ],
        ),
        out_shape=state,
        compiler_params=params,
        cost_estimate=pl.CostEstimate(
            flops=32 * piece_flops, bytes_accessed=28 << 20, transcendentals=12 * ROWS * BLK
        ),
        name="own",
    )(meta, queries, key, value, okey, ovalue)
    *rest, stat = cut(early, total, stat)
    sent += rest

    landed = [None] * total
    swapped = []

    def send(n):
        a, b = groups[n]
        for j in range(a, b):
            landed[j] = lax.ppermute(sent[j], "ctx", order[j])

    def pack(n, stat):
        a, b = groups[n]
        late = list(range(*groups[n + 2])) if n + 2 < len(groups) else []
        count = b - a
        joined, stat, *through = pl.pallas_call(
            functools.partial(pack_kernel, count, len(late)),
            in_specs=[vmem_spec] * count + [any_spec] * (1 + len(late)),
            out_specs=[vmem_spec] + [any_spec] * (1 + len(late)),
            out_shape=(jax.ShapeDtypeStruct((count * 2 * BLK, HD), jnp.bfloat16), state[1], *[piece_shape] * len(late)),
            input_output_aliases={count + i: 1 + i for i in range(1 + len(late))},
            compiler_params=params,
            cost_estimate=pl.CostEstimate(flops=0, bytes_accessed=count << 19, transcendentals=0),
            name="pack",
        )(*landed[a:b], stat, *[sent[j] for j in late])
        swapped.append(lax.ppermute(joined, "head", swap))
        for j, x in zip(late, through):
            sent[j] = x
        if late:
            send(n + 2)
        return stat

    def far(here, swaps, acc, stat, out):
        a, b = groups[here] if here is not None else (0, 0)
        a0, b0 = groups[swaps] if swaps is not None else (0, 0)
        here_end = max(b, b0)
        swap_end = b0 if swaps is not None else (groups[here - 1][1] if here else 0)
        n_here = b - a
        pieces = n_here + b0 - a0
        others = [swapped[swaps]] if swaps is not None else []
        base = 1 + n_here + len(others)
        return pl.pallas_call(
            functools.partial(
                far_kernel, n_here, len(others),
                here_at + a, (here_at + here_end, swap_at), swap_at + a0, (swap_at + swap_end, end),
            ),
            grid_spec=pltpu.PrefetchScalarGridSpec(
                num_scalar_prefetch=1,
                grid=(),
                in_specs=[any_spec] * (base - 1 + 4),
                out_specs=[any_spec] * 3,
                scratch_shapes=[
                    VMEM((KVH, BLK, WIDE), jnp.bfloat16),
                    VMEM((KVH, GROUP, HD, BLK), jnp.float32),
                    VMEM((KVH, 2 * GROUP, BLK), jnp.float32),
                    VMEM((KVH, BLK, WIDE), jnp.bfloat16),
                    VMEM((pieces, 2 * BLK, HD), jnp.bfloat16),
                    VMEM((HD, BLK), jnp.bfloat16),
                    pltpu.SMEM((KVH,), jnp.int32),
                    pltpu.SMEM((KVH,), jnp.int32),
                    pltpu.SMEM((KVH,), jnp.int32),
                    pltpu.SemaphoreType.DMA((pieces,)),
                    pltpu.SemaphoreType.DMA((KVH, 3)),
                    pltpu.SemaphoreType.DMA((KVH, 3)),
                ],
            ),
            out_shape=state,
            input_output_aliases={base + 1 + i: i for i in range(3)},
            compiler_params=params,
            cost_estimate=pl.CostEstimate(
                flops=8 * pieces * piece_flops, bytes_accessed=pieces << 21, transcendentals=pieces * ROWS * BLK
            ),
            name="far",
        )(meta, *landed[a:b], *others, queries, acc, stat, out)

    send(0)
    send(1)
    last = len(groups) - 1
    for n in range(last):
        stat = pack(n, stat)
        acc, stat, out = far(n, n - 1 if n else None, acc, stat, out)
    acc, stat, out = far(None, last - 1, acc, stat, out)
    stat = pack(last, stat)
    acc, stat, out = far(last, None, acc, stat, out)
    acc, stat, out = far(None, last, acc, stat, out)
    return out


def solution(mesh):
    placed = (P(("ctx", "head"), None), P(("ctx", "head"), None), P(("ctx", "head"), None), P())
    return jax.shard_map(
        body, mesh=mesh, in_specs=placed, out_specs=P(("ctx", "head"), None), check_vma=False
    )
```

time: 134 us -> 156 us (1.16); the launches traced: 132 us -> 157 us
  starting transfers between devices: 36.3 us -> 47.2 us
  local copies, waits for them, and re-layouts: 3.7 us -> 14.1 us
  waiting for transfers between devices: 9.78 us -> 18.3 us
  Pallas kernels: 80.1 us -> 75.9 us
    ppermute x20, starting transfers between devices: 35.8 us -> 46.7 us  [the longest x5 27.3 us: pack(): swapped.append(lax.ppermute(joined, 'head', swap))]
    unnamed x32 -> x54, local copies, waits for them, and re-layouts: 2.12 us -> 11.7 us
    ppermute x20, waiting for transfers between devices: 8.93 us -> 17.5 us  [the longest x15 17.5 us: send(): landed[j] = lax.ppermute(sent[j], 'ctx', order[j])]
    pallas_call x13 -> x15, Pallas kernels: 80.1 us -> 75.9 us  [the longest x7 49.5 us: far(): pl.pallas_call(functools.partial(far_kernel, n_here, len(others), here_at...]
  transfers between devices with their start and end apart: 22 -> 22, of which waited for: 4 -> 3; matrix products, arithmetic and copies ran while one was open for 2% -> 2% of each run, Pallas kernels for 53% -> 43%
where the time goes in v1:
time: 156 us; the launch traced here: 157 us
  Pallas kernels  75.9 us (49%)
  starting transfers between devices  47.2 us (30%)
  waiting for transfers between devices  18.3 us (12%)
  local copies, waits for them, and re-layouts  14.1 us (9%)
    pallas_call x7, Pallas kernels, far(): pl.pallas_call(functools.partial(far_kernel, n_here, len(others), here_at...  49.5 us
    ppermute x5, starting transfers between devices, pack(): swapped.append(lax.ppermute(joined, 'head', swap))  27.3 us
    pallas_call x1, Pallas kernels, body(): pl.pallas_call(functools.partial(own_kernel, local_at, (here_at, end)), g...  20.1 us
    ppermute x15, starting transfers between devices, send(): landed[j] = lax.ppermute(sent[j], 'ctx', order[j])  19.4 us
    ppermute x15, waiting for transfers between devices, send(): landed[j] = lax.ppermute(sent[j], 'ctx', order[j])  17.5 us
    unnamed x54, local copies, waits for them, and re-layouts  11.7 us
    pallas_call x2, Pallas kernels, cut(): pl.pallas_call(functools.partial(cut_kernel, first, count, len(through)),...  6.07 us
  transfers between devices with their start and end apart: 22, of which 3 were waited for; matrix products, arithmetic and copies ran while one was open for 2% of the time, Pallas kernels for 43%

profile of v1, /device:TPU:30, one launch (start us, length us, event | category | flops | bytes accessed | tf_op | source)
XLA Modules:
  0.0 157.1 jit_solution(4898939854172443270)
XLA Ops:
  0.0 0.5 collective-permute-start.1
  0.5 0.8 slice.12
  1.4 0.3 compare_reduce_fusion
  1.7 0.1 copy.46
  1.8 0.1 select_reduce_fusion.1
  1.9 0.1 reduce_max.44
  2.0 0.1 reduce_max.45
  2.1 0.7 constant_dynamic-slice_fusion
  2.8 0.1 slice_bitcast_fusion
  2.9 0.2 select_reduce_fusion
  3.1 0.1 compare_reduce_fusion.1
  3.1 0.1 select_reduce_fusion.2
  3.2 0.6 concatenate.3.meta
  3.8 0.7 collective-permute-done.1.ovalue.ov
  4.5 0.3 copy-done.9
  4.8 2.9 %cut.2 = (bf16[1024,128]{1,0:T(8,128)(2,1)}, bf16[1024,128]{1,0:T(8,128)(2,1)}, bf16[1024,128]{1,0:T(8,128)(2,1)}, bf16[1024,128]{1,0:T(8,128)(2,1)}, bf16[1024,128]{1,0:T(8,128)(2,1)}) custom-call(s32[54]{0:T(128)} %concatenate.3.meta, bf16[512,1024]{1,0:T(8,128)(2,1)} %key.3, bf16[512,1024]{1,0:T(8,128)(2,1)} %value.3, bf16[512,1024]{1,0:T(8,128)(2,1)} %copy-done.9, ...), custom_call_target="tpu_custom_call" | custom-call | bytes 2621440 | tf_op jit(solution)/shard_map/cut/pallas_call | solution.py:309
  7.7 1.3 collective-permute-start.2
  9.0 1.3 collective-permute-start.3
  10.3 1.3 collective-permute-start.4
  11.6 1.3 collective-permute-start.9
  12.9 1.3 collective-permute-start.10
  14.2 1.2 copy-done.10
  15.5 20.1 %own.1 = (f32[8,4,128,512]{3,2,1,0:T(8,128)}, f32[8,8,512]{2,1,0:T(8,128)S(1)}, bf16[512,4096]{1,0:T(8,128)(2,1)}) custom-call(s32[54]{0:T(128)S(1)} %copy-done.25, bf16[512,4096]{1,0:T(8,128)(2,1)} %refs_1_.5, bf16[512,1024]{1,0:T(8,128)(2,1)S(1)} %copy-done.7, bf16[512,1024]{1,0:T(8,128)(2,1)S(1)} %copy-done.8, bf16[512,1024]{1,0:T(8,128)(2,1)S(1)} %copy-done.10, ...), custom_call_target="tpu_custom_call" | custom-call | flops 17179869184 | bytes 29360128 | tf_op jit(solution)/shard_map/own/pallas_call | solution.py:329
  35.6 0.6 copy-done.3
  36.2 3.1 %cut.3 = (bf16[1024,128]{1,0:T(8,128)(2,1)}, bf16[1024,128]{1,0:T(8,128)(2,1)}, bf16[1024,128]{1,0:T(8,128)(2,1)}, bf16[1024,128]{1,0:T(8,128)(2,1)}, bf16[1024,...) custom-call(s32[54]{0:T(128)} %concatenate.3.meta, ...), custom_call_target="tpu_custom_call", output_to_operand_aliasing={{10}: (5, {})} | custom-call | bytes 5242880 | tf_op jit(solution)/shard_map/cut/pallas_call | solution.py:309
  39.4 1.3 collective-permute-start.11
  40.7 0.9 copy-done.4
  41.6 0.9 copy-done.15
  42.5 0.9 copy-done.18
  43.5 0.9 copy-done.21
  44.4 0.1 pack.5
  44.5 0.6 copy-done.5
  45.2 0.7 copy-done.16
  45.8 0.7 copy-done.19
  46.5 0.7 copy-done.22
  47.2 1.3 collective-permute-start.5
  48.5 12.3 %collective-permute-start.12 = (bf16[3072,128]{1,0:T(8,128)(2,1)S(1)}, bf16[3072,128]{1,0:T(8,128)(2,1)S(1)}, u32[]{:S(2)}, u32[]{:S(2)}) collective-permute-start(bf16[3072,128]{1,0:T(8,128)(2,1)S(1)} %get-tuple-element.78), channel_id=1, source_target_pairs={{0,1},{1,0},{2,3},{3,2},{4,5},{5,4},{6,7},{7,6},{8,9},{9,8},{10,11... | collective-permute-start | bytes 2359304 | tf_op jit(solution)/shard_map/ppermute | solution.py:379
  60.8 2.2 %copy-done = bf16[512,4096]{1,0:T(8,128)(2,1)S(1)} copy-done((bf16[512,4096]{1,0:T(8,128)(2,1)S(1)}, bf16[512,4096]{1,0:T(8,128)(2,1)}, u32[]{:S(2)}) %copy-start) | copy-done | bytes 4194328
  63.0 0.9 copy-done.6
  63.9 7.4 %far.7 = (f32[8,4,128,512]{3,2,1,0:T(8,128)}, f32[8,8,512]{2,1,0:T(8,128)S(1)}, bf16[512,4096]{1,0:T(8,128)(2,1)}) custom-call(s32[54]{0:T(128)S(1)} %copy-done.26, bf16[1024,128]{1,0:T(8,128)(2,1)S(1)} %collective-permute-done.2.refs_0_, ...), custom_call_target="tpu_custom_call", output_to_operand_aliasing={{0}: (5, {}), {1}: (6, {}), {2}: (7, {})} | custom-call | flops 12884901888 | bytes 6291456 | tf_op jit(solution)/shard_map/far/pallas_call | solution.py:395
  71.4 1.3 collective-permute-start.6
  72.7 1.3 collective-permute-start.7
  74.0 1.3 collective-permute-start.8
  75.4 0.1 pack.6
  75.5 0.1 collective-permute-start.18
  75.6 7.2 %far.8 = (f32[8,4,128,512]{3,2,1,0:T(8,128)}, f32[8,8,512]{2,1,0:T(8,128)S(1)}, bf16[512,4096]{1,0:T(8,128)(2,1)}) custom-call(s32[54]{0:T(128)S(1)} %copy-done.26, bf16[1024,128]{1,0:T(8,128)(2,1)S(1)} %collective-permute-done.9.refs_0_, ...), custom_call_target="tpu_custom_call", output_to_operand_aliasing={{0}: (6, {}), {1}: (7, {}), {2}: (8, {})} | custom-call | flops 25769803776 | bytes 12582912 | tf_op jit(solution)/shard_map/far/pallas_call | solution.py:395
  82.8 1.3 collective-permute-start.14
  84.1 5.3 %collective-permute-done.6.refs_1_ = bf16[1024,128]{1,0:T(8,128)(2,1)S(1)} collective-permute-done((bf16[1024,128]{1,0:T(8,128)(2,1)S(1)}, bf16[1024,128]{1,0:T(8,128)(2,1)S(1)}, u32[]{:S(2)}, u32[]{:S(2)}) %collective-permute-start.6) | collective-permute-done | bytes 262176 | tf_op jit(solution)/shard_map/ppermute | solution.py:363
  89.4 1.3 collective-permute-start.15
  90.7 1.3 collective-permute-start.16
  92.0 1.3 collective-permute-start.17
  93.4 0.1 pack.7
  93.4 0.6 collective-permute-start.20
  94.0 13.4 %far.9 = (f32[8,4,128,512]{3,2,1,0:T(8,128)}, f32[8,8,512]{2,1,0:T(8,128)S(1)}, bf16[512,4096]{1,0:T(8,128)(2,1)}) custom-call(s32[54]{0:T(128)S(1)} %copy-done.26, bf16[1024,128]{1,0:T(8,128)(2,1)S(1)} %collective-permute-done.5.refs_0_, ...), custom_call_target="tpu_custom_call", output_to_operand_aliasing={{0}: (7, {}), {1}: (8, {}), {2}: (9, {})} | custom-call | flops 30064771072 | bytes 14680064 | tf_op jit(solution)/shard_map/far/pallas_call | solution.py:395
  107.4 1.3 collective-permute-start.13
  108.7 12.2 %collective-permute-done.15.refs_1_ = bf16[1024,128]{1,0:T(8,128)(2,1)S(1)} collective-permute-done((bf16[1024,128]{1,0:T(8,128)(2,1)S(1)}, bf16[1024,128]{1,0:T(8,128)(2,1)S(1)}, u32[]{:S(2)}, u32[]{:S(2)}) %collective-permute-start.15) | collective-permute-done | bytes 262176 | tf_op jit(solution)/shard_map/ppermute | solution.py:363
  120.9 0.1 pack.8
  121.0 0.1 collective-permute-start.19
  121.1 0.0 copy-start.2
  121.1 9.8 %far.10 = (f32[8,4,128,512]{3,2,1,0:T(8,128)}, f32[8,8,512]{2,1,0:T(8,128)S(1)}, bf16[512,4096]{1,0:T(8,128)(2,1)}) custom-call(s32[54]{0:T(128)S(1)} %copy-done.26, bf16[1024,128]{1,0:T(8,128)(2,1)S(1)} %collective-permute-done.14.refs_0_, ...), custom_call_target="tpu_custom_call", output_to_operand_aliasing={{0}: (7, {}), {1}: (8, {}), {2}: (9, {})} | custom-call | flops 34359738368 | bytes 16777216 | tf_op jit(solution)/shard_map/far/pallas_call | solution.py:395
  130.9 1.2 far.11
  132.2 14.4 %collective-permute-start.21 = (bf16[1024,128]{1,0:T(8,128)(2,1)S(1)}, bf16[1024,128]{1,0:T(8,128)(2,1)S(1)}, u32[]{:S(2)}, u32[]{:S(2)}) collective-permute-start(bf16[1024,128]{1,0:T(8,128)(2,1)S(1)} %get-tuple-element.111), channel_id=1, source_target_pairs={{0,1},{1,0},{2,3},{3,2},{4,5},{5,4},{6,7},{7,6},{8,9},{9,8},{10,11... | collective-permute-start | bytes 786440 | tf_op jit(solution)/shard_map/ppermute | solution.py:379
  146.5 5.2 %far.12 = (f32[8,4,128,512]{3,2,1,0:T(8,128)}, f32[8,8,512]{2,1,0:T(8,128)S(1)}, bf16[512,4096]{1,0:T(8,128)(2,1)}) custom-call(s32[54]{0:T(128)S(1)} %copy-done.26, bf16[1024,128]{1,0:T(8,128)(2,1)S(1)} %collective-permute-done.13.refs_0_, bf16[512,4096]{1,0:T(8,128)(2,1)S(1)} %copy-done.2, ...), custom_call_target="tpu_custom_call", output_to_operand_aliasing={{0}: (3, {}), {1}: (4, {}), {2}: (5, {})} | custom-call | flops 4294967296 | bytes 2097152 | tf_op jit(solution)/shard_map/far/pallas_call | solution.py:395
  151.7 5.2 %far.13 = (f32[8,4,128,512]{3,2,1,0:T(8,128)}, f32[8,8,512]{2,1,0:T(8,128)S(1)}, bf16[512,4096]{1,0:T(8,128)(2,1)}) custom-call(s32[54]{0:T(128)S(1)} %copy-done.26, bf16[1024,128]{1,0:T(8,128)(2,1)S(1)} %collective-permute-done.21.refs_0_, bf16[512,4096]{1,0:T(8,128)(2,1)S(1)} %copy-done.2, ...), custom_call_target="tpu_custom_call", output_to_operand_aliasing={{0}: (3, {}), {1}: (4, {}), {2}: (5, {})} | custom-call | flops 4294967296 | bytes 2097152 | tf_op jit(solution)/shard_map/far/pallas_call | solution.py:395
  (64 shorter events, 0.2 us)
Async XLA Ops:
  0.0 14.2 %copy-start.7 = (bf16[512,1024]{1,0:T(8,128)(2,1)S(1)}, bf16[512,1024]{1,0:T(8,128)(2,1)}, u32[]{:S(2)}) copy-start(bf16[512,1024]{1,0:T(8,128)(2,1)} %key.3) | copy-start | bytes 3145732
  0.0 14.2 %copy-start.8 = (bf16[512,1024]{1,0:T(8,128)(2,1)S(1)}, bf16[512,1024]{1,0:T(8,128)(2,1)}, u32[]{:S(2)}) copy-start(bf16[512,1024]{1,0:T(8,128)(2,1)} %value.3) | copy-start | bytes 3145732
  0.0 3.8 %collective-permute-start = (bf16[512,1024]{1,0:T(8,128)(2,1)}, bf16[512,1024]{1,0:T(8,128)(2,1)S(1)}, u32[]{:S(2)}, u32[]{:S(2)}) collective-permute-start(bf16[512,1024]{1,0:T(8,128)(2,1)} %key.3), channel_id=1, source_target_pairs={{0,1},{1,0},{2,3},{3,2},{4,5},{5,4},{6,7},{7,6},{8,9},{9,8},{10,11... | collective-permute-start | bytes 3145736 | tf_op jit(solution)/shard_map/ppermute | solution.py:271
  0.0 4.5 %collective-permute-start.1 = (bf16[512,1024]{1,0:T(8,128)(2,1)}, bf16[512,1024]{1,0:T(8,128)(2,1)}, u32[]{:S(2)}, u32[]{:S(2)}) collective-permute-start(bf16[512,1024]{1,0:T(8,128)(2,1)} %value.3), channel_id=1, source_target_pairs={{0,1},{1,0},{2,3},{3,2},{4,5},{5,4},{6,7},{7,6},{8,9},{9,8},{10,11... | collective-permute-start | bytes 3145736 | tf_op jit(solution)/shard_map/ppermute | solution.py:271
  3.8 10.4 %copy-start.25 = (s32[54]{0:T(128)S(1)}, s32[54]{0:T(128)}, u32[]{:S(2)}) copy-start(s32[54]{0:T(128)} %concatenate.3.meta) | copy-start | bytes 652
  3.8 1.0 copy-start.9
  7.7 31.7 %collective-permute-start.2 = (bf16[1024,128]{1,0:T(8,128)(2,1)}, bf16[1024,128]{1,0:T(8,128)(2,1)S(1)}, u32[]{:S(2)}, u32[]{:S(2)}) collective-permute-start(bf16[1024,128]{1,0:T(8,128)(2,1)} %get-tuple-element.62), channel_id=1, source_target_pairs={{0,16},{2,18},{4,20},{6,22},{8,24},{10,26},{12,28},{14,30},{1,17},... | collective-permute-start | bytes 786440 | tf_op jit(solution)/shard_map/ppermute | solution.py:363
  9.0 31.7 %collective-permute-start.3 = (bf16[1024,128]{1,0:T(8,128)(2,1)}, bf16[1024,128]{1,0:T(8,128)(2,1)S(1)}, u32[]{:S(2)}, u32[]{:S(2)}) collective-permute-start(bf16[1024,128]{1,0:T(8,128)(2,1)} %get-tuple-element.63), channel_id=1, source_target_pairs={{0,24},{2,26},{4,28},{6,30},{8,16},{10,18},{12,20},{14,22},{1,25},... | collective-permute-start | bytes 786440 | tf_op jit(solution)/shard_map/ppermute | solution.py:363
  10.3 30.4 %collective-permute-start.4 = (bf16[1024,128]{1,0:T(8,128)(2,1)}, bf16[1024,128]{1,0:T(8,128)(2,1)S(1)}, u32[]{:S(2)}, u32[]{:S(2)}) collective-permute-start(bf16[1024,128]{1,0:T(8,128)(2,1)} %get-tuple-element.64), channel_id=1, source_target_pairs={{0,8},{2,10},{4,12},{6,14},{16,24},{18,26},{20,28},{22,30},{1,9},{... | collective-permute-start | bytes 786440 | tf_op jit(solution)/shard_map/ppermute | solution.py:363
  11.6 59.8 %collective-permute-start.9 = (bf16[1024,128]{1,0:T(8,128)(2,1)}, bf16[1024,128]{1,0:T(8,128)(2,1)S(1)}, u32[]{:S(2)}, u32[]{:S(2)}) collective-permute-start(bf16[1024,128]{1,0:T(8,128)(2,1)} %get-tuple-element.75), channel_id=1, source_target_pairs={{0,18},{2,16},{4,22},{6,20},{8,26},{10,24},{12,30},{14,28},{1,19},... | collective-permute-start | bytes 786440 | tf_op jit(solution)/shard_map/ppermute | solution.py:363
  12.9 59.8 %collective-permute-start.10 = (bf16[1024,128]{1,0:T(8,128)(2,1)}, bf16[1024,128]{1,0:T(8,128)(2,1)S(1)}, u32[]{:S(2)}, u32[]{:S(2)}) collective-permute-start(bf16[1024,128]{1,0:T(8,128)(2,1)} %get-tuple-element.76), channel_id=1, source_target_pairs={{0,26},{2,24},{4,30},{6,28},{8,18},{10,16},{12,22},{14,20},{1,27},... | collective-permute-start | bytes 786440 | tf_op jit(solution)/shard_map/ppermute | solution.py:363
  14.2 1.2 copy-start.10
  35.5 0.6 copy-start.3
  36.2 24.6 %copy-start.26 = (s32[54]{0:T(128)S(1)}, s32[54]{0:T(128)}, u32[]{:S(2)}) copy-start(s32[54]{0:T(128)} %concatenate.3.meta) | copy-start | bytes 652
  39.4 34.7 %collective-permute-start.11 = (bf16[1024,128]{1,0:T(8,128)(2,1)}, bf16[1024,128]{1,0:T(8,128)(2,1)S(1)}, u32[]{:S(2)}, u32[]{:S(2)}) collective-permute-start(bf16[1024,128]{1,0:T(8,128)(2,1)} %get-tuple-element.77), channel_id=1, source_target_pairs={{0,10},{2,8},{4,14},{6,12},{16,26},{18,24},{20,30},{22,28},{1,11},... | collective-permute-start | bytes 786440 | tf_op jit(solution)/shard_map/ppermute | solution.py:363
  40.7 0.9 copy-start.4
  41.6 0.9 copy-start.15
  42.5 0.9 copy-start.18
  43.5 0.9 copy-start.21
  44.5 0.7 copy-start.5
  45.2 0.7 copy-start.16
  45.8 0.7 copy-start.19
  46.5 0.7 copy-start.22
  47.2 35.5 %collective-permute-start.5 = (bf16[1024,128]{1,0:T(8,128)(2,1)}, bf16[1024,128]{1,0:T(8,128)(2,1)S(1)}, u32[]{:S(2)}, u32[]{:S(2)}) collective-permute-start(bf16[1024,128]{1,0:T(8,128)(2,1)} %get-tuple-element.71), channel_id=1, source_target_pairs={{0,20},{2,22},{4,16},{6,18},{8,28},{10,30},{12,24},{14,26},{1,21},... | collective-permute-start | bytes 786440 | tf_op jit(solution)/shard_map/ppermute | solution.py:363
  48.5 26.9 %collective-permute-start.12 = (bf16[3072,128]{1,0:T(8,128)(2,1)S(1)}, bf16[3072,128]{1,0:T(8,128)(2,1)S(1)}, u32[]{:S(2)}, u32[]{:S(2)}) collective-permute-start(bf16[3072,128]{1,0:T(8,128)(2,1)S(1)} %get-tuple-element.78), channel_id=1, source_target_pairs={{0,1},{1,0},{2,3},{3,2},{4,5},{5,4},{6,7},{7,6},{8,9},{9,8},{10,11... | collective-permute-start | bytes 2359304 | tf_op jit(solution)/shard_map/ppermute | solution.py:379
  60.8 2.2 %copy-start = (bf16[512,4096]{1,0:T(8,128)(2,1)S(1)}, bf16[512,4096]{1,0:T(8,128)(2,1)}, u32[]{:S(2)}) copy-start(bf16[512,4096]{1,0:T(8,128)(2,1)} %refs_1_.5) | copy-start | bytes 12582916
  63.0 0.9 copy-start.6
  63.9 7.5 %copy-start.17 = (bf16[1024,128]{1,0:T(8,128)(2,1)S(1)}, bf16[1024,128]{1,0:T(8,128)(2,1)}, u32[]{:S(2)}) copy-start(bf16[1024,128]{1,0:T(8,128)(2,1)} %copy-done.16) | copy-start | bytes 786436
  63.9 8.8 %copy-start.20 = (bf16[1024,128]{1,0:T(8,128)(2,1)S(1)}, bf16[1024,128]{1,0:T(8,128)(2,1)}, u32[]{:S(2)}) copy-start(bf16[1024,128]{1,0:T(8,128)(2,1)} %copy-done.19) | copy-start | bytes 786436
  63.9 10.2 %copy-start.23 = (bf16[1024,128]{1,0:T(8,128)(2,1)S(1)}, bf16[1024,128]{1,0:T(8,128)(2,1)}, u32[]{:S(2)}) copy-start(bf16[1024,128]{1,0:T(8,128)(2,1)} %copy-done.22) | copy-start | bytes 786436
  63.9 11.5 %copy-start.11 = (bf16[1024,128]{1,0:T(8,128)(2,1)S(1)}, bf16[1024,128]{1,0:T(8,128)(2,1)}, u32[]{:S(2)}) copy-start(bf16[1024,128]{1,0:T(8,128)(2,1)} %get-tuple-element.84.refs_4_) | copy-start | bytes 786436
  63.9 11.5 %copy-start.12 = (bf16[1024,128]{1,0:T(8,128)(2,1)S(1)}, bf16[1024,128]{1,0:T(8,128)(2,1)}, u32[]{:S(2)}) copy-start(bf16[1024,128]{1,0:T(8,128)(2,1)} %get-tuple-element.85.refs_5_) | copy-start | bytes 786436
  63.9 11.5 %copy-start.13 = (bf16[1024,128]{1,0:T(8,128)(2,1)S(1)}, bf16[1024,128]{1,0:T(8,128)(2,1)}, u32[]{:S(2)}) copy-start(bf16[1024,128]{1,0:T(8,128)(2,1)} %get-tuple-element.86.refs_6_) | copy-start | bytes 786436
  63.9 11.5 %copy-start.14 = (bf16[1024,128]{1,0:T(8,128)(2,1)S(1)}, bf16[1024,128]{1,0:T(8,128)(2,1)}, u32[]{:S(2)}) copy-start(bf16[1024,128]{1,0:T(8,128)(2,1)} %get-tuple-element.87.refs_7_) | copy-start | bytes 786436
  63.9 11.6 %copy-start.1 = (bf16[512,4096]{1,0:T(8,128)(2,1)S(1)}, bf16[512,4096]{1,0:T(8,128)(2,1)}, u32[]{:S(2)}) copy-start(bf16[512,4096]{1,0:T(8,128)(2,1)} %refs_1_.5) | copy-start | bytes 12582916
  71.4 18.0 %collective-permute-start.6 = (bf16[1024,128]{1,0:T(8,128)(2,1)S(1)}, bf16[1024,128]{1,0:T(8,128)(2,1)S(1)}, u32[]{:S(2)}, u32[]{:S(2)}) collective-permute-start(bf16[1024,128]{1,0:T(8,128)(2,1)S(1)} %copy-done.17), channel_id=1, source_target_pairs={{0,28},{2,30},{4,24},{6,26},{8,20},{10,22},{12,16},{14,18},{1,29},... | collective-permute-start | bytes 786440 | tf_op jit(solution)/shard_map/ppermute | solution.py:363
  72.7 18.0 %collective-permute-start.7 = (bf16[1024,128]{1,0:T(8,128)(2,1)S(1)}, bf16[1024,128]{1,0:T(8,128)(2,1)S(1)}, u32[]{:S(2)}, u32[]{:S(2)}) collective-permute-start(bf16[1024,128]{1,0:T(8,128)(2,1)S(1)} %copy-done.20), channel_id=1, source_target_pairs={{0,12},{2,14},{4,8},{6,10},{16,28},{18,30},{20,24},{22,26},{1,13},... | collective-permute-start | bytes 786440 | tf_op jit(solution)/shard_map/ppermute | solution.py:363
  74.0 18.0 %collective-permute-start.8 = (bf16[1024,128]{1,0:T(8,128)(2,1)S(1)}, bf16[1024,128]{1,0:T(8,128)(2,1)S(1)}, u32[]{:S(2)}, u32[]{:S(2)}) collective-permute-start(bf16[1024,128]{1,0:T(8,128)(2,1)S(1)} %copy-done.23), channel_id=1, source_target_pairs={{0,2},{4,6},{8,10},{12,14},{16,18},{20,22},{24,26},{28,30},{1,3},{... | collective-permute-start | bytes 786440 | tf_op jit(solution)/shard_map/ppermute | solution.py:363
  75.5 18.0 %collective-permute-start.18 = (bf16[3072,128]{1,0:T(8,128)(2,1)S(1)}, bf16[3072,128]{1,0:T(8,128)(2,1)S(1)}, u32[]{:S(2)}, u32[]{:S(2)}) collective-permute-start(bf16[3072,128]{1,0:T(8,128)(2,1)S(1)} %get-tuple-element.97), channel_id=1, source_target_pairs={{0,1},{1,0},{2,3},{3,2},{4,5},{5,4},{6,7},{7,6},{8,9},{9,8},{10,11... | collective-permute-start | bytes 2359304 | tf_op jit(solution)/shard_map/ppermute | solution.py:379
  75.6 17.8 %copy-start.24 = (bf16[1024,128]{1,0:T(8,128)(2,1)S(1)}, bf16[1024,128]{1,0:T(8,128)(2,1)}, u32[]{:S(2)}) copy-start(bf16[1024,128]{1,0:T(8,128)(2,1)} %get-tuple-element.91.refs_5_) | copy-start | bytes 786436
  82.8 24.6 %collective-permute-start.14 = (bf16[1024,128]{1,0:T(8,128)(2,1)S(1)}, bf16[1024,128]{1,0:T(8,128)(2,1)S(1)}, u32[]{:S(2)}, u32[]{:S(2)}) collective-permute-start(bf16[1024,128]{1,0:T(8,128)(2,1)S(1)} %get-tuple-element.93), channel_id=1, source_target_pairs={{0,22},{2,20},{4,18},{6,16},{8,30},{10,28},{12,26},{14,24},{1,23},... | collective-permute-start | bytes 786440 | tf_op jit(solution)/shard_map/ppermute | solution.py:363
  89.4 31.4 %collective-permute-start.15 = (bf16[1024,128]{1,0:T(8,128)(2,1)S(1)}, bf16[1024,128]{1,0:T(8,128)(2,1)S(1)}, u32[]{:S(2)}, u32[]{:S(2)}) collective-permute-start(bf16[1024,128]{1,0:T(8,128)(2,1)S(1)} %get-tuple-element.94), channel_id=1, source_target_pairs={{0,4},{2,6},{8,12},{10,14},{16,20},{18,22},{24,28},{26,30},{1,5},{... | collective-permute-start | bytes 786440 | tf_op jit(solution)/shard_map/ppermute | solution.py:363
  90.7 30.1 %collective-permute-start.16 = (bf16[1024,128]{1,0:T(8,128)(2,1)S(1)}, bf16[1024,128]{1,0:T(8,128)(2,1)S(1)}, u32[]{:S(2)}, u32[]{:S(2)}) collective-permute-start(bf16[1024,128]{1,0:T(8,128)(2,1)S(1)} %get-tuple-element.95), channel_id=1, source_target_pairs={{0,6},{2,4},{8,14},{10,12},{16,22},{18,20},{24,30},{26,28},{1,7},{... | collective-permute-start | bytes 786440 | tf_op jit(solution)/shard_map/ppermute | solution.py:363
  92.0 28.8 %collective-permute-start.17 = (bf16[1024,128]{1,0:T(8,128)(2,1)S(1)}, bf16[1024,128]{1,0:T(8,128)(2,1)S(1)}, u32[]{:S(2)}, u32[]{:S(2)}) collective-permute-start(bf16[1024,128]{1,0:T(8,128)(2,1)S(1)} %get-tuple-element.96), channel_id=1, source_target_pairs={{0,14},{2,12},{4,10},{6,8},{16,30},{18,28},{20,26},{22,24},{1,15},... | collective-permute-start | bytes 786440 | tf_op jit(solution)/shard_map/ppermute | solution.py:363
  93.4 27.6 %collective-permute-start.20 = (bf16[4096,128]{1,0:T(8,128)(2,1)S(1)}, bf16[4096,128]{1,0:T(8,128)(2,1)S(1)}, u32[]{:S(2)}, u32[]{:S(2)}) collective-permute-start(bf16[4096,128]{1,0:T(8,128)(2,1)S(1)} %get-tuple-element.103), channel_id=1, source_target_pairs={{0,1},{1,0},{2,3},{3,2},{4,5},{5,4},{6,7},{7,6},{8,9},{9,8},{10,11... | collective-permute-start | bytes 3145736 | tf_op jit(solution)/shard_map/ppermute | solution.py:379
  107.4 24.7 %collective-permute-start.13 = (bf16[1024,128]{1,0:T(8,128)(2,1)S(1)}, bf16[1024,128]{1,0:T(8,128)(2,1)S(1)}, u32[]{:S(2)}, u32[]{:S(2)}) collective-permute-start(bf16[1024,128]{1,0:T(8,128)(2,1)S(1)} %get-tuple-element.92), channel_id=1, source_target_pairs={{0,30},{2,28},{4,26},{6,24},{8,22},{10,20},{12,18},{14,16},{1,31},... | collective-permute-start | bytes 786440 | tf_op jit(solution)/shard_map/ppermute | solution.py:363
  121.0 9.9 %collective-permute-start.19 = (bf16[4096,128]{1,0:T(8,128)(2,1)S(1)}, bf16[4096,128]{1,0:T(8,128)(2,1)S(1)}, u32[]{:S(2)}, u32[]{:S(2)}) collective-permute-start(bf16[4096,128]{1,0:T(8,128)(2,1)S(1)} %get-tuple-element.102), channel_id=1, source_target_pairs={{0,1},{1,0},{2,3},{3,2},{4,5},{5,4},{6,7},{7,6},{8,9},{9,8},{10,11... | collective-permute-start | bytes 3145736 | tf_op jit(solution)/shard_map/ppermute | solution.py:379
  121.1 9.9 %copy-start.2 = (bf16[512,4096]{1,0:T(8,128)(2,1)S(1)}, bf16[512,4096]{1,0:T(8,128)(2,1)}, u32[]{:S(2)}) copy-start(bf16[512,4096]{1,0:T(8,128)(2,1)} %refs_1_.5) | copy-start | bytes 12582916
  132.2 19.5 %collective-permute-start.21 = (bf16[1024,128]{1,0:T(8,128)(2,1)S(1)}, bf16[1024,128]{1,0:T(8,128)(2,1)S(1)}, u32[]{:S(2)}, u32[]{:S(2)}) collective-permute-start(bf16[1024,128]{1,0:T(8,128)(2,1)S(1)} %get-tuple-element.111), channel_id=1, source_target_pairs={{0,1},{1,0},{2,3},{3,2},{4,5},{5,4},{6,7},{7,6},{8,9},{9,8},{10,11... | collective-permute-start | bytes 786440 | tf_op jit(solution)/shard_map/ppermute | solution.py:379

commit v2 on v1

v2 whole, which is shorter than its diff:
```python
import functools
import math

import jax
import jax.numpy as jnp
import numpy as np
from jax import lax
from jax.experimental import pallas as pl
from jax.experimental.pallas import tpu as pltpu
from jax.sharding import PartitionSpec as P

QH = 32
KVH = 8
HD = 128
BLK = 512
TOPK = 3
GROUP = QH // KVH
KVG = KVH // 2
WIDE = GROUP * HD
ROWS = GROUP * BLK
SCALE = math.log2(math.e) / math.sqrt(HD)
TILE = 128
VMEM = pltpu.VMEM
ANY = pl.ANY


def patterns(peers):
    fast = 4 if peers % 4 == 0 else 1
    slow = peers // fast

    def permute(moves, flip):
        pairs = [(a * fast + f, b * fast + (f ^ flip)) for a, b in moves for f in range(fast)]
        return [(a, b) for a, b in pairs if a < b]

    level = [(a, a) for a in range(slow)]
    if (fast, slow) == (4, 4):
        two, one, zero = [(0, 2), (1, 3)], [(0, 3), (1, 2)], [(0, 1), (2, 3)]
        order = []
        for m in range(3):
            order += [permute(two, m), permute(one, m), permute(zero, m)]
        order += [permute(level, 1), permute(two, 3), permute(level, 2), permute(level, 3), permute(zero, 3)]
        order += [permute(one, 3)]
        edges = [0, 3, 6, 10, 14, 15]
    else:
        order = []
        for m in range(fast):
            order += [permute([(a, a + d) for a in range(slow - d)], m) for d in range(1, slow)]
        order += [permute(level, m) for m in range(1, fast)]
        edges = [round(i * len(order) / 5) for i in range(6)]
    table = np.full((peers, 2 * len(order)), -2, np.int32)
    for n, pairs in enumerate(order):
        for a, b in pairs:
            table[a, n] = b
            table[b, len(order) + n] = a
    return order, table, list(zip(edges[:-1], edges[1:]))


def scores_of(k, q):
    return lax.dot_general(k, q, (((1,), (1,)), ((), ())), preferred_element_type=jnp.float32)


def total_of(vt, weights):
    return jnp.dot(vt, weights.astype(jnp.bfloat16), preferred_element_type=jnp.float32)


def cut_kernel(count, meta, key, value, okey, ovalue, *rest):
    outs, sems = rest[:-1], rest[-1]
    side = meta[0]

    def each(act):
        for j in range(count):
            code = meta[1 + j] - 1
            block, head = code // KVH, code % KVH
            col = pl.multiple_of(jnp.maximum(head, 0) * HD, HD)
            for t, (here, there) in enumerate(((key, okey), (value, ovalue))):
                to = outs[j].at[pl.ds(t * BLK, BLK), :]
                mine = pltpu.make_async_copy(here.at[:, pl.ds(col, HD)], to, sems.at[j, t])
                other = pltpu.make_async_copy(there.at[:, pl.ds(col, HD)], to, sems.at[j, t])
                act(jnp.logical_and(code >= 0, block == side), mine)
                act(jnp.logical_and(code >= 0, block != side), other)

    def start(flag, copy):
        pl.when(flag)(copy.start)

    def wait(flag, copy):
        pl.when(flag)(copy.wait)

    each(start)
    each(wait)


def own_kernel(local_at, work, meta, q, k, v, ok, ov, acc_out, stat_out, out, vt, outs, later, sems):
    low = lax.broadcasted_iota(jnp.int32, (TILE, TILE), 1) >= lax.broadcasted_iota(jnp.int32, (TILE, TILE), 0)
    count_heads(meta, later, work)

    def finish(g):
        return pltpu.make_async_copy(outs.at[g], out.at[:, wide(g)], sems.at[g])

    def head(g, carry):
        cols = pl.ds(pl.multiple_of(g * HD, HD), HD)
        vt[...] = v[:, cols].T
        for r in reversed(range(BLK // TILE)):
            keys, at = (r + 1) * TILE, slice(r * TILE, (r + 1) * TILE)
            for j in range(GROUP):
                scores = scores_of(k[:keys, cols], q[at, part(g, j)])
                last = jnp.where(low, scores[r * TILE :], -1e30)
                scores = jnp.concatenate([scores[: r * TILE], last], axis=0) if r else last
                m = jnp.max(scores, axis=0, keepdims=True)
                weights = jnp.exp2((scores - m) * SCALE)
                stat_out[g, j : j + 1, at] = m
                stat_out[g, GROUP + j : GROUP + j + 1, at] = jnp.sum(weights, axis=0, keepdims=True)
                acc_out[g, j, :, at] = total_of(vt[:, :keys], weights)

        @pl.when(meta[local_at + g] > 0)
        def _():
            vt[...] = ov[:, cols].T
            fold(g, q, ok.at[:, cols], vt, acc_out, stat_out, acc_out, stat_out)

        @pl.when(later[g] == 0)
        def _():
            write_out(g, acc_out, stat_out, outs)
            finish(g).start()

        return carry

    lax.fori_loop(0, KVH, head, 0)
    for g in range(KVH):
        pl.when(later[g] == 0)(finish(g).wait)


def wide(g):
    return pl.ds(pl.multiple_of(g * WIDE, WIDE), WIDE)


def part(g, j):
    return pl.ds(pl.multiple_of(g * WIDE + j * HD, HD), HD)


def count_heads(meta, counts, *spans):
    for g in range(KVH):
        counts[g] = 0

    def count(i, carry):
        g = meta[i]

        @pl.when(g >= 0)
        def _():
            counts[g] = counts[g] + 1

        return carry

    for span in spans:
        lax.fori_loop(*span, count, 0)


def write_out(g, acc, stat, outs):
    for j in range(GROUP):
        total = stat[g, GROUP + j : GROUP + j + 1, :]
        outs[g, :, j * HD : (j + 1) * HD] = (acc[g, j] / total).astype(jnp.bfloat16).T


def fold(g, q, k, vt, acc, stat, acc_out, stat_out):
    for j in range(GROUP):
        for r in range(BLK // TILE):
            at, total = slice(r * TILE, (r + 1) * TILE), GROUP + j
            scores = scores_of(k[...], q[at, part(g, j)])
            m_old = stat[g, j : j + 1, at]
            m = jnp.maximum(m_old, jnp.max(scores, axis=0, keepdims=True))
            weights = jnp.exp2((scores - m) * SCALE)
            alpha = jnp.exp2((m_old - m) * SCALE)
            sums = stat[g, total : total + 1, at] * alpha + jnp.sum(weights, axis=0, keepdims=True)
            stat_out[g, j : j + 1, at] = m
            stat_out[g, total : total + 1, at] = sums
            acc_out[g, j, :, at] = acc[g, j, :, at] * alpha + total_of(vt[...], weights)


def far_kernel(n_here, n_swap, here_at, here_later, swap_at, swap_later, meta, *refs):
    arrived, refs = refs[:n_here], refs[n_here:]
    swapped, refs = refs[:n_swap], refs[n_swap:]
    q, acc, stat, _, acc_out, stat_out, out, outs, kv, vt, seen, here, later, kv_sem, out_sem = refs
    pieces = n_here + (swapped[0].shape[0] // (2 * BLK) if n_swap else 0)

    def finish(g):
        return pltpu.make_async_copy(outs.at[g], out.at[:, wide(g)], out_sem.at[g])

    for i in range(pieces):
        g = meta[here_at + i] if i < n_here else meta[swap_at + i - n_here]
        block = arrived[i] if i < n_here else swapped[0].at[pl.ds((i - n_here) * 2 * BLK, 2 * BLK), :]
        pl.when(g >= 0)(pltpu.make_async_copy(block, kv.at[i], kv_sem.at[i]).start)

    count_heads(meta, here, (here_at, here_at + n_here), (swap_at, swap_at + pieces - n_here))
    count_heads(meta, later, here_later, swap_later)
    for g in range(KVH):
        seen[g] = 0

        @pl.when(jnp.logical_and(later[g] > 0, here[g] == 0))
        def _():
            acc_out[g] = acc[g]
            stat_out[g] = stat[g]

    def piece(i, carry):
        g = meta[jnp.where(i < n_here, here_at + i, swap_at + i - n_here)]

        @pl.when(g >= 0)
        def _():
            @pl.when(seen[g] == 0)
            def _():
                acc_out[g] = acc[g]
                stat_out[g] = stat[g]

            pltpu.make_async_copy(kv.at[i], kv.at[i], kv_sem.at[i]).wait()
            vt[...] = kv[i, BLK:, :].T
            fold(g, q, kv.at[i, pl.ds(0, BLK), :], vt, acc_out, stat_out, acc_out, stat_out)
            seen[g] = seen[g] + 1

            @pl.when(jnp.logical_and(seen[g] == here[g], later[g] == 0))
            def _():
                write_out(g, acc_out, stat_out, outs)
                finish(g).start()

        return carry

    lax.fori_loop(0, pieces, piece, 0)
    for g in range(KVH):
        pl.when(jnp.logical_and(here[g] > 0, later[g] == 0))(finish(g).wait)


def pack_kernel(count, *refs):
    joined = refs[count + 1]
    for i in range(count):
        joined[i * 2 * BLK : (i + 1) * 2 * BLK, :] = refs[i][...]
    refs[count + 2][...] = refs[count][...]


def body(queries, key, value, selection):
    me, side = lax.axis_index("ctx"), lax.axis_index("head")
    peers = lax.axis_size("ctx")
    order, table, groups = patterns(peers)
    total = len(order)
    swap = [(0, 1), (1, 0)]
    okey, ovalue = lax.ppermute(key, "head", swap), lax.ppermute(value, "head", swap)

    ends = lax.dynamic_index_in_dim(jnp.asarray(table), me, 0, keepdims=False)
    targets, sources = ends[:total], ends[total:]
    picks = selection[:, :, 1:]
    asked = lax.dynamic_slice_in_dim(picks, side * KVG, KVG, 1)
    codes = (asked - 2 * me) * KVH + (side * KVG + jnp.arange(KVG, dtype=jnp.int32))[None, :, None] + 1
    wanted = jnp.max(
        jnp.where((asked >> 1) == me, codes, 0).reshape(peers, 2 * KVG * TOPK), axis=1
    )
    cuts = jnp.max(
        jnp.where(targets[:, None] == jnp.arange(peers, dtype=jnp.int32)[None, :], wanted[None, :], 0), axis=1
    )
    mine = lax.dynamic_slice_in_dim(picks, 2 * me + side, 1, 0)[0]
    owners = jnp.where(mine >= 0, mine >> 1, -1)
    local = jnp.any(owners == me, axis=1).astype(jnp.int32)
    heads = jnp.arange(KVH, dtype=jnp.int32)
    hit = jnp.any(owners[None, :, :] == sources[:, None, None], axis=2)
    near = (heads // KVG) == side
    work_here = jnp.max(jnp.where(hit & near, heads, -1), axis=1)
    work_swap = jnp.max(jnp.where(hit & ~near, heads, -1), axis=1)
    meta = jnp.concatenate([side[None].astype(jnp.int32), cuts, local, work_here, work_swap])
    local_at = 1 + total
    here_at = local_at + KVH
    swap_at = here_at + total
    end = swap_at + total

    piece_shape = jax.ShapeDtypeStruct((2 * BLK, HD), jnp.bfloat16)
    any_spec, vmem_spec = pl.BlockSpec(memory_space=ANY), pl.BlockSpec(memory_space=VMEM)
    state = (
        jax.ShapeDtypeStruct((KVH, GROUP, HD, BLK), jnp.float32),
        jax.ShapeDtypeStruct((KVH, 2 * GROUP, BLK), jnp.float32),
        jax.ShapeDtypeStruct((BLK, QH * HD), jnp.bfloat16),
    )
    params = pltpu.CompilerParams(vmem_limit_bytes=16 << 20)

    sent = pl.pallas_call(
        functools.partial(cut_kernel, total),
        grid_spec=pltpu.PrefetchScalarGridSpec(
            num_scalar_prefetch=1,
            grid=(),
            in_specs=[vmem_spec] * 4,
            out_specs=[any_spec] * total,
            scratch_shapes=[pltpu.SemaphoreType.DMA((total, 2))],
        ),
        out_shape=[piece_shape] * total,
        compiler_params=params,
        cost_estimate=pl.CostEstimate(flops=0, bytes_accessed=total << 19, transcendentals=0),
        name="cut",
    )(meta, key, value, okey, ovalue)

    piece_flops = 4 * ROWS * BLK * HD
    acc, stat, out = pl.pallas_call(
        functools.partial(own_kernel, local_at, (here_at, end)),
        grid_spec=pltpu.PrefetchScalarGridSpec(
            num_scalar_prefetch=1,
            grid=(),
            in_specs=[vmem_spec] * 5,
            out_specs=[vmem_spec, vmem_spec, any_spec],
            scratch_shapes=[
                VMEM((HD, BLK), jnp.bfloat16),
                VMEM((KVH, BLK, WIDE), jnp.bfloat16),
                pltpu.SMEM((KVH,), jnp.int32),
                pltpu.SemaphoreType.DMA((KVH,)),
            ],
        ),
        out_shape=state,
        compiler_params=params,
        cost_estimate=pl.CostEstimate(
            flops=32 * piece_flops, bytes_accessed=28 << 20, transcendentals=12 * ROWS * BLK
        ),
        name="own",
    )(meta, queries, key, value, okey, ovalue)

    landed = [None] * total
    swapped = []

    def send(n):
        a, b = groups[n]
        for j in range(a, b):
            landed[j] = lax.ppermute(sent[j], "ctx", order[j])

    def pack(n, stat):
        a, b = groups[n]
        count = b - a
        joined, stat = pl.pallas_call(
            functools.partial(pack_kernel, count),
            in_specs=[vmem_spec] * (count + 1),
            out_specs=[vmem_spec] * 2,
            out_shape=(jax.ShapeDtypeStruct((count * 2 * BLK, HD), jnp.bfloat16), state[1]),
            input_output_aliases={count: 1},
            compiler_params=params,
            cost_estimate=pl.CostEstimate(flops=0, bytes_accessed=count << 19, transcendentals=0),
            name="pack",
        )(*landed[a:b], stat)
        swapped.append(lax.ppermute(joined, "head", swap))
        return stat

    def far(here, swaps, acc, stat, out):
        a, b = groups[here] if here is not None else (0, 0)
        a0, b0 = groups[swaps] if swaps is not None else (0, 0)
        here_end = max(b, b0)
        swap_end = b0 if swaps is not None else (groups[here - 1][1] if here else 0)
        n_here = b - a
        pieces = n_here + b0 - a0
        others = [swapped[swaps]] if swaps is not None else []
        base = 1 + n_here + len(others)
        return pl.pallas_call(
            functools.partial(
                far_kernel, n_here, len(others),
                here_at + a, (here_at + here_end, swap_at), swap_at + a0, (swap_at + swap_end, end),
            ),
            grid_spec=pltpu.PrefetchScalarGridSpec(
                num_scalar_prefetch=1,
                grid=(),
                in_specs=[any_spec] * (base - 1) + [vmem_spec] * 3 + [any_spec],
                out_specs=[vmem_spec, vmem_spec, any_spec],
                scratch_shapes=[
                    VMEM((KVH, BLK, WIDE), jnp.bfloat16),
                    VMEM((pieces, 2 * BLK, HD), jnp.bfloat16),
                    VMEM((HD, BLK), jnp.bfloat16),
                    pltpu.SMEM((KVH,), jnp.int32),
                    pltpu.SMEM((KVH,), jnp.int32),
                    pltpu.SMEM((KVH,), jnp.int32),
                    pltpu.SemaphoreType.DMA((pieces,)),
                    pltpu.SemaphoreType.DMA((KVH,)),
                ],
            ),
            out_shape=state,
            input_output_aliases={base + 1 + i: i for i in range(3)},
            compiler_params=params,
            cost_estimate=pl.CostEstimate(
                flops=8 * pieces * piece_flops, bytes_accessed=pieces << 21, transcendentals=pieces * ROWS * BLK
            ),
            name="far",
        )(meta, *landed[a:b], *others, queries, acc, stat, out)

    for n in range(len(groups)):
        send(n)
    last = len(groups) - 1
    for n in range(last):
        stat = pack(n, stat)
        acc, stat, out = far(n, n - 1 if n else None, acc, stat, out)
    acc, stat, out = far(None, last - 1, acc, stat, out)
    stat = pack(last, stat)
    acc, stat, out = far(last, None, acc, stat, out)
    acc, stat, out = far(None, last, acc, stat, out)
    return out


def solution(mesh):
    placed = (P(("ctx", "head"), None), P(("ctx", "head"), None), P(("ctx", "head"), None), P())
    return jax.shard_map(
        body, mesh=mesh, in_specs=placed, out_specs=P(("ctx", "head"), None), check_vma=False
    )
```

time: 156 us -> 146 us (0.936)
  the two profiles are of different devices: /device:TPU:30 before, /device:TPU:29 now
where the time goes in v2:
time: 146 us; the launch traced here: 148 us
  Pallas kernels  73.5 us (50%)
  waiting for transfers between devices  38.9 us (27%)
  starting transfers between devices  29.5 us (20%)
  local copies, waits for them, and re-layouts  4.21 us (3%)
    pallas_call x7, Pallas kernels, far(): pl.pallas_call(functools.partial(far_kernel, n_here, len(others), here_at...  40.9 us
    ppermute x15, waiting for transfers between devices, send(): landed[j] = lax.ppermute(sent[j], 'ctx', order[j])  37.6 us
    pallas_call x1, Pallas kernels, body(): pl.pallas_call(functools.partial(own_kernel, local_at, (here_at, end)), g...  30.8 us
    ppermute x15, starting transfers between devices, send(): landed[j] = lax.ppermute(sent[j], 'ctx', order[j])  21.5 us
    ppermute x5, starting transfers between devices, pack(): swapped.append(lax.ppermute(joined, 'head', swap))  7.33 us
  transfers between devices with their start and end apart: 22, of which 6 were waited for; matrix products, arithmetic and copies ran while one was open for 2% of the time, Pallas kernels for 46%

profile of v2, /device:TPU:29, one launch (start us, length us, event | category | flops | bytes accessed | tf_op | source)
XLA Modules:
  0.0 147.6 jit_solution(6637727097075873489)
XLA Ops:
  0.0 0.7 collective-permute-start
  0.7 0.0 collective-permute-start.1
  0.7 0.7 slice.12
  1.4 0.3 compare_reduce_fusion
  1.7 0.1 copy.36
  1.8 0.1 select_reduce_fusion.1
  1.9 0.1 reduce_max.44
  2.0 0.1 reduce_max.45
  2.1 0.7 constant_dynamic-slice_fusion
  2.9 0.1 slice_bitcast_fusion
  2.9 0.2 select_reduce_fusion
  3.1 0.1 compare_reduce_fusion.1
  3.2 0.1 select_reduce_fusion.2
  3.3 0.1 concatenate.3.meta
  3.4 0.0 collective-permute-done.okey.ok
  3.4 1.3 collective-permute-done.1.ovalue.ov
  4.7 1.2 copy-done.1
  5.9 1.2 copy-done.2
  7.1 1.5 %cut.1 = (bf16[1024,128]{1,0:T(8,128)(2,1)S(1)}, bf16[1024,128]{1,0:T(8,128)(2,1)S(1)}, bf16[1024,128]{1,0:T(8,128)(2,1)S(1)}, bf16[1024,128]{1,0:T(8,128)(2,1)S...) custom-call(s32[54]{0:T(128)S(1)} %concatenate.3.meta, ...), custom_call_target="tpu_custom_call" | custom-call | bytes 7864320 | tf_op jit(solution)/shard_map/cut/pallas_call | solution.py:277
  8.7 1.3 collective-permute-start.7
  10.0 1.3 collective-permute-start.11
  11.3 1.3 collective-permute-start.14
  12.6 1.3 collective-permute-start.15
  13.9 1.3 collective-permute-start.16
  15.2 30.8 %own.1 = (f32[8,4,128,512]{3,2,1,0:T(8,128)S(1)}, f32[8,8,512]{2,1,0:T(8,128)S(1)}, bf16[512,4096]{1,0:T(8,128)(2,1)}) custom-call(s32[54]{0:T(128)S(1)} %concatenate.3.meta, bf16[512,4096]{1,0:T(8,128)(2,1)S(1)} %copy-done, bf16[512,1024]{1,0:T(8,128)(2,1)S(1)} %copy-done.1, bf16[512,1024]{1,0:T(8,128)(2,1)S(1)} %copy-done.2, ...), custom_call_target="tpu_custom_call" | custom-call | flops 17179869184 | bytes 29360128 | tf_op jit(solution)/shard_map/own/pallas_call | solution.py:293
  45.9 7.4 %collective-permute-done.14.refs_0_ = bf16[1024,128]{1,0:T(8,128)(2,1)S(1)} collective-permute-done((bf16[1024,128]{1,0:T(8,128)(2,1)S(1)}, bf16[1024,128]{1,0:T(8,128)(2,1)S(1)}, u32[]{:S(2)}, u32[]{:S(2)}) %collective-permute-start.14) | collective-permute-done | bytes 262176 | tf_op jit(solution)/shard_map/ppermute | solution.py:321
  53.3 1.3 collective-permute-start.12
  54.6 0.0 collective-permute-done.15.refs_1_
  54.6 1.3 collective-permute-start.13
  55.9 0.1 pack.5
  56.0 1.0 collective-permute-start.18
  57.0 2.1 %far.7 = (f32[8,4,128,512]{3,2,1,0:T(8,128)S(1)}, f32[8,8,512]{2,1,0:T(8,128)S(1)}, bf16[512,4096]{1,0:T(8,128)(2,1)}) custom-call(s32[54]{0:T(128)S(1)} %concatenate.3.meta, bf16[1024,128]{1,0:T(8,128)(2,1)S(1)} %collective-permute-done.14.refs_0_, ...), custom_call_target="tpu_custom_call", output_to_operand_aliasing={{0}: (5, {}), {1}: (6, {}), {2}: (7, {})} | custom-call | flops 12884901888 | bytes 6291456 | tf_op jit(solution)/shard_map/far/pallas_call | solution.py:348
  59.0 0.0 collective-permute-done.11.refs_0_
  59.0 1.3 collective-permute-start.8
  60.3 4.5 %collective-permute-done.12.refs_1_ = bf16[1024,128]{1,0:T(8,128)(2,1)S(1)} collective-permute-done((bf16[1024,128]{1,0:T(8,128)(2,1)S(1)}, bf16[1024,128]{1,0:T(8,128)(2,1)S(1)}, u32[]{:S(2)}, u32[]{:S(2)}) %collective-permute-start.12) | collective-permute-done | bytes 262176 | tf_op jit(solution)/shard_map/ppermute | solution.py:321
  64.9 1.3 collective-permute-start.9
  66.2 6.6 %collective-permute-done.13.refs_2_ = bf16[1024,128]{1,0:T(8,128)(2,1)S(1)} collective-permute-done((bf16[1024,128]{1,0:T(8,128)(2,1)S(1)}, bf16[1024,128]{1,0:T(8,128)(2,1)S(1)}, u32[]{:S(2)}, u32[]{:S(2)}) %collective-permute-start.13) | collective-permute-done | bytes 262176 | tf_op jit(solution)/shard_map/ppermute | solution.py:321
  72.8 3.4 %collective-permute-start.10 = (bf16[1024,128]{1,0:T(8,128)(2,1)S(1)}, bf16[1024,128]{1,0:T(8,128)(2,1)S(1)}, u32[]{:S(2)}, u32[]{:S(2)}) collective-permute-start(bf16[1024,128]{1,0:T(8,128)(2,1)S(1)} %get-tuple-element.60), channel_id=1, source_target_pairs={{0,2},{4,6},{8,10},{12,14},{16,18},{20,22},{24,26},{28,30},{1,3},{... | collective-permute-start | bytes 786440 | tf_op jit(solution)/shard_map/ppermute | solution.py:321
  76.2 0.1 pack.6
  76.3 0.0 collective-permute-done.18.refs_3_
  76.3 0.9 collective-permute-start.17
  77.2 11.1 %far.8 = (f32[8,4,128,512]{3,2,1,0:T(8,128)S(1)}, f32[8,8,512]{2,1,0:T(8,128)S(1)}, bf16[512,4096]{1,0:T(8,128)(2,1)}) custom-call(s32[54]{0:T(128)S(1)} %concatenate.3.meta, bf16[1024,128]{1,0:T(8,128)(2,1)S(1)} %collective-permute-done.11.refs_0_, ...), custom_call_target="tpu_custom_call", output_to_operand_aliasing={{0}: (6, {}), {1}: (7, {}), {2}: (8, {})} | custom-call | flops 25769803776 | bytes 12582912 | tf_op jit(solution)/shard_map/far/pallas_call | solution.py:348
  88.3 0.0 collective-permute-done.7.refs_0_
  88.4 1.3 collective-permute-start.3
  89.7 1.3 collective-permute-start.4
  91.0 0.0 collective-permute-done.9.refs_2_
  91.0 1.3 collective-permute-start.5
  92.3 0.0 collective-permute-done.10.refs_3_
  92.3 1.3 collective-permute-start.6
  93.6 0.1 pack.7
  93.7 0.1 collective-permute-start.20
  93.8 7.6 %far.9 = (f32[8,4,128,512]{3,2,1,0:T(8,128)S(1)}, f32[8,8,512]{2,1,0:T(8,128)S(1)}, bf16[512,4096]{1,0:T(8,128)(2,1)}) custom-call(s32[54]{0:T(128)S(1)} %concatenate.3.meta, bf16[1024,128]{1,0:T(8,128)(2,1)S(1)} %collective-permute-done.7.refs_0_, ...), custom_call_target="tpu_custom_call", output_to_operand_aliasing={{0}: (7, {}), {1}: (8, {}), {2}: (9, {})} | custom-call | flops 30064771072 | bytes 14680064 | tf_op jit(solution)/shard_map/far/pallas_call | solution.py:348
  101.4 0.3 collective-permute-done.3.refs_0_
  101.7 1.3 collective-permute-start.2
  103.0 18.8 %collective-permute-done.4.refs_1_ = bf16[1024,128]{1,0:T(8,128)(2,1)S(1)} collective-permute-done((bf16[1024,128]{1,0:T(8,128)(2,1)S(1)}, bf16[1024,128]{1,0:T(8,128)(2,1)S(1)}, u32[]{:S(2)}, u32[]{:S(2)}) %collective-permute-start.4) | collective-permute-done | bytes 262176 | tf_op jit(solution)/shard_map/ppermute | solution.py:321
  121.7 0.1 pack.8
  121.8 0.4 collective-permute-start.19
  122.3 0.0 collective-permute-done.20.refs_4_
  122.3 5.8 %far.10 = (f32[8,4,128,512]{3,2,1,0:T(8,128)S(1)}, f32[8,8,512]{2,1,0:T(8,128)S(1)}, bf16[512,4096]{1,0:T(8,128)(2,1)}) custom-call(s32[54]{0:T(128)S(1)} %concatenate.3.meta, bf16[1024,128]{1,0:T(8,128)(2,1)S(1)} %collective-permute-done.3.refs_0_, ...), custom_call_target="tpu_custom_call", output_to_operand_aliasing={{0}: (7, {}), {1}: (8, {}), {2}: (9, {})} | custom-call | flops 34359738368 | bytes 16777216 | tf_op jit(solution)/shard_map/far/pallas_call | solution.py:348
  128.1 6.7 %far.11 = (f32[8,4,128,512]{3,2,1,0:T(8,128)S(1)}, f32[8,8,512]{2,1,0:T(8,128)S(1)}, bf16[512,4096]{1,0:T(8,128)(2,1)}) custom-call(s32[54]{0:T(128)S(1)} %concatenate.3.meta, bf16[4096,128]{1,0:T(8,128)(2,1)S(1)} %collective-permute-done.19.refs_0_, bf16[512,4096]{1,0:T(8,128)(2,1)S(1)} %copy-done, ...), custom_call_target="tpu_custom_call", output_to_operand_aliasing={{0}: (3, {}), {1}: (4, {}), {2}: (5, {})} | custom-call | flops 17179869184 | bytes 8388608 | tf_op jit(solution)/shard_map/far/pallas_call | solution.py:348
  134.8 0.0 collective-permute-done.2.refs_0_
  134.8 4.9 %collective-permute-start.21 = (bf16[1024,128]{1,0:T(8,128)(2,1)S(1)}, bf16[1024,128]{1,0:T(8,128)(2,1)S(1)}, u32[]{:S(2)}, u32[]{:S(2)}) collective-permute-start(bf16[1024,128]{1,0:T(8,128)(2,1)S(1)} %get-tuple-element.91), channel_id=1, source_target_pairs={{0,1},{1,0},{2,3},{3,2},{4,5},{5,4},{6,7},{7,6},{8,9},{9,8},{10,11... | collective-permute-start | bytes 786440 | tf_op jit(solution)/shard_map/ppermute | solution.py:336
  139.7 3.9 %far.12 = (f32[8,4,128,512]{3,2,1,0:T(8,128)S(1)}, f32[8,8,512]{2,1,0:T(8,128)S(1)}, bf16[512,4096]{1,0:T(8,128)(2,1)}) custom-call(s32[54]{0:T(128)S(1)} %concatenate.3.meta, bf16[1024,128]{1,0:T(8,128)(2,1)S(1)} %collective-permute-done.2.refs_0_, bf16[512,4096]{1,0:T(8,128)(2,1)S(1)} %copy-done, ...), custom_call_target="tpu_custom_call", output_to_operand_aliasing={{0}: (3, {}), {1}: (4, {}), {2}: (5, {})} | custom-call | flops 4294967296 | bytes 2097152 | tf_op jit(solution)/shard_map/far/pallas_call | solution.py:348
  143.6 3.7 %far.13 = (f32[8,4,128,512]{3,2,1,0:T(8,128)S(1)}, f32[8,8,512]{2,1,0:T(8,128)S(1)}, bf16[512,4096]{1,0:T(8,128)(2,1)}) custom-call(s32[54]{0:T(128)S(1)} %concatenate.3.meta, bf16[1024,128]{1,0:T(8,128)(2,1)S(1)} %collective-permute-done.21.refs_0_, bf16[512,4096]{1,0:T(8,128)(2,1)S(1)} %copy-done, ...), custom_call_target="tpu_custom_call", output_to_operand_aliasing={{0}: (3, {}), {1}: (4, {}), {2}: (5, {})} | custom-call | flops 4294967296 | bytes 2097152 | tf_op jit(solution)/shard_map/far/pallas_call | solution.py:348
  (15 shorter events, 0.1 us)
Async XLA Ops:
  0.0 3.4 %collective-permute-start = (bf16[512,1024]{1,0:T(8,128)(2,1)}, bf16[512,1024]{1,0:T(8,128)(2,1)S(1)}, u32[]{:S(2)}, u32[]{:S(2)}) collective-permute-start(bf16[512,1024]{1,0:T(8,128)(2,1)} %k.1), channel_id=1, source_target_pairs={{0,1},{1,0},{2,3},{3,2},{4,5},{5,4},{6,7},{7,6},{8,9},{9,8},{10,11... | collective-permute-start | bytes 3145736 | tf_op jit(solution)/shard_map/ppermute | solution.py:241
  0.7 4.0 %collective-permute-start.1 = (bf16[512,1024]{1,0:T(8,128)(2,1)}, bf16[512,1024]{1,0:T(8,128)(2,1)S(1)}, u32[]{:S(2)}, u32[]{:S(2)}) collective-permute-start(bf16[512,1024]{1,0:T(8,128)(2,1)} %v.1), channel_id=1, source_target_pairs={{0,1},{1,0},{2,3},{3,2},{4,5},{5,4},{6,7},{7,6},{8,9},{9,8},{10,11... | collective-permute-start | bytes 3145736 | tf_op jit(solution)/shard_map/ppermute | solution.py:241
  3.4 11.8 %copy-start = (bf16[512,4096]{1,0:T(8,128)(2,1)S(1)}, bf16[512,4096]{1,0:T(8,128)(2,1)}, u32[]{:S(2)}) copy-start(bf16[512,4096]{1,0:T(8,128)(2,1)} %refs_1_.5) | copy-start | bytes 12582916
  4.7 1.2 copy-start.1
  5.9 1.2 copy-start.2
  8.7 79.7 %collective-permute-start.7 = (bf16[1024,128]{1,0:T(8,128)(2,1)S(1)}, bf16[1024,128]{1,0:T(8,128)(2,1)S(1)}, u32[]{:S(2)}, u32[]{:S(2)}) collective-permute-start(bf16[1024,128]{1,0:T(8,128)(2,1)S(1)} %get-tuple-element.57), channel_id=1, source_target_pairs={{0,20},{2,22},{4,16},{6,18},{8,28},{10,30},{12,24},{14,26},{1,21},... | collective-permute-start | bytes 786440 | tf_op jit(solution)/shard_map/ppermute | solution.py:321
  10.0 49.1 %collective-permute-start.11 = (bf16[1024,128]{1,0:T(8,128)(2,1)S(1)}, bf16[1024,128]{1,0:T(8,128)(2,1)S(1)}, u32[]{:S(2)}, u32[]{:S(2)}) collective-permute-start(bf16[1024,128]{1,0:T(8,128)(2,1)S(1)} %get-tuple-element.61), channel_id=1, source_target_pairs={{0,18},{2,16},{4,22},{6,20},{8,26},{10,24},{12,30},{14,28},{1,19},... | collective-permute-start | bytes 786440 | tf_op jit(solution)/shard_map/ppermute | solution.py:321
  11.3 42.0 %collective-permute-start.14 = (bf16[1024,128]{1,0:T(8,128)(2,1)S(1)}, bf16[1024,128]{1,0:T(8,128)(2,1)S(1)}, u32[]{:S(2)}, u32[]{:S(2)}) collective-permute-start(bf16[1024,128]{1,0:T(8,128)(2,1)S(1)} %get-tuple-element.64), channel_id=1, source_target_pairs={{0,16},{2,18},{4,20},{6,22},{8,24},{10,26},{12,28},{14,30},{1,17},... | collective-permute-start | bytes 786440 | tf_op jit(solution)/shard_map/ppermute | solution.py:321
  12.6 42.0 %collective-permute-start.15 = (bf16[1024,128]{1,0:T(8,128)(2,1)S(1)}, bf16[1024,128]{1,0:T(8,128)(2,1)S(1)}, u32[]{:S(2)}, u32[]{:S(2)}) collective-permute-start(bf16[1024,128]{1,0:T(8,128)(2,1)S(1)} %get-tuple-element.65), channel_id=1, source_target_pairs={{0,24},{2,26},{4,28},{6,30},{8,16},{10,18},{12,20},{14,22},{1,25},... | collective-permute-start | bytes 786440 | tf_op jit(solution)/shard_map/ppermute | solution.py:321
  13.9 42.0 %collective-permute-start.16 = (bf16[1024,128]{1,0:T(8,128)(2,1)S(1)}, bf16[1024,128]{1,0:T(8,128)(2,1)S(1)}, u32[]{:S(2)}, u32[]{:S(2)}) collective-permute-start(bf16[1024,128]{1,0:T(8,128)(2,1)S(1)} %get-tuple-element.66), channel_id=1, source_target_pairs={{0,8},{2,10},{4,12},{6,14},{16,24},{18,26},{20,28},{22,30},{1,9},{... | collective-permute-start | bytes 786440 | tf_op jit(solution)/shard_map/ppermute | solution.py:321
  53.3 11.6 %collective-permute-start.12 = (bf16[1024,128]{1,0:T(8,128)(2,1)S(1)}, bf16[1024,128]{1,0:T(8,128)(2,1)S(1)}, u32[]{:S(2)}, u32[]{:S(2)}) collective-permute-start(bf16[1024,128]{1,0:T(8,128)(2,1)S(1)} %get-tuple-element.62), channel_id=1, source_target_pairs={{0,26},{2,24},{4,30},{6,28},{8,18},{10,16},{12,22},{14,20},{1,27},... | collective-permute-start | bytes 786440 | tf_op jit(solution)/shard_map/ppermute | solution.py:321
  54.6 18.2 %collective-permute-start.13 = (bf16[1024,128]{1,0:T(8,128)(2,1)S(1)}, bf16[1024,128]{1,0:T(8,128)(2,1)S(1)}, u32[]{:S(2)}, u32[]{:S(2)}) collective-permute-start(bf16[1024,128]{1,0:T(8,128)(2,1)S(1)} %get-tuple-element.63), channel_id=1, source_target_pairs={{0,10},{2,8},{4,14},{6,12},{16,26},{18,24},{20,30},{22,28},{1,11},... | collective-permute-start | bytes 786440 | tf_op jit(solution)/shard_map/ppermute | solution.py:321
  56.0 20.3 %collective-permute-start.18 = (bf16[3072,128]{1,0:T(8,128)(2,1)S(1)}, bf16[3072,128]{1,0:T(8,128)(2,1)S(1)}, u32[]{:S(2)}, u32[]{:S(2)}) collective-permute-start(bf16[3072,128]{1,0:T(8,128)(2,1)S(1)} %get-tuple-element.73), channel_id=1, source_target_pairs={{0,1},{1,0},{2,3},{3,2},{4,5},{5,4},{6,7},{7,6},{8,9},{9,8},{10,11... | collective-permute-start | bytes 2359304 | tf_op jit(solution)/shard_map/ppermute | solution.py:336
  59.0 30.6 %collective-permute-start.8 = (bf16[1024,128]{1,0:T(8,128)(2,1)S(1)}, bf16[1024,128]{1,0:T(8,128)(2,1)S(1)}, u32[]{:S(2)}, u32[]{:S(2)}) collective-permute-start(bf16[1024,128]{1,0:T(8,128)(2,1)S(1)} %get-tuple-element.58), channel_id=1, source_target_pairs={{0,28},{2,30},{4,24},{6,26},{8,20},{10,22},{12,16},{14,18},{1,29},... | collective-permute-start | bytes 786440 | tf_op jit(solution)/shard_map/ppermute | solution.py:321
  64.9 26.1 %collective-permute-start.9 = (bf16[1024,128]{1,0:T(8,128)(2,1)S(1)}, bf16[1024,128]{1,0:T(8,128)(2,1)S(1)}, u32[]{:S(2)}, u32[]{:S(2)}) collective-permute-start(bf16[1024,128]{1,0:T(8,128)(2,1)S(1)} %get-tuple-element.59), channel_id=1, source_target_pairs={{0,12},{2,14},{4,8},{6,10},{16,28},{18,30},{20,24},{22,26},{1,13},... | collective-permute-start | bytes 786440 | tf_op jit(solution)/shard_map/ppermute | solution.py:321
  72.8 19.5 %collective-permute-start.10 = (bf16[1024,128]{1,0:T(8,128)(2,1)S(1)}, bf16[1024,128]{1,0:T(8,128)(2,1)S(1)}, u32[]{:S(2)}, u32[]{:S(2)}) collective-permute-start(bf16[1024,128]{1,0:T(8,128)(2,1)S(1)} %get-tuple-element.60), channel_id=1, source_target_pairs={{0,2},{4,6},{8,10},{12,14},{16,18},{20,22},{24,26},{28,30},{1,3},{... | collective-permute-start | bytes 786440 | tf_op jit(solution)/shard_map/ppermute | solution.py:321
  76.3 17.4 %collective-permute-start.17 = (bf16[3072,128]{1,0:T(8,128)(2,1)S(1)}, bf16[3072,128]{1,0:T(8,128)(2,1)S(1)}, u32[]{:S(2)}, u32[]{:S(2)}) collective-permute-start(bf16[3072,128]{1,0:T(8,128)(2,1)S(1)} %get-tuple-element.72), channel_id=1, source_target_pairs={{0,1},{1,0},{2,3},{3,2},{4,5},{5,4},{6,7},{7,6},{8,9},{9,8},{10,11... | collective-permute-start | bytes 2359304 | tf_op jit(solution)/shard_map/ppermute | solution.py:336
  88.4 13.3 %collective-permute-start.3 = (bf16[1024,128]{1,0:T(8,128)(2,1)S(1)}, bf16[1024,128]{1,0:T(8,128)(2,1)S(1)}, u32[]{:S(2)}, u32[]{:S(2)}) collective-permute-start(bf16[1024,128]{1,0:T(8,128)(2,1)S(1)} %get-tuple-element.53), channel_id=1, source_target_pairs={{0,22},{2,20},{4,18},{6,16},{8,30},{10,28},{12,26},{14,24},{1,23},... | collective-permute-start | bytes 786440 | tf_op jit(solution)/shard_map/ppermute | solution.py:321
  89.7 32.1 %collective-permute-start.4 = (bf16[1024,128]{1,0:T(8,128)(2,1)S(1)}, bf16[1024,128]{1,0:T(8,128)(2,1)S(1)}, u32[]{:S(2)}, u32[]{:S(2)}) collective-permute-start(bf16[1024,128]{1,0:T(8,128)(2,1)S(1)} %get-tuple-element.54), channel_id=1, source_target_pairs={{0,4},{2,6},{8,12},{10,14},{16,20},{18,22},{24,28},{26,30},{1,5},{... | collective-permute-start | bytes 786440 | tf_op jit(solution)/shard_map/ppermute | solution.py:321
  91.0 30.8 %collective-permute-start.5 = (bf16[1024,128]{1,0:T(8,128)(2,1)S(1)}, bf16[1024,128]{1,0:T(8,128)(2,1)S(1)}, u32[]{:S(2)}, u32[]{:S(2)}) collective-permute-start(bf16[1024,128]{1,0:T(8,128)(2,1)S(1)} %get-tuple-element.55), channel_id=1, source_target_pairs={{0,6},{2,4},{8,14},{10,12},{16,22},{18,20},{24,30},{26,28},{1,7},{... | collective-permute-start | bytes 786440 | tf_op jit(solution)/shard_map/ppermute | solution.py:321
  92.3 29.5 %collective-permute-start.6 = (bf16[1024,128]{1,0:T(8,128)(2,1)S(1)}, bf16[1024,128]{1,0:T(8,128)(2,1)S(1)}, u32[]{:S(2)}, u32[]{:S(2)}) collective-permute-start(bf16[1024,128]{1,0:T(8,128)(2,1)S(1)} %get-tuple-element.56), channel_id=1, source_target_pairs={{0,14},{2,12},{4,10},{6,8},{16,30},{18,28},{20,26},{22,24},{1,15},... | collective-permute-start | bytes 786440 | tf_op jit(solution)/shard_map/ppermute | solution.py:321
  93.7 28.6 %collective-permute-start.20 = (bf16[4096,128]{1,0:T(8,128)(2,1)S(1)}, bf16[4096,128]{1,0:T(8,128)(2,1)S(1)}, u32[]{:S(2)}, u32[]{:S(2)}) collective-permute-start(bf16[4096,128]{1,0:T(8,128)(2,1)S(1)} %get-tuple-element.83), channel_id=1, source_target_pairs={{0,1},{1,0},{2,3},{3,2},{4,5},{5,4},{6,7},{7,6},{8,9},{9,8},{10,11... | collective-permute-start | bytes 3145736 | tf_op jit(solution)/shard_map/ppermute | solution.py:336
  101.7 33.1 %collective-permute-start.2 = (bf16[1024,128]{1,0:T(8,128)(2,1)S(1)}, bf16[1024,128]{1,0:T(8,128)(2,1)S(1)}, u32[]{:S(2)}, u32[]{:S(2)}) collective-permute-start(bf16[1024,128]{1,0:T(8,128)(2,1)S(1)} %get-tuple-element.52), channel_id=1, source_target_pairs={{0,30},{2,28},{4,26},{6,24},{8,22},{10,20},{12,18},{14,16},{1,31},... | collective-permute-start | bytes 786440 | tf_op jit(solution)/shard_map/ppermute | solution.py:321
  121.8 6.3 %collective-permute-start.19 = (bf16[4096,128]{1,0:T(8,128)(2,1)S(1)}, bf16[4096,128]{1,0:T(8,128)(2,1)S(1)}, u32[]{:S(2)}, u32[]{:S(2)}) collective-permute-start(bf16[4096,128]{1,0:T(8,128)(2,1)S(1)} %get-tuple-element.82), channel_id=1, source_target_pairs={{0,1},{1,0},{2,3},{3,2},{4,5},{5,4},{6,7},{7,6},{8,9},{9,8},{10,11... | collective-permute-start | bytes 3145736 | tf_op jit(solution)/shard_map/ppermute | solution.py:336
  134.8 8.8 %collective-permute-start.21 = (bf16[1024,128]{1,0:T(8,128)(2,1)S(1)}, bf16[1024,128]{1,0:T(8,128)(2,1)S(1)}, u32[]{:S(2)}, u32[]{:S(2)}) collective-permute-start(bf16[1024,128]{1,0:T(8,128)(2,1)S(1)} %get-tuple-element.91), channel_id=1, source_target_pairs={{0,1},{1,0},{2,3},{3,2},{4,5},{5,4},{6,7},{7,6},{8,9},{9,8},{10,11... | collective-permute-start | bytes 786440 | tf_op jit(solution)/shard_map/ppermute | solution.py:336

commit v3 on v2

--- a/solution.py
+++ b/solution.py
@@ -20,6 +20,10 @@
 ROWS = GROUP * BLK
 SCALE = math.log2(math.e) / math.sqrt(HD)
 TILE = 128
+SPAN = 256
+ALL_TILES = [
+    (j, r, lo, lo + SPAN, False, False) for lo in range(0, BLK, SPAN) for j in range(GROUP) for r in range(BLK // TILE)
+]
 VMEM = pltpu.VMEM
 ANY = pl.ANY
 
@@ -35,10 +39,10 @@
     level = [(a, a) for a in range(slow)]
     if (fast, slow) == (4, 4):
         two, one, zero = [(0, 2), (1, 3)], [(0, 3), (1, 2)], [(0, 1), (2, 3)]
-        order = []
-        for m in range(3):
-            order += [permute(two, m), permute(one, m), permute(zero, m)]
-        order += [permute(level, 1), permute(two, 3), permute(level, 2), permute(level, 3), permute(zero, 3)]
+        order = [permute(two, 0), permute(one, 0), permute(level, 1)]
+        order += [permute(two, 1), permute(one, 1), permute(zero, 0)]
+        order += [permute(two, 2), permute(one, 2), permute(zero, 1), permute(level, 2)]
+        order += [permute(two, 3), permute(zero, 2), permute(level, 3), permute(zero, 3)]
         order += [permute(one, 3)]
         edges = [0, 3, 6, 10, 14, 15]
     else:
@@ -63,35 +67,39 @@
     return jnp.dot(vt, weights.astype(jnp.bfloat16), preferred_element_type=jnp.float32)
 
 
-def cut_kernel(count, meta, key, value, okey, ovalue, *rest):
+def cut_copies(act, own, first, meta, key, value, okey, ovalue, outs, sems):
+    for j, to in enumerate(outs):
+        code = meta[1 + first + j] - 1
+        block, head = code // KVH, code % KVH
+        col = pl.ds(pl.multiple_of(jnp.maximum(head, 0) * HD, HD), HD)
+        flag = jnp.logical_and(code >= 0, (block == meta[0]) if own else (block != meta[0]))
+        for t, source in enumerate((key, value) if own else (okey, ovalue)):
+            copy = pltpu.make_async_copy(source.at[:, col], to.at[pl.ds(t * BLK, BLK), :], sems.at[j, t])
+            pl.when(flag)(copy.start if act == "start" else copy.wait)
+
+
+def cut_kernel(meta, key, value, okey, ovalue, *rest):
     outs, sems = rest[:-1], rest[-1]
-    side = meta[0]
-
-    def each(act):
-        for j in range(count):
-            code = meta[1 + j] - 1
-            block, head = code // KVH, code % KVH
-            col = pl.multiple_of(jnp.maximum(head, 0) * HD, HD)
-            for t, (here, there) in enumerate(((key, okey), (value, ovalue))):
-                to = outs[j].at[pl.ds(t * BLK, BLK), :]
-                mine = pltpu.make_async_copy(here.at[:, pl.ds(col, HD)], to, sems.at[j, t])
-                other = pltpu.make_async_copy(there.at[:, pl.ds(col, HD)], to, sems.at[j, t])
-                act(jnp.logical_and(code >= 0, block == side), mine)
-                act(jnp.logical_and(code >= 0, block != side), other)
-
-    def start(flag, copy):
-        pl.when(flag)(copy.start)
-
-    def wait(flag, copy):
-        pl.when(flag)(copy.wait)
-
-    each(start)
-    each(wait)
-
-
-def own_kernel(local_at, work, meta, q, k, v, ok, ov, acc_out, stat_out, out, vt, outs, later, sems):
-    low = lax.broadcasted_iota(jnp.int32, (TILE, TILE), 1) >= lax.broadcasted_iota(jnp.int32, (TILE, TILE), 0)
+    args = (0, meta, key, value, okey, ovalue, outs, sems)
+    for act in ("start", "wait"):
+        for own in (False, True):
+            cut_copies(act, own, *args)
+
+
+def own_kernel(local_at, work, first, meta, q, k, v, ok, ov, acc_out, stat_out, out, *rest):
+    sent, (vt, outs, later, sems, cut_sems) = rest[:-5], rest[-5:]
+    args = (first, meta, k, v, ok, ov, sent, cut_sems)
+    for own in (False, True):
+        cut_copies("start", own, *args)
     count_heads(meta, later, work)
+    for g in range(KVH):
+        later[g] = later[g] + meta[local_at + g]
+    tiles = []
+    for lo in range(0, BLK, SPAN):
+        for j in range(GROUP):
+            for r in range(lo // TILE, BLK // TILE):
+                hi = min(lo + SPAN, (r + 1) * TILE)
+                tiles.append((j, r, lo, hi, hi == (r + 1) * TILE, lo == 0))
 
     def finish(g):
         return pltpu.make_async_copy(outs.at[g], out.at[:, wide(g)], sems.at[g])
@@ -99,22 +107,7 @@
     def head(g, carry):
         cols = pl.ds(pl.multiple_of(g * HD, HD), HD)
         vt[...] = v[:, cols].T
-        for r in reversed(range(BLK // TILE)):
-            keys, at = (r + 1) * TILE, slice(r * TILE, (r + 1) * TILE)
-            for j in range(GROUP):
-                scores = scores_of(k[:keys, cols], q[at, part(g, j)])
-                last = jnp.where(low, scores[r * TILE :], -1e30)
-                scores = jnp.concatenate([scores[: r * TILE], last], axis=0) if r else last
-                m = jnp.max(scores, axis=0, keepdims=True)
-                weights = jnp.exp2((scores - m) * SCALE)
-                stat_out[g, j : j + 1, at] = m
-                stat_out[g, GROUP + j : GROUP + j + 1, at] = jnp.sum(weights, axis=0, keepdims=True)
-                acc_out[g, j, :, at] = total_of(vt[:, :keys], weights)
-
-        @pl.when(meta[local_at + g] > 0)
-        def _():
-            vt[...] = ov[:, cols].T
-            fold(g, q, ok.at[:, cols], vt, acc_out, stat_out, acc_out, stat_out)
+        fold(tiles, g, q, k.at[:, cols], vt, acc_out, stat_out)
 
         @pl.when(later[g] == 0)
         def _():
@@ -126,6 +119,46 @@
     lax.fori_loop(0, KVH, head, 0)
     for g in range(KVH):
         pl.when(later[g] == 0)(finish(g).wait)
+    for own in (False, True):
+        cut_copies("wait", own, *args)
+
+
+def near_kernel(local_at, work, first, meta, q, k, v, ok, ov, acc, stat, _, acc_out, stat_out, out, *rest):
+    sent, (vt, outs, later, sems, cut_sems) = rest[:-5], rest[-5:]
+    args = (first, meta, k, v, ok, ov, sent, cut_sems)
+    for own in (False, True):
+        cut_copies("start", own, *args)
+    count_heads(meta, later, work)
+
+    def finish(g):
+        return pltpu.make_async_copy(outs.at[g], out.at[:, wide(g)], sems.at[g])
+
+    def head(g, carry):
+        local = meta[local_at + g] > 0
+
+        @pl.when(jnp.logical_or(local, later[g] > 0))
+        def _():
+            acc_out[g] = acc[g]
+            stat_out[g] = stat[g]
+
+        @pl.when(local)
+        def _():
+            cols = pl.ds(pl.multiple_of(g * HD, HD), HD)
+            vt[...] = ov[:, cols].T
+            fold(ALL_TILES, g, q, ok.at[:, cols], vt, acc_out, stat_out)
+
+            @pl.when(later[g] == 0)
+            def _():
+                write_out(g, acc_out, stat_out, outs)
+                finish(g).start()
+
+        return carry
+
+    lax.fori_loop(0, KVH, head, 0)
+    for g in range(KVH):
+        pl.when(jnp.logical_and(meta[local_at + g] > 0, later[g] == 0))(finish(g).wait)
+    for own in (False, True):
+        cut_copies("wait", own, *args)
 
 
 def wide(g):
@@ -159,19 +192,51 @@
         outs[g, :, j * HD : (j + 1) * HD] = (acc[g, j] / total).astype(jnp.bfloat16).T
 
 
-def fold(g, q, k, vt, acc, stat, acc_out, stat_out):
-    for j in range(GROUP):
-        for r in range(BLK // TILE):
-            at, total = slice(r * TILE, (r + 1) * TILE), GROUP + j
-            scores = scores_of(k[...], q[at, part(g, j)])
-            m_old = stat[g, j : j + 1, at]
-            m = jnp.maximum(m_old, jnp.max(scores, axis=0, keepdims=True))
-            weights = jnp.exp2((scores - m) * SCALE)
-            alpha = jnp.exp2((m_old - m) * SCALE)
-            sums = stat[g, total : total + 1, at] * alpha + jnp.sum(weights, axis=0, keepdims=True)
-            stat_out[g, j : j + 1, at] = m
-            stat_out[g, total : total + 1, at] = sums
-            acc_out[g, j, :, at] = acc[g, j, :, at] * alpha + total_of(vt[...], weights)
+def fold(tiles, g, q, k, vt, acc, stat):
+    low = lax.broadcasted_iota(jnp.int32, (TILE, TILE), 1) >= lax.broadcasted_iota(jnp.int32, (TILE, TILE), 0)
+    peaks, sums, scores, weights = {}, {}, {}, {}
+    fresh = {t[:2] for t in tiles if t[5]}
+    for j, r in {t[:2]: None for t in tiles if t[:2] not in fresh}:
+        at = slice(r * TILE, (r + 1) * TILE)
+        peaks[j, r], sums[j, r] = stat[g, j : j + 1, at], stat[g, GROUP + j : GROUP + j + 1, at]
+
+    def score(j, r, lo, hi, diagonal, first):
+        s = scores_of(k[lo:hi, :], q[r * TILE : (r + 1) * TILE, part(g, j)])
+        if diagonal:
+            last = jnp.where(low, s[hi - lo - TILE :], -1e30)
+            s = jnp.concatenate([s[: hi - lo - TILE], last], axis=0) if hi - lo > TILE else last
+        return s
+
+    def weigh(s, j, r, lo, hi, diagonal, first):
+        m = jnp.max(s, axis=0, keepdims=True)
+        m = m if first else jnp.maximum(peaks[j, r], m)
+        w = jnp.exp2((s - m) * SCALE)
+        total = jnp.sum(w, axis=0, keepdims=True)
+        alpha = None
+        if not first:
+            alpha = jnp.exp2((peaks[j, r] - m) * SCALE)
+            total = total + sums[j, r] * alpha
+        peaks[j, r], sums[j, r] = m, total
+        return w, alpha
+
+    def gather(pair, j, r, lo, hi, diagonal, first):
+        w, alpha = pair
+        at = slice(r * TILE, (r + 1) * TILE)
+        new = total_of(vt[:, lo:hi], w)
+        acc[g, j, :, at] = new if first else acc[g, j, :, at] * alpha + new
+
+    count = len(tiles)
+    for t in range(count + 3):
+        if t < count:
+            scores[t] = score(*tiles[t])
+        if 0 <= t - 2 < count:
+            weights[t - 2] = weigh(scores.pop(t - 2), *tiles[t - 2])
+        if 0 <= t - 3:
+            gather(weights.pop(t - 3), *tiles[t - 3])
+    for (j, r), m in peaks.items():
+        at = slice(r * TILE, (r + 1) * TILE)
+        stat[g, j : j + 1, at] = m
+        stat[g, GROUP + j : GROUP + j + 1, at] = sums[j, r]
 
 
 def far_kernel(n_here, n_swap, here_at, here_later, swap_at, swap_later, meta, *refs):
@@ -210,7 +275,7 @@
 
             pltpu.make_async_copy(kv.at[i], kv.at[i], kv_sem.at[i]).wait()
             vt[...] = kv[i, BLK:, :].T
-            fold(g, q, kv.at[i, pl.ds(0, BLK), :], vt, acc_out, stat_out, acc_out, stat_out)
+            fold(ALL_TILES, g, q, kv.at[i, pl.ds(0, BLK), :], vt, acc_out, stat_out)
             seen[g] = seen[g] + 1
 
             @pl.when(jnp.logical_and(seen[g] == here[g], later[g] == 0))
@@ -274,43 +339,51 @@
     )
     params = pltpu.CompilerParams(vmem_limit_bytes=16 << 20)
 
+    firsts = [0, groups[0][1], groups[1][1], total]
+    counts = [b - a for a, b in zip(firsts[:-1], firsts[1:])]
     sent = pl.pallas_call(
-        functools.partial(cut_kernel, total),
+        cut_kernel,
         grid_spec=pltpu.PrefetchScalarGridSpec(
             num_scalar_prefetch=1,
             grid=(),
             in_specs=[vmem_spec] * 4,
-            out_specs=[any_spec] * total,
-            scratch_shapes=[pltpu.SemaphoreType.DMA((total, 2))],
+            out_specs=[any_spec] * counts[0],
+            scratch_shapes=[pltpu.SemaphoreType.DMA((counts[0], 2))],
         ),
-        out_shape=[piece_shape] * total,
+        out_shape=[piece_shape] * counts[0],
         compiler_params=params,
-        cost_estimate=pl.CostEstimate(flops=0, bytes_accessed=total << 19, transcendentals=0),
+        cost_estimate=pl.CostEstimate(flops=0, bytes_accessed=1 << 10, transcendentals=0),
         name="cut",
     )(meta, key, value, okey, ovalue)
 
-    piece_flops = 4 * ROWS * BLK * HD
-    acc, stat, out = pl.pallas_call(
-        functools.partial(own_kernel, local_at, (here_at, end)),
-        grid_spec=pltpu.PrefetchScalarGridSpec(
-            num_scalar_prefetch=1,
-            grid=(),
-            in_specs=[vmem_spec] * 5,
-            out_specs=[vmem_spec, vmem_spec, any_spec],
-            scratch_shapes=[
-                VMEM((HD, BLK), jnp.bfloat16),
-                VMEM((KVH, BLK, WIDE), jnp.bfloat16),
-                pltpu.SMEM((KVH,), jnp.int32),
-                pltpu.SemaphoreType.DMA((KVH,)),
-            ],
-        ),
-        out_shape=state,
-        compiler_params=params,
-        cost_estimate=pl.CostEstimate(
-            flops=32 * piece_flops, bytes_accessed=28 << 20, transcendentals=12 * ROWS * BLK
-        ),
-        name="own",
-    )(meta, queries, key, value, okey, ovalue)
+    def inner(kernel, name, first, count, *through):
+        return pl.pallas_call(
+            functools.partial(kernel, local_at, (here_at, end), first),
+            grid_spec=pltpu.PrefetchScalarGridSpec(
+                num_scalar_prefetch=1,
+                grid=(),
+                in_specs=[vmem_spec] * 5 + [vmem_spec, vmem_spec, any_spec][: len(through)],
+                out_specs=[vmem_spec, vmem_spec] + [any_spec] * (1 + count),
+                scratch_shapes=[
+                    VMEM((HD, BLK), jnp.bfloat16),
+                    VMEM((KVH, BLK, WIDE), jnp.bfloat16),
+                    pltpu.SMEM((KVH,), jnp.int32),
+                    pltpu.SemaphoreType.DMA((KVH,)),
+                    pltpu.SemaphoreType.DMA((count, 2)),
+                ],
+            ),
+            out_shape=(*state, *[piece_shape] * count),
+            input_output_aliases={6 + i: i for i in range(len(through))},
+            compiler_params=params,
+            cost_estimate=pl.CostEstimate(
+                flops=0, bytes_accessed=1 << 10, transcendentals=0
+            ),
+            name=name,
+        )(meta, queries, key, value, okey, ovalue, *through)
+
+    acc, stat, out, *second = inner(own_kernel, "own", firsts[1], counts[1])
+    acc, stat, out, *third = inner(near_kernel, "near", firsts[2], counts[2], acc, stat, out)
+    sent = [*sent, *second, *third]
 
     landed = [None] * total
     swapped = []
@@ -330,7 +403,7 @@
             out_shape=(jax.ShapeDtypeStruct((count * 2 * BLK, HD), jnp.bfloat16), state[1]),
             input_output_aliases={count: 1},
             compiler_params=params,
-            cost_estimate=pl.CostEstimate(flops=0, bytes_accessed=count << 19, transcendentals=0),
+            cost_estimate=pl.CostEstimate(flops=0, bytes_accessed=1 << 10, transcendentals=0),
             name="pack",
         )(*landed[a:b], stat)
         swapped.append(lax.ppermute(joined, "head", swap))
@@ -370,7 +443,7 @@
             input_output_aliases={base + 1 + i: i for i in range(3)},
             compiler_params=params,
             cost_estimate=pl.CostEstimate(
-                flops=8 * pieces * piece_flops, bytes_accessed=pieces << 21, transcendentals=pieces * ROWS * BLK
+                flops=32 * pieces * ROWS * BLK * HD, bytes_accessed=pieces << 21, transcendentals=pieces * ROWS * BLK
             ),
             name="far",
         )(meta, *landed[a:b], *others, queries, acc, stat, out)

time: 146 us -> 137 us (0.938)
  waiting for transfers between devices: 38.9 us -> 17.2 us
  starting transfers between devices: 29.5 us -> 50.2 us
  Pallas kernels: 73.5 us -> 65.2 us
    ppermute x15, waiting for transfers between devices: 37.6 us -> 15.9 us  [send(): landed[j] = lax.ppermute(sent[j], 'ctx', order[j])]
    ppermute x5, starting transfers between devices: 7.33 us -> 28.4 us  [pack(): swapped.append(lax.ppermute(joined, 'head', swap))]
    pallas_call x7, Pallas kernels: 40.9 us -> 32.5 us  [far(): pl.pallas_call(functools.partial(far_kernel, n_here, len(others), here_at...]
    pallas_call x2 -> x3, Pallas kernels: 32.3 us -> 32.3 us  [the longest x2 31.5 us: inner(): pl.pallas_call(functools.partial(kernel, local_at, (here_at, end), first)...]
  transfers between devices with their start and end apart: 22 -> 22, of which waited for: 6 -> 4; matrix products, arithmetic and copies ran while one was open for 2% -> 2% of each run, Pallas kernels for 46% -> 44%
where the time goes in v3:
time: 137 us; the launch traced here: 138 us
  Pallas kernels  65.2 us (48%)
  starting transfers between devices  50.2 us (37%)
  waiting for transfers between devices  17.2 us (13%)
  local copies, waits for them, and re-layouts  4.21 us (3%)
    pallas_call x7, Pallas kernels, far(): pl.pallas_call(functools.partial(far_kernel, n_here, len(others), here_at...  32.5 us
    pallas_call x2, Pallas kernels, inner(): pl.pallas_call(functools.partial(kernel, local_at, (here_at, end), first)...  31.5 us
    ppermute x5, starting transfers between devices, pack(): swapped.append(lax.ppermute(joined, 'head', swap))  28.4 us
    ppermute x15, starting transfers between devices, send(): landed[j] = lax.ppermute(sent[j], 'ctx', order[j])  21.1 us
    ppermute x15, waiting for transfers between devices, send(): landed[j] = lax.ppermute(sent[j], 'ctx', order[j])  15.9 us
  transfers between devices with their start and end apart: 22, of which 4 were waited for; matrix products, arithmetic and copies ran while one was open for 2% of the time, Pallas kernels for 44%

profile of v3, /device:TPU:29, one launch (start us, length us, event | category | flops | bytes accessed | tf_op | source)
XLA Modules:
  0.0 138.3 jit_solution(8035604577927389610)
XLA Ops:
  0.0 0.7 collective-permute-start
  0.7 0.0 collective-permute-start.1
  0.7 0.7 slice.12
  1.4 0.3 compare_reduce_fusion
  1.7 0.1 copy.39
  1.8 0.1 select_reduce_fusion.1
  1.9 0.1 reduce_max.44
  2.0 0.1 reduce_max.45
  2.1 0.7 constant_dynamic-slice_fusion
  2.8 0.1 slice_bitcast_fusion
  2.9 0.2 select_reduce_fusion
  3.1 0.1 compare_reduce_fusion.1
  3.2 0.1 select_reduce_fusion.2
  3.3 0.1 concatenate.3.meta
  3.4 0.0 collective-permute-done.ok.okey
  3.4 1.3 collective-permute-done.1.ov.ovalue
  4.7 1.2 copy-done.1
  5.9 1.2 copy-done.2
  7.1 0.8 cut.1
  8.0 1.3 collective-permute-start.14
  9.3 1.3 collective-permute-start.15
  10.6 3.1 %collective-permute-start.16 = (bf16[1024,128]{1,0:T(8,128)(2,1)S(1)}, bf16[1024,128]{1,0:T(8,128)(2,1)S(1)}, u32[]{:S(2)}, u32[]{:S(2)}) collective-permute-start(bf16[1024,128]{1,0:T(8,128)(2,1)S(1)} %get-tuple-element.72), channel_id=1, source_target_pairs={{0,2},{4,6},{8,10},{12,14},{16,18},{20,22},{24,26},{28,30},{1,3},{... | collective-permute-start | bytes 786440 | tf_op jit(solution)/shard_map/ppermute | solution.py:394
  13.6 14.4 %own.1 = (f32[8,4,128,512]{3,2,1,0:T(8,128)S(1)}, f32[8,8,512]{2,1,0:T(8,128)S(1)}, bf16[512,4096]{1,0:T(8,128)(2,1)}, bf16[1024,128]{1,0:T(8,128)(2,1)S(1)}, bf...) custom-call(s32[54]{0:T(128)S(1)} %concatenate.3.meta, bf16[512,4096]{1,0:T(8,128)(2,1)S(1)} %copy-done, ...), custom_call_target="tpu_custom_call" | custom-call | bytes 1024 | tf_op jit(solution)/shard_map/own/pallas_call | solution.py:360
  28.0 1.3 collective-permute-start.11
  29.3 1.3 collective-permute-start.12
  30.6 17.1 %near.1 = (f32[8,4,128,512]{3,2,1,0:T(8,128)S(1)}, f32[8,8,512]{2,1,0:T(8,128)S(1)}, bf16[512,4096]{1,0:T(8,128)(2,1)}, bf16[1024,128]{1,0:T(8,128)(2,1)S(1)}, b...) custom-call(s32[54]{0:T(128)S(1)} %concatenate.3.meta, ...), custom_call_target="tpu_custom_call", output_to_operand_aliasing={{0}: (6, {}), {1}: (7, {}), {2}: (8, {})} | custom-call | bytes 1024 | tf_op jit(solution)/shard_map/near/pallas_call | solution.py:360
  47.8 0.0 collective-permute-done.14.refs_0_
  47.8 1.3 collective-permute-start.13
  49.1 0.0 collective-permute-done.15.refs_1_
  49.1 1.3 collective-permute-start.10
  50.4 0.1 pack.5
  50.5 0.1 collective-permute-start.18
  50.6 2.2 %far.7 = (f32[8,4,128,512]{3,2,1,0:T(8,128)S(1)}, f32[8,8,512]{2,1,0:T(8,128)S(1)}, bf16[512,4096]{1,0:T(8,128)(2,1)}) custom-call(s32[54]{0:T(128)S(1)} %concatenate.3.meta, bf16[1024,128]{1,0:T(8,128)(2,1)S(1)} %collective-permute-done.14.refs_0_, ...), custom_call_target="tpu_custom_call", output_to_operand_aliasing={{0}: (5, {}), {1}: (6, {}), {2}: (7, {})} | custom-call | flops 12884901888 | bytes 6291456 | tf_op jit(solution)/shard_map/far/pallas_call | solution.py:421
  52.8 0.7 collective-permute-done.11.refs_0_
  53.5 1.3 collective-permute-start.7
  54.8 0.0 collective-permute-done.12.refs_1_
  54.8 1.3 collective-permute-start.8
  56.1 1.3 collective-permute-start.9
  57.4 0.1 pack.6
  57.5 4.1 %collective-permute-start.17 = (bf16[3072,128]{1,0:T(8,128)(2,1)S(1)}, bf16[3072,128]{1,0:T(8,128)(2,1)S(1)}, u32[]{:S(2)}, u32[]{:S(2)}) collective-permute-start(bf16[3072,128]{1,0:T(8,128)(2,1)S(1)} %get-tuple-element.78), channel_id=1, source_target_pairs={{0,1},{1,0},{2,3},{3,2},{4,5},{5,4},{6,7},{7,6},{8,9},{9,8},{10,11... | collective-permute-start | bytes 2359304 | tf_op jit(solution)/shard_map/ppermute | solution.py:409
  61.6 2.4 %far.8 = (f32[8,4,128,512]{3,2,1,0:T(8,128)S(1)}, f32[8,8,512]{2,1,0:T(8,128)S(1)}, bf16[512,4096]{1,0:T(8,128)(2,1)}) custom-call(s32[54]{0:T(128)S(1)} %concatenate.3.meta, bf16[1024,128]{1,0:T(8,128)(2,1)S(1)} %collective-permute-done.11.refs_0_, ...), custom_call_target="tpu_custom_call", output_to_operand_aliasing={{0}: (6, {}), {1}: (7, {}), {2}: (8, {})} | custom-call | flops 25769803776 | bytes 12582912 | tf_op jit(solution)/shard_map/far/pallas_call | solution.py:421
  64.0 0.0 collective-permute-done.10.refs_3_
  64.0 1.3 collective-permute-start.3
  65.3 10.0 %collective-permute-done.7.refs_0_ = bf16[1024,128]{1,0:T(8,128)(2,1)S(1)} collective-permute-done((bf16[1024,128]{1,0:T(8,128)(2,1)S(1)}, bf16[1024,128]{1,0:T(8,128)(2,1)S(1)}, u32[]{:S(2)}, u32[]{:S(2)}) %collective-permute-start.7) | collective-permute-done | bytes 262176 | tf_op jit(solution)/shard_map/ppermute | solution.py:394
  75.3 1.3 collective-permute-start.4
  76.6 0.0 collective-permute-done.8.refs_1_
  76.6 1.3 collective-permute-start.5
  77.9 0.0 collective-permute-done.9.refs_2_
  78.0 1.3 collective-permute-start.6
  79.3 0.1 pack.7
  79.4 9.5 %collective-permute-start.20 = (bf16[4096,128]{1,0:T(8,128)(2,1)S(1)}, bf16[4096,128]{1,0:T(8,128)(2,1)S(1)}, u32[]{:S(2)}, u32[]{:S(2)}) collective-permute-start(bf16[4096,128]{1,0:T(8,128)(2,1)S(1)} %get-tuple-element.89), channel_id=1, source_target_pairs={{0,1},{1,0},{2,3},{3,2},{4,5},{5,4},{6,7},{7,6},{8,9},{9,8},{10,11... | collective-permute-start | bytes 3145736 | tf_op jit(solution)/shard_map/ppermute | solution.py:409
  88.9 7.4 %far.9 = (f32[8,4,128,512]{3,2,1,0:T(8,128)S(1)}, f32[8,8,512]{2,1,0:T(8,128)S(1)}, bf16[512,4096]{1,0:T(8,128)(2,1)}) custom-call(s32[54]{0:T(128)S(1)} %concatenate.3.meta, bf16[1024,128]{1,0:T(8,128)(2,1)S(1)} %collective-permute-done.7.refs_0_, ...), custom_call_target="tpu_custom_call", output_to_operand_aliasing={{0}: (7, {}), {1}: (8, {}), {2}: (9, {})} | custom-call | flops 30064771072 | bytes 14680064 | tf_op jit(solution)/shard_map/far/pallas_call | solution.py:421
  96.3 1.3 collective-permute-start.2
  97.6 0.0 collective-permute-done.4.refs_1_
  97.6 0.0 collective-permute-done.5.refs_2_
  97.6 5.1 %collective-permute-done.6.refs_3_ = bf16[1024,128]{1,0:T(8,128)(2,1)S(1)} collective-permute-done((bf16[1024,128]{1,0:T(8,128)(2,1)S(1)}, bf16[1024,128]{1,0:T(8,128)(2,1)S(1)}, u32[]{:S(2)}, u32[]{:S(2)}) %collective-permute-start.6) | collective-permute-done | bytes 262176 | tf_op jit(solution)/shard_map/ppermute | solution.py:394
  102.6 0.1 pack.8
  102.7 9.4 %collective-permute-start.19 = (bf16[4096,128]{1,0:T(8,128)(2,1)S(1)}, bf16[4096,128]{1,0:T(8,128)(2,1)S(1)}, u32[]{:S(2)}, u32[]{:S(2)}) collective-permute-start(bf16[4096,128]{1,0:T(8,128)(2,1)S(1)} %get-tuple-element.88), channel_id=1, source_target_pairs={{0,1},{1,0},{2,3},{3,2},{4,5},{5,4},{6,7},{7,6},{8,9},{9,8},{10,11... | collective-permute-start | bytes 3145736 | tf_op jit(solution)/shard_map/ppermute | solution.py:409
  112.1 12.0 %far.10 = (f32[8,4,128,512]{3,2,1,0:T(8,128)S(1)}, f32[8,8,512]{2,1,0:T(8,128)S(1)}, bf16[512,4096]{1,0:T(8,128)(2,1)}) custom-call(s32[54]{0:T(128)S(1)} %concatenate.3.meta, bf16[1024,128]{1,0:T(8,128)(2,1)S(1)} %collective-permute-done.3.refs_0_, ...), custom_call_target="tpu_custom_call", output_to_operand_aliasing={{0}: (7, {}), {1}: (8, {}), {2}: (9, {})} | custom-call | flops 34359738368 | bytes 16777216 | tf_op jit(solution)/shard_map/far/pallas_call | solution.py:421
  124.1 1.4 %far.11 = (f32[8,4,128,512]{3,2,1,0:T(8,128)S(1)}, f32[8,8,512]{2,1,0:T(8,128)S(1)}, bf16[512,4096]{1,0:T(8,128)(2,1)}) custom-call(s32[54]{0:T(128)S(1)} %concatenate.3.meta, bf16[4096,128]{1,0:T(8,128)(2,1)S(1)} %collective-permute-done.19.refs_0_, bf16[512,4096]{1,0:T(8,128)(2,1)S(1)} %copy-done, ...), custom_call_target="tpu_custom_call", output_to_operand_aliasing={{0}: (3, {}), {1}: (4, {}), {2}: (5, {})} | custom-call | flops 17179869184 | bytes 8388608 | tf_op jit(solution)/shard_map/far/pallas_call | solution.py:421
  125.5 0.0 collective-permute-done.2.refs_0_
  125.6 5.4 %collective-permute-start.21 = (bf16[1024,128]{1,0:T(8,128)(2,1)S(1)}, bf16[1024,128]{1,0:T(8,128)(2,1)S(1)}, u32[]{:S(2)}, u32[]{:S(2)}) collective-permute-start(bf16[1024,128]{1,0:T(8,128)(2,1)S(1)} %get-tuple-element.97), channel_id=1, source_target_pairs={{0,1},{1,0},{2,3},{3,2},{4,5},{5,4},{6,7},{7,6},{8,9},{9,8},{10,11... | collective-permute-start | bytes 786440 | tf_op jit(solution)/shard_map/ppermute | solution.py:409
  131.0 3.6 %far.12 = (f32[8,4,128,512]{3,2,1,0:T(8,128)S(1)}, f32[8,8,512]{2,1,0:T(8,128)S(1)}, bf16[512,4096]{1,0:T(8,128)(2,1)}) custom-call(s32[54]{0:T(128)S(1)} %concatenate.3.meta, bf16[1024,128]{1,0:T(8,128)(2,1)S(1)} %collective-permute-done.2.refs_0_, bf16[512,4096]{1,0:T(8,128)(2,1)S(1)} %copy-done, ...), custom_call_target="tpu_custom_call", output_to_operand_aliasing={{0}: (3, {}), {1}: (4, {}), {2}: (5, {})} | custom-call | flops 4294967296 | bytes 2097152 | tf_op jit(solution)/shard_map/far/pallas_call | solution.py:421
  134.6 3.5 %far.13 = (f32[8,4,128,512]{3,2,1,0:T(8,128)S(1)}, f32[8,8,512]{2,1,0:T(8,128)S(1)}, bf16[512,4096]{1,0:T(8,128)(2,1)}) custom-call(s32[54]{0:T(128)S(1)} %concatenate.3.meta, bf16[1024,128]{1,0:T(8,128)(2,1)S(1)} %collective-permute-done.21.refs_0_, bf16[512,4096]{1,0:T(8,128)(2,1)S(1)} %copy-done, ...), custom_call_target="tpu_custom_call", output_to_operand_aliasing={{0}: (3, {}), {1}: (4, {}), {2}: (5, {})} | custom-call | flops 4294967296 | bytes 2097152 | tf_op jit(solution)/shard_map/far/pallas_call | solution.py:421
  (16 shorter events, 0.1 us)
Async XLA Ops:
  0.0 3.4 %collective-permute-start = (bf16[512,1024]{1,0:T(8,128)(2,1)}, bf16[512,1024]{1,0:T(8,128)(2,1)S(1)}, u32[]{:S(2)}, u32[]{:S(2)}) collective-permute-start(bf16[512,1024]{1,0:T(8,128)(2,1)} %key.1), channel_id=1, source_target_pairs={{0,1},{1,0},{2,3},{3,2},{4,5},{5,4},{6,7},{7,6},{8,9},{9,8},{10,11... | collective-permute-start | bytes 3145736 | tf_op jit(solution)/shard_map/ppermute | solution.py:306
  0.7 4.0 %collective-permute-start.1 = (bf16[512,1024]{1,0:T(8,128)(2,1)}, bf16[512,1024]{1,0:T(8,128)(2,1)S(1)}, u32[]{:S(2)}, u32[]{:S(2)}) collective-permute-start(bf16[512,1024]{1,0:T(8,128)(2,1)} %value.1), channel_id=1, source_target_pairs={{0,1},{1,0},{2,3},{3,2},{4,5},{5,4},{6,7},{7,6},{8,9},{9,8},{10,11... | collective-permute-start | bytes 3145736 | tf_op jit(solution)/shard_map/ppermute | solution.py:306
  3.4 10.3 %copy-start = (bf16[512,4096]{1,0:T(8,128)(2,1)S(1)}, bf16[512,4096]{1,0:T(8,128)(2,1)}, u32[]{:S(2)}) copy-start(bf16[512,4096]{1,0:T(8,128)(2,1)} %refs_1_.5) | copy-start | bytes 12582916
  4.7 1.2 copy-start.1
  5.9 1.2 copy-start.2
  8.0 39.8 %collective-permute-start.14 = (bf16[1024,128]{1,0:T(8,128)(2,1)S(1)}, bf16[1024,128]{1,0:T(8,128)(2,1)S(1)}, u32[]{:S(2)}, u32[]{:S(2)}) collective-permute-start(bf16[1024,128]{1,0:T(8,128)(2,1)S(1)} %get-tuple-element.70), channel_id=1, source_target_pairs={{0,16},{2,18},{4,20},{6,22},{8,24},{10,26},{12,28},{14,30},{1,17},... | collective-permute-start | bytes 786440 | tf_op jit(solution)/shard_map/ppermute | solution.py:394
  9.3 39.8 %collective-permute-start.15 = (bf16[1024,128]{1,0:T(8,128)(2,1)S(1)}, bf16[1024,128]{1,0:T(8,128)(2,1)S(1)}, u32[]{:S(2)}, u32[]{:S(2)}) collective-permute-start(bf16[1024,128]{1,0:T(8,128)(2,1)S(1)} %get-tuple-element.71), channel_id=1, source_target_pairs={{0,24},{2,26},{4,28},{6,30},{8,16},{10,18},{12,20},{14,22},{1,25},... | collective-permute-start | bytes 786440 | tf_op jit(solution)/shard_map/ppermute | solution.py:394
  10.6 39.8 %collective-permute-start.16 = (bf16[1024,128]{1,0:T(8,128)(2,1)S(1)}, bf16[1024,128]{1,0:T(8,128)(2,1)S(1)}, u32[]{:S(2)}, u32[]{:S(2)}) collective-permute-start(bf16[1024,128]{1,0:T(8,128)(2,1)S(1)} %get-tuple-element.72), channel_id=1, source_target_pairs={{0,2},{4,6},{8,10},{12,14},{16,18},{20,22},{24,26},{28,30},{1,3},{... | collective-permute-start | bytes 786440 | tf_op jit(solution)/shard_map/ppermute | solution.py:394
  28.0 25.5 %collective-permute-start.11 = (bf16[1024,128]{1,0:T(8,128)(2,1)S(1)}, bf16[1024,128]{1,0:T(8,128)(2,1)S(1)}, u32[]{:S(2)}, u32[]{:S(2)}) collective-permute-start(bf16[1024,128]{1,0:T(8,128)(2,1)S(1)} %get-tuple-element.67), channel_id=1, source_target_pairs={{0,18},{2,16},{4,22},{6,20},{8,26},{10,24},{12,30},{14,28},{1,19},... | collective-permute-start | bytes 786440 | tf_op jit(solution)/shard_map/ppermute | solution.py:394
  29.3 25.5 %collective-permute-start.12 = (bf16[1024,128]{1,0:T(8,128)(2,1)S(1)}, bf16[1024,128]{1,0:T(8,128)(2,1)S(1)}, u32[]{:S(2)}, u32[]{:S(2)}) collective-permute-start(bf16[1024,128]{1,0:T(8,128)(2,1)S(1)} %get-tuple-element.68), channel_id=1, source_target_pairs={{0,26},{2,24},{4,30},{6,28},{8,18},{10,16},{12,22},{14,20},{1,27},... | collective-permute-start | bytes 786440 | tf_op jit(solution)/shard_map/ppermute | solution.py:394
  47.8 8.3 %collective-permute-start.13 = (bf16[1024,128]{1,0:T(8,128)(2,1)S(1)}, bf16[1024,128]{1,0:T(8,128)(2,1)S(1)}, u32[]{:S(2)}, u32[]{:S(2)}) collective-permute-start(bf16[1024,128]{1,0:T(8,128)(2,1)S(1)} %get-tuple-element.69), channel_id=1, source_target_pairs={{0,8},{2,10},{4,12},{6,14},{16,24},{18,26},{20,28},{22,30},{1,9},{... | collective-permute-start | bytes 786440 | tf_op jit(solution)/shard_map/ppermute | solution.py:394
  49.1 14.9 %collective-permute-start.10 = (bf16[1024,128]{1,0:T(8,128)(2,1)S(1)}, bf16[1024,128]{1,0:T(8,128)(2,1)S(1)}, u32[]{:S(2)}, u32[]{:S(2)}) collective-permute-start(bf16[1024,128]{1,0:T(8,128)(2,1)S(1)} %get-tuple-element.66), channel_id=1, source_target_pairs={{0,4},{2,6},{8,12},{10,14},{16,20},{18,22},{24,28},{26,30},{1,5},{... | collective-permute-start | bytes 786440 | tf_op jit(solution)/shard_map/ppermute | solution.py:394
  50.5 7.0 %collective-permute-start.18 = (bf16[3072,128]{1,0:T(8,128)(2,1)S(1)}, bf16[3072,128]{1,0:T(8,128)(2,1)S(1)}, u32[]{:S(2)}, u32[]{:S(2)}) collective-permute-start(bf16[3072,128]{1,0:T(8,128)(2,1)S(1)} %get-tuple-element.79), channel_id=1, source_target_pairs={{0,1},{1,0},{2,3},{3,2},{4,5},{5,4},{6,7},{7,6},{8,9},{9,8},{10,11... | collective-permute-start | bytes 2359304 | tf_op jit(solution)/shard_map/ppermute | solution.py:409
  53.5 21.9 %collective-permute-start.7 = (bf16[1024,128]{1,0:T(8,128)(2,1)S(1)}, bf16[1024,128]{1,0:T(8,128)(2,1)S(1)}, u32[]{:S(2)}, u32[]{:S(2)}) collective-permute-start(bf16[1024,128]{1,0:T(8,128)(2,1)S(1)} %get-tuple-element.63), channel_id=1, source_target_pairs={{0,20},{2,22},{4,16},{6,18},{8,28},{10,30},{12,24},{14,26},{1,21},... | collective-permute-start | bytes 786440 | tf_op jit(solution)/shard_map/ppermute | solution.py:394
  54.8 21.8 %collective-permute-start.8 = (bf16[1024,128]{1,0:T(8,128)(2,1)S(1)}, bf16[1024,128]{1,0:T(8,128)(2,1)S(1)}, u32[]{:S(2)}, u32[]{:S(2)}) collective-permute-start(bf16[1024,128]{1,0:T(8,128)(2,1)S(1)} %get-tuple-element.64), channel_id=1, source_target_pairs={{0,28},{2,30},{4,24},{6,26},{8,20},{10,22},{12,16},{14,18},{1,29},... | collective-permute-start | bytes 786440 | tf_op jit(solution)/shard_map/ppermute | solution.py:394
  56.1 21.8 %collective-permute-start.9 = (bf16[1024,128]{1,0:T(8,128)(2,1)S(1)}, bf16[1024,128]{1,0:T(8,128)(2,1)S(1)}, u32[]{:S(2)}, u32[]{:S(2)}) collective-permute-start(bf16[1024,128]{1,0:T(8,128)(2,1)S(1)} %get-tuple-element.65), channel_id=1, source_target_pairs={{0,10},{2,8},{4,14},{6,12},{16,26},{18,24},{20,30},{22,28},{1,11},... | collective-permute-start | bytes 786440 | tf_op jit(solution)/shard_map/ppermute | solution.py:394
  57.5 21.9 %collective-permute-start.17 = (bf16[3072,128]{1,0:T(8,128)(2,1)S(1)}, bf16[3072,128]{1,0:T(8,128)(2,1)S(1)}, u32[]{:S(2)}, u32[]{:S(2)}) collective-permute-start(bf16[3072,128]{1,0:T(8,128)(2,1)S(1)} %get-tuple-element.78), channel_id=1, source_target_pairs={{0,1},{1,0},{2,3},{3,2},{4,5},{5,4},{6,7},{7,6},{8,9},{9,8},{10,11... | collective-permute-start | bytes 2359304 | tf_op jit(solution)/shard_map/ppermute | solution.py:409
  64.0 32.2 %collective-permute-start.3 = (bf16[1024,128]{1,0:T(8,128)(2,1)S(1)}, bf16[1024,128]{1,0:T(8,128)(2,1)S(1)}, u32[]{:S(2)}, u32[]{:S(2)}) collective-permute-start(bf16[1024,128]{1,0:T(8,128)(2,1)S(1)} %get-tuple-element.59), channel_id=1, source_target_pairs={{0,22},{2,20},{4,18},{6,16},{8,30},{10,28},{12,26},{14,24},{1,23},... | collective-permute-start | bytes 786440 | tf_op jit(solution)/shard_map/ppermute | solution.py:394
  75.3 22.2 %collective-permute-start.4 = (bf16[1024,128]{1,0:T(8,128)(2,1)S(1)}, bf16[1024,128]{1,0:T(8,128)(2,1)S(1)}, u32[]{:S(2)}, u32[]{:S(2)}) collective-permute-start(bf16[1024,128]{1,0:T(8,128)(2,1)S(1)} %get-tuple-element.60), channel_id=1, source_target_pairs={{0,12},{2,14},{4,8},{6,10},{16,28},{18,30},{20,24},{22,26},{1,13},... | collective-permute-start | bytes 786440 | tf_op jit(solution)/shard_map/ppermute | solution.py:394
  76.6 20.9 %collective-permute-start.5 = (bf16[1024,128]{1,0:T(8,128)(2,1)S(1)}, bf16[1024,128]{1,0:T(8,128)(2,1)S(1)}, u32[]{:S(2)}, u32[]{:S(2)}) collective-permute-start(bf16[1024,128]{1,0:T(8,128)(2,1)S(1)} %get-tuple-element.61), channel_id=1, source_target_pairs={{0,6},{2,4},{8,14},{10,12},{16,22},{18,20},{24,30},{26,28},{1,7},{... | collective-permute-start | bytes 786440 | tf_op jit(solution)/shard_map/ppermute | solution.py:394
  78.0 24.7 %collective-permute-start.6 = (bf16[1024,128]{1,0:T(8,128)(2,1)S(1)}, bf16[1024,128]{1,0:T(8,128)(2,1)S(1)}, u32[]{:S(2)}, u32[]{:S(2)}) collective-permute-start(bf16[1024,128]{1,0:T(8,128)(2,1)S(1)} %get-tuple-element.62), channel_id=1, source_target_pairs={{0,14},{2,12},{4,10},{6,8},{16,30},{18,28},{20,26},{22,24},{1,15},... | collective-permute-start | bytes 786440 | tf_op jit(solution)/shard_map/ppermute | solution.py:394
  79.4 32.8 %collective-permute-start.20 = (bf16[4096,128]{1,0:T(8,128)(2,1)S(1)}, bf16[4096,128]{1,0:T(8,128)(2,1)S(1)}, u32[]{:S(2)}, u32[]{:S(2)}) collective-permute-start(bf16[4096,128]{1,0:T(8,128)(2,1)S(1)} %get-tuple-element.89), channel_id=1, source_target_pairs={{0,1},{1,0},{2,3},{3,2},{4,5},{5,4},{6,7},{7,6},{8,9},{9,8},{10,11... | collective-permute-start | bytes 3145736 | tf_op jit(solution)/shard_map/ppermute | solution.py:409
  96.3 29.3 %collective-permute-start.2 = (bf16[1024,128]{1,0:T(8,128)(2,1)S(1)}, bf16[1024,128]{1,0:T(8,128)(2,1)S(1)}, u32[]{:S(2)}, u32[]{:S(2)}) collective-permute-start(bf16[1024,128]{1,0:T(8,128)(2,1)S(1)} %get-tuple-element.58), channel_id=1, source_target_pairs={{0,30},{2,28},{4,26},{6,24},{8,22},{10,20},{12,18},{14,16},{1,31},... | collective-permute-start | bytes 786440 | tf_op jit(solution)/shard_map/ppermute | solution.py:394
  102.7 21.4 %collective-permute-start.19 = (bf16[4096,128]{1,0:T(8,128)(2,1)S(1)}, bf16[4096,128]{1,0:T(8,128)(2,1)S(1)}, u32[]{:S(2)}, u32[]{:S(2)}) collective-permute-start(bf16[4096,128]{1,0:T(8,128)(2,1)S(1)} %get-tuple-element.88), channel_id=1, source_target_pairs={{0,1},{1,0},{2,3},{3,2},{4,5},{5,4},{6,7},{7,6},{8,9},{9,8},{10,11... | collective-permute-start | bytes 3145736 | tf_op jit(solution)/shard_map/ppermute | solution.py:409
  125.6 9.0 %collective-permute-start.21 = (bf16[1024,128]{1,0:T(8,128)(2,1)S(1)}, bf16[1024,128]{1,0:T(8,128)(2,1)S(1)}, u32[]{:S(2)}, u32[]{:S(2)}) collective-permute-start(bf16[1024,128]{1,0:T(8,128)(2,1)S(1)} %get-tuple-element.97), channel_id=1, source_target_pairs={{0,1},{1,0},{2,3},{3,2},{4,5},{5,4},{6,7},{7,6},{8,9},{9,8},{10,11... | collective-permute-start | bytes 786440 | tf_op jit(solution)/shard_map/ppermute | solution.py:409

commit v4 on v3

--- a/solution.py
+++ b/solution.py
@@ -39,12 +39,12 @@
     level = [(a, a) for a in range(slow)]
     if (fast, slow) == (4, 4):
         two, one, zero = [(0, 2), (1, 3)], [(0, 3), (1, 2)], [(0, 1), (2, 3)]
-        order = [permute(two, 0), permute(one, 0), permute(level, 1)]
-        order += [permute(two, 1), permute(one, 1), permute(zero, 0)]
-        order += [permute(two, 2), permute(one, 2), permute(zero, 1), permute(level, 2)]
-        order += [permute(two, 3), permute(zero, 2), permute(level, 3), permute(zero, 3)]
+        order = [permute(two, 0), permute(level, 1), permute(level, 2), permute(level, 3)]
+        order += [permute(one, 0), permute(two, 1), permute(one, 1)]
+        order += [permute(two, 2), permute(one, 2), permute(zero, 0), permute(zero, 1)]
+        order += [permute(two, 3), permute(zero, 2), permute(zero, 3)]
         order += [permute(one, 3)]
-        edges = [0, 3, 6, 10, 14, 15]
+        edges = [0, 4, 7, 11, 14, 15]
     else:
         order = []
         for m in range(fast):
@@ -78,9 +78,12 @@
             pl.when(flag)(copy.start if act == "start" else copy.wait)
 
 
-def cut_kernel(meta, key, value, okey, ovalue, *rest):
-    outs, sems = rest[:-1], rest[-1]
-    args = (0, meta, key, value, okey, ovalue, outs, sems)
+def cut_kernel(first, count, meta, key, value, okey, ovalue, *rest):
+    *through, sems = rest
+    outs = through[len(through) - count :]
+    args = (first, meta, key, value, okey, ovalue, outs, sems)
+    if len(through) > count:
+        through[1][...] = through[0][...]
     for act in ("start", "wait"):
         for own in (False, True):
             cut_copies(act, own, *args)
@@ -339,22 +342,26 @@
     )
     params = pltpu.CompilerParams(vmem_limit_bytes=16 << 20)
 
-    firsts = [0, groups[0][1], groups[1][1], total]
+    firsts = [0, groups[1][1], groups[2][1], groups[3][1]]
     counts = [b - a for a, b in zip(firsts[:-1], firsts[1:])]
-    sent = pl.pallas_call(
-        cut_kernel,
-        grid_spec=pltpu.PrefetchScalarGridSpec(
-            num_scalar_prefetch=1,
-            grid=(),
-            in_specs=[vmem_spec] * 4,
-            out_specs=[any_spec] * counts[0],
-            scratch_shapes=[pltpu.SemaphoreType.DMA((counts[0], 2))],
-        ),
-        out_shape=[piece_shape] * counts[0],
-        compiler_params=params,
-        cost_estimate=pl.CostEstimate(flops=0, bytes_accessed=1 << 10, transcendentals=0),
-        name="cut",
-    )(meta, key, value, okey, ovalue)
+    def cut(first, count, *through):
+        return pl.pallas_call(
+            functools.partial(cut_kernel, first, count),
+            grid_spec=pltpu.PrefetchScalarGridSpec(
+                num_scalar_prefetch=1,
+                grid=(),
+                in_specs=[vmem_spec] * (4 + len(through)),
+                out_specs=[vmem_spec] * len(through) + [any_spec] * count,
+                scratch_shapes=[pltpu.SemaphoreType.DMA((count, 2))],
+            ),
+            out_shape=[*[state[1]] * len(through), *[piece_shape] * count],
+            input_output_aliases={5 + i: i for i in range(len(through))},
+            compiler_params=params,
+            cost_estimate=pl.CostEstimate(flops=0, bytes_accessed=1 << 10, transcendentals=0),
+            name="cut",
+        )(meta, key, value, okey, ovalue, *through)
+
+    sent = cut(0, counts[0])
 
     def inner(kernel, name, first, count, *through):
         return pl.pallas_call(
@@ -382,8 +389,7 @@
         )(meta, queries, key, value, okey, ovalue, *through)
 
     acc, stat, out, *second = inner(own_kernel, "own", firsts[1], counts[1])
-    acc, stat, out, *third = inner(near_kernel, "near", firsts[2], counts[2], acc, stat, out)
-    sent = [*sent, *second, *third]
+    sent = [*sent, *second]
 
     landed = [None] * total
     swapped = []
@@ -448,12 +454,22 @@
             name="far",
         )(meta, *landed[a:b], *others, queries, acc, stat, out)
 
-    for n in range(len(groups)):
+    for n in range(3):
         send(n)
+    stat = pack(0, stat)
+    acc, stat, out, *third = inner(near_kernel, "near", firsts[2], counts[2], acc, stat, out)
+    sent += third
+    send(3)
     last = len(groups) - 1
-    for n in range(last):
+    acc, stat, out = far(0, None, acc, stat, out)
+    for n in range(1, last):
         stat = pack(n, stat)
-        acc, stat, out = far(n, n - 1 if n else None, acc, stat, out)
+        if n == last - 2:
+            a, b = groups[last]
+            stat, *final = cut(a, b - a, stat)
+            sent += final
+            send(last)
+        acc, stat, out = far(n, n - 1, acc, stat, out)
     acc, stat, out = far(None, last - 1, acc, stat, out)
     stat = pack(last, stat)
     acc, stat, out = far(last, None, acc, stat, out)

time: 137 us -> 135 us (0.985)
  the two profiles are of different devices: /device:TPU:29 before, /device:TPU:28 now
where the time goes in v4:
time: 135 us; the launch traced here: 136 us
  Pallas kernels  62.5 us (46%)
  waiting for transfers between devices  39.1 us (29%)
  starting transfers between devices  28.1 us (21%)
  local copies, waits for them, and re-layouts  4.3 us (3%)
    pallas_call x7, Pallas kernels, far(): pl.pallas_call(functools.partial(far_kernel, n_here, len(others), here_at...  43.6 us
    ppermute x15, waiting for transfers between devices, send(): landed[j] = lax.ppermute(sent[j], 'ctx', order[j])  37.9 us
    ppermute x15, starting transfers between devices, send(): landed[j] = lax.ppermute(sent[j], 'ctx', order[j])  21.5 us
    pallas_call x2, Pallas kernels, inner(): pl.pallas_call(functools.partial(kernel, local_at, (here_at, end), first)...  16.8 us
    ppermute x5, starting transfers between devices, pack(): swapped.append(lax.ppermute(joined, 'head', swap))  6.07 us
  transfers between devices with their start and end apart: 22, of which 5 were waited for; matrix products, arithmetic and copies ran while one was open for 2% of the time, Pallas kernels for 43%

profile of v4, /device:TPU:28, one launch (start us, length us, event | category | flops | bytes accessed | tf_op | source)
XLA Modules:
  0.0 135.6 jit_solution(11557194542121077435)
XLA Ops:
  0.0 0.0 collective-permute-start
  0.0 0.5 collective-permute-start.1
  0.5 0.7 slice.12
  1.2 0.3 compare_reduce_fusion
  1.6 0.1 copy.40
  1.7 0.1 select_reduce_fusion.1
  1.8 0.1 reduce_max.44
  1.8 0.1 reduce_max.45
  2.0 0.7 constant_dynamic-slice_fusion
  2.7 0.1 slice_bitcast_fusion
  2.8 0.2 select_reduce_fusion
  2.9 0.1 compare_reduce_fusion.1
  3.0 0.1 select_reduce_fusion.2
  3.1 0.1 concatenate.3.meta
  3.2 0.0 collective-permute-done.ok.okey
  3.2 1.2 collective-permute-done.1.ov.ovalue
  4.4 1.3 copy-done.1
  5.7 1.2 copy-done.3
  6.9 1.1 cut.2
  8.0 1.3 collective-permute-start.9
  9.3 3.3 %collective-permute-start.10 = (bf16[1024,128]{1,0:T(8,128)(2,1)S(1)}, bf16[1024,128]{1,0:T(8,128)(2,1)S(1)}, u32[]{:S(2)}, u32[]{:S(2)}) collective-permute-start(bf16[1024,128]{1,0:T(8,128)(2,1)S(1)} %get-tuple-element.64), channel_id=1, source_target_pairs={{0,2},{4,6},{8,10},{12,14},{16,18},{20,22},{24,26},{28,30},{1,3},{... | collective-permute-start | bytes 786440 | tf_op jit(solution)/shard_map/ppermute | solution.py:400
  12.7 1.3 collective-permute-start.11
  14.0 1.3 collective-permute-start.12
  15.3 0.0 copy-start.2
  15.3 0.0 copy-start.4
  15.3 1.4 %collective-permute-start.6 = (bf16[1024,128]{1,0:T(8,128)(2,1)S(1)}, bf16[1024,128]{1,0:T(8,128)(2,1)S(1)}, u32[]{:S(2)}, u32[]{:S(2)}) collective-permute-start(bf16[1024,128]{1,0:T(8,128)(2,1)S(1)} %get-tuple-element.60), channel_id=1, source_target_pairs={{0,24},{2,26},{4,28},{6,30},{8,16},{10,18},{12,20},{14,22},{1,25},... | collective-permute-start | bytes 786440 | tf_op jit(solution)/shard_map/ppermute | solution.py:400
  16.8 14.4 %own.1 = (f32[8,4,128,512]{3,2,1,0:T(8,128)S(1)}, f32[8,8,512]{2,1,0:T(8,128)S(1)}, bf16[512,4096]{1,0:T(8,128)(2,1)}, bf16[1024,128]{1,0:T(8,128)(2,1)S(1)}, bf...) custom-call(s32[54]{0:T(128)S(1)} %concatenate.3.meta, ...), custom_call_target="tpu_custom_call" | custom-call | bytes 1024 | tf_op jit(solution)/shard_map/own/pallas_call | solution.py:367
  31.2 0.0 collective-permute-done.9.refs_0_
  31.2 1.3 collective-permute-start.7
  32.5 0.0 collective-permute-done.10.refs_1_
  32.5 1.3 collective-permute-start.8
  33.8 1.3 collective-permute-start.2
  35.1 0.0 collective-permute-done.12.refs_3_
  35.1 0.1 pack.5
  35.2 0.1 collective-permute-start.13
  35.3 2.4 %near.1 = (f32[8,4,128,512]{3,2,1,0:T(8,128)S(1)}, f32[8,8,512]{2,1,0:T(8,128)S(1)}, bf16[512,4096]{1,0:T(8,128)(2,1)}, bf16[1024,128]{1,0:T(8,128)(2,1)S(1)}, b...) custom-call(s32[54]{0:T(128)S(1)} %concatenate.3.meta, ...), custom_call_target="tpu_custom_call", output_to_operand_aliasing={{0}: (6, {}), {1}: (7, {}), {2}: (8, {})} | custom-call | bytes 1024 | tf_op jit(solution)/shard_map/near/pallas_call | solution.py:367
  37.7 5.5 %far.7 = (f32[8,4,128,512]{3,2,1,0:T(8,128)S(1)}, f32[8,8,512]{2,1,0:T(8,128)S(1)}, bf16[512,4096]{1,0:T(8,128)(2,1)}) custom-call(s32[54]{0:T(128)S(1)} %concatenate.3.meta, bf16[1024,128]{1,0:T(8,128)(2,1)S(1)} %collective-permute-done.9.refs_0_, ...), custom_call_target="tpu_custom_call", output_to_operand_aliasing={{0}: (6, {}), {1}: (7, {}), {2}: (8, {})} | custom-call | flops 17179869184 | bytes 8388608 | tf_op jit(solution)/shard_map/far/pallas_call | solution.py:427
  43.3 0.0 collective-permute-done.6.refs_0_
  43.3 1.3 collective-permute-start.3
  44.6 18.1 %collective-permute-done.7.refs_1_ = bf16[1024,128]{1,0:T(8,128)(2,1)S(1)} collective-permute-done((bf16[1024,128]{1,0:T(8,128)(2,1)S(1)}, bf16[1024,128]{1,0:T(8,128)(2,1)S(1)}, u32[]{:S(2)}, u32[]{:S(2)}) %collective-permute-start.7) | collective-permute-done | bytes 262176 | tf_op jit(solution)/shard_map/ppermute | solution.py:400
  62.7 1.3 collective-permute-start.4
  64.0 0.0 collective-permute-done.8.refs_2_
  64.0 1.3 collective-permute-start.5
  65.3 0.1 pack.6
  65.4 0.1 collective-permute-start.18
  65.4 10.9 %far.8 = (f32[8,4,128,512]{3,2,1,0:T(8,128)S(1)}, f32[8,8,512]{2,1,0:T(8,128)S(1)}, bf16[512,4096]{1,0:T(8,128)(2,1)}) custom-call(s32[54]{0:T(128)S(1)} %concatenate.3.meta, bf16[1024,128]{1,0:T(8,128)(2,1)S(1)} %collective-permute-done.6.refs_0_, ...), custom_call_target="tpu_custom_call", output_to_operand_aliasing={{0}: (6, {}), {1}: (7, {}), {2}: (8, {})} | custom-call | flops 30064771072 | bytes 14680064 | tf_op jit(solution)/shard_map/far/pallas_call | solution.py:427
  76.4 2.5 %collective-permute-done.2.refs_0_ = bf16[1024,128]{1,0:T(8,128)(2,1)S(1)} collective-permute-done((bf16[1024,128]{1,0:T(8,128)(2,1)S(1)}, bf16[1024,128]{1,0:T(8,128)(2,1)S(1)}, u32[]{:S(2)}, u32[]{:S(2)}) %collective-permute-start.2) | collective-permute-done | bytes 262176 | tf_op jit(solution)/shard_map/ppermute | solution.py:400
  78.9 1.3 collective-permute-start.15
  80.2 1.3 collective-permute-start.16
  81.5 1.3 collective-permute-start.17
  82.8 9.1 %collective-permute-done.5.refs_3_ = bf16[1024,128]{1,0:T(8,128)(2,1)S(1)} collective-permute-done((bf16[1024,128]{1,0:T(8,128)(2,1)S(1)}, bf16[1024,128]{1,0:T(8,128)(2,1)S(1)}, u32[]{:S(2)}, u32[]{:S(2)}) %collective-permute-start.5) | collective-permute-done | bytes 262176 | tf_op jit(solution)/shard_map/ppermute | solution.py:400
  91.9 0.1 pack.7
  92.0 0.6 cut.3
  92.6 1.3 collective-permute-start.14
  93.9 0.1 collective-permute-start.20
  94.0 9.8 %far.9 = (f32[8,4,128,512]{3,2,1,0:T(8,128)S(1)}, f32[8,8,512]{2,1,0:T(8,128)S(1)}, bf16[512,4096]{1,0:T(8,128)(2,1)}) custom-call(s32[54]{0:T(128)S(1)} %concatenate.3.meta, bf16[1024,128]{1,0:T(8,128)(2,1)S(1)} %collective-permute-done.2.refs_0_, ...), custom_call_target="tpu_custom_call", output_to_operand_aliasing={{0}: (7, {}), {1}: (8, {}), {2}: (9, {})} | custom-call | flops 30064771072 | bytes 14680064 | tf_op jit(solution)/shard_map/far/pallas_call | solution.py:427
  103.9 8.2 %collective-permute-done.17.refs_2_ = bf16[1024,128]{1,0:T(8,128)(2,1)S(1)} collective-permute-done((bf16[1024,128]{1,0:T(8,128)(2,1)S(1)}, bf16[1024,128]{1,0:T(8,128)(2,1)S(1)}, u32[]{:S(2)}, u32[]{:S(2)}) %collective-permute-start.17) | collective-permute-done | bytes 262176 | tf_op jit(solution)/shard_map/ppermute | solution.py:400
  112.0 0.1 pack.8
  112.1 0.1 collective-permute-start.19
  112.2 6.1 %far.10 = (f32[8,4,128,512]{3,2,1,0:T(8,128)S(1)}, f32[8,8,512]{2,1,0:T(8,128)S(1)}, bf16[512,4096]{1,0:T(8,128)(2,1)}) custom-call(s32[54]{0:T(128)S(1)} %concatenate.3.meta, bf16[1024,128]{1,0:T(8,128)(2,1)S(1)} %collective-permute-done.15.refs_0_, ...), custom_call_target="tpu_custom_call", output_to_operand_aliasing={{0}: (6, {}), {1}: (7, {}), {2}: (8, {})} | custom-call | flops 30064771072 | bytes 14680064 | tf_op jit(solution)/shard_map/far/pallas_call | solution.py:427
  118.4 4.1 %far.11 = (f32[8,4,128,512]{3,2,1,0:T(8,128)S(1)}, f32[8,8,512]{2,1,0:T(8,128)S(1)}, bf16[512,4096]{1,0:T(8,128)(2,1)}) custom-call(s32[54]{0:T(128)S(1)} %concatenate.3.meta, bf16[3072,128]{1,0:T(8,128)(2,1)S(1)} %collective-permute-done.19.refs_0_, bf16[512,4096]{1,0:T(8,128)(2,1)S(1)} %copy-done, ...), custom_call_target="tpu_custom_call", output_to_operand_aliasing={{0}: (3, {}), {1}: (4, {}), {2}: (5, {})} | custom-call | flops 12884901888 | bytes 6291456 | tf_op jit(solution)/shard_map/far/pallas_call | solution.py:427
  122.5 5.8 %collective-permute-start.21 = (bf16[1024,128]{1,0:T(8,128)(2,1)S(1)}, bf16[1024,128]{1,0:T(8,128)(2,1)S(1)}, u32[]{:S(2)}, u32[]{:S(2)}) collective-permute-start(bf16[1024,128]{1,0:T(8,128)(2,1)S(1)} %get-tuple-element.99), channel_id=1, source_target_pairs={{0,1},{1,0},{2,3},{3,2},{4,5},{5,4},{6,7},{7,6},{8,9},{9,8},{10,11... | collective-permute-start | bytes 786440 | tf_op jit(solution)/shard_map/ppermute | solution.py:415
  128.3 3.6 %far.12 = (f32[8,4,128,512]{3,2,1,0:T(8,128)S(1)}, f32[8,8,512]{2,1,0:T(8,128)S(1)}, bf16[512,4096]{1,0:T(8,128)(2,1)}) custom-call(s32[54]{0:T(128)S(1)} %concatenate.3.meta, bf16[1024,128]{1,0:T(8,128)(2,1)S(1)} %collective-permute-done.14.refs_0_, bf16[512,4096]{1,0:T(8,128)(2,1)S(1)} %copy-done, ...), custom_call_target="tpu_custom_call", output_to_operand_aliasing={{0}: (3, {}), {1}: (4, {}), {2}: (5, {})} | custom-call | flops 4294967296 | bytes 2097152 | tf_op jit(solution)/shard_map/far/pallas_call | solution.py:427
  131.9 3.5 %far.13 = (f32[8,4,128,512]{3,2,1,0:T(8,128)S(1)}, f32[8,8,512]{2,1,0:T(8,128)S(1)}, bf16[512,4096]{1,0:T(8,128)(2,1)}) custom-call(s32[54]{0:T(128)S(1)} %concatenate.3.meta, bf16[1024,128]{1,0:T(8,128)(2,1)S(1)} %collective-permute-done.21.refs_0_, bf16[512,4096]{1,0:T(8,128)(2,1)S(1)} %copy-done, ...), custom_call_target="tpu_custom_call", output_to_operand_aliasing={{0}: (3, {}), {1}: (4, {}), {2}: (5, {})} | custom-call | flops 4294967296 | bytes 2097152 | tf_op jit(solution)/shard_map/far/pallas_call | solution.py:427
  (21 shorter events, 0.1 us)
Async XLA Ops:
  0.0 3.2 %collective-permute-start = (bf16[512,1024]{1,0:T(8,128)(2,1)}, bf16[512,1024]{1,0:T(8,128)(2,1)S(1)}, u32[]{:S(2)}, u32[]{:S(2)}) collective-permute-start(bf16[512,1024]{1,0:T(8,128)(2,1)} %key.3), channel_id=1, source_target_pairs={{0,1},{1,0},{2,3},{3,2},{4,5},{5,4},{6,7},{7,6},{8,9},{9,8},{10,11... | collective-permute-start | bytes 3145736 | tf_op jit(solution)/shard_map/ppermute | solution.py:309
  0.0 4.4 %collective-permute-start.1 = (bf16[512,1024]{1,0:T(8,128)(2,1)}, bf16[512,1024]{1,0:T(8,128)(2,1)S(1)}, u32[]{:S(2)}, u32[]{:S(2)}) collective-permute-start(bf16[512,1024]{1,0:T(8,128)(2,1)} %value.3), channel_id=1, source_target_pairs={{0,1},{1,0},{2,3},{3,2},{4,5},{5,4},{6,7},{7,6},{8,9},{9,8},{10,11... | collective-permute-start | bytes 3145736 | tf_op jit(solution)/shard_map/ppermute | solution.py:309
  3.2 13.6 %copy-start = (bf16[512,4096]{1,0:T(8,128)(2,1)S(1)}, bf16[512,4096]{1,0:T(8,128)(2,1)}, u32[]{:S(2)}) copy-start(bf16[512,4096]{1,0:T(8,128)(2,1)} %refs_1_.5) | copy-start | bytes 12582916
  4.4 1.3 copy-start.1
  5.7 1.2 copy-start.3
  8.0 23.2 %collective-permute-start.9 = (bf16[1024,128]{1,0:T(8,128)(2,1)S(1)}, bf16[1024,128]{1,0:T(8,128)(2,1)S(1)}, u32[]{:S(2)}, u32[]{:S(2)}) collective-permute-start(bf16[1024,128]{1,0:T(8,128)(2,1)S(1)} %get-tuple-element.63), channel_id=1, source_target_pairs={{0,16},{2,18},{4,20},{6,22},{8,24},{10,26},{12,28},{14,30},{1,17},... | collective-permute-start | bytes 786440 | tf_op jit(solution)/shard_map/ppermute | solution.py:400
  9.3 23.2 %collective-permute-start.10 = (bf16[1024,128]{1,0:T(8,128)(2,1)S(1)}, bf16[1024,128]{1,0:T(8,128)(2,1)S(1)}, u32[]{:S(2)}, u32[]{:S(2)}) collective-permute-start(bf16[1024,128]{1,0:T(8,128)(2,1)S(1)} %get-tuple-element.64), channel_id=1, source_target_pairs={{0,2},{4,6},{8,10},{12,14},{16,18},{20,22},{24,26},{28,30},{1,3},{... | collective-permute-start | bytes 786440 | tf_op jit(solution)/shard_map/ppermute | solution.py:400
  12.7 21.1 %collective-permute-start.11 = (bf16[1024,128]{1,0:T(8,128)(2,1)S(1)}, bf16[1024,128]{1,0:T(8,128)(2,1)S(1)}, u32[]{:S(2)}, u32[]{:S(2)}) collective-permute-start(bf16[1024,128]{1,0:T(8,128)(2,1)S(1)} %get-tuple-element.65), channel_id=1, source_target_pairs={{0,4},{2,6},{8,12},{10,14},{16,20},{18,22},{24,28},{26,30},{1,5},{... | collective-permute-start | bytes 786440 | tf_op jit(solution)/shard_map/ppermute | solution.py:400
  14.0 21.1 %collective-permute-start.12 = (bf16[1024,128]{1,0:T(8,128)(2,1)S(1)}, bf16[1024,128]{1,0:T(8,128)(2,1)S(1)}, u32[]{:S(2)}, u32[]{:S(2)}) collective-permute-start(bf16[1024,128]{1,0:T(8,128)(2,1)S(1)} %get-tuple-element.66), channel_id=1, source_target_pairs={{0,6},{2,4},{8,14},{10,12},{16,22},{18,20},{24,30},{26,28},{1,7},{... | collective-permute-start | bytes 786440 | tf_op jit(solution)/shard_map/ppermute | solution.py:400
  15.3 20.0 %copy-start.2 = (bf16[512,1024]{1,0:T(8,128)(2,1)S(1)}, bf16[512,1024]{1,0:T(8,128)(2,1)}, u32[]{:S(2)}) copy-start(bf16[512,1024]{1,0:T(8,128)(2,1)} %key.3) | copy-start | bytes 3145732
  15.3 20.0 %copy-start.4 = (bf16[512,1024]{1,0:T(8,128)(2,1)S(1)}, bf16[512,1024]{1,0:T(8,128)(2,1)}, u32[]{:S(2)}) copy-start(bf16[512,1024]{1,0:T(8,128)(2,1)} %value.3) | copy-start | bytes 3145732
  15.3 27.9 %collective-permute-start.6 = (bf16[1024,128]{1,0:T(8,128)(2,1)S(1)}, bf16[1024,128]{1,0:T(8,128)(2,1)S(1)}, u32[]{:S(2)}, u32[]{:S(2)}) collective-permute-start(bf16[1024,128]{1,0:T(8,128)(2,1)S(1)} %get-tuple-element.60), channel_id=1, source_target_pairs={{0,24},{2,26},{4,28},{6,30},{8,16},{10,18},{12,20},{14,22},{1,25},... | collective-permute-start | bytes 786440 | tf_op jit(solution)/shard_map/ppermute | solution.py:400
  31.2 31.5 %collective-permute-start.7 = (bf16[1024,128]{1,0:T(8,128)(2,1)S(1)}, bf16[1024,128]{1,0:T(8,128)(2,1)S(1)}, u32[]{:S(2)}, u32[]{:S(2)}) collective-permute-start(bf16[1024,128]{1,0:T(8,128)(2,1)S(1)} %get-tuple-element.61), channel_id=1, source_target_pairs={{0,18},{2,16},{4,22},{6,20},{8,26},{10,24},{12,30},{14,28},{1,19},... | collective-permute-start | bytes 786440 | tf_op jit(solution)/shard_map/ppermute | solution.py:400
  32.5 31.4 %collective-permute-start.8 = (bf16[1024,128]{1,0:T(8,128)(2,1)S(1)}, bf16[1024,128]{1,0:T(8,128)(2,1)S(1)}, u32[]{:S(2)}, u32[]{:S(2)}) collective-permute-start(bf16[1024,128]{1,0:T(8,128)(2,1)S(1)} %get-tuple-element.62), channel_id=1, source_target_pairs={{0,26},{2,24},{4,30},{6,28},{8,18},{10,16},{12,22},{14,20},{1,27},... | collective-permute-start | bytes 786440 | tf_op jit(solution)/shard_map/ppermute | solution.py:400
  33.8 45.1 %collective-permute-start.2 = (bf16[1024,128]{1,0:T(8,128)(2,1)S(1)}, bf16[1024,128]{1,0:T(8,128)(2,1)S(1)}, u32[]{:S(2)}, u32[]{:S(2)}) collective-permute-start(bf16[1024,128]{1,0:T(8,128)(2,1)S(1)} %get-tuple-element.56), channel_id=1, source_target_pairs={{0,20},{2,22},{4,16},{6,18},{8,28},{10,30},{12,24},{14,26},{1,21},... | collective-permute-start | bytes 786440 | tf_op jit(solution)/shard_map/ppermute | solution.py:400
  35.2 30.1 %collective-permute-start.13 = (bf16[4096,128]{1,0:T(8,128)(2,1)S(1)}, bf16[4096,128]{1,0:T(8,128)(2,1)S(1)}, u32[]{:S(2)}, u32[]{:S(2)}) collective-permute-start(bf16[4096,128]{1,0:T(8,128)(2,1)S(1)} %get-tuple-element.68), channel_id=1, source_target_pairs={{0,1},{1,0},{2,3},{3,2},{4,5},{5,4},{6,7},{7,6},{8,9},{9,8},{10,11... | collective-permute-start | bytes 3145736 | tf_op jit(solution)/shard_map/ppermute | solution.py:415
  43.3 36.9 %collective-permute-start.3 = (bf16[1024,128]{1,0:T(8,128)(2,1)S(1)}, bf16[1024,128]{1,0:T(8,128)(2,1)S(1)}, u32[]{:S(2)}, u32[]{:S(2)}) collective-permute-start(bf16[1024,128]{1,0:T(8,128)(2,1)S(1)} %get-tuple-element.57), channel_id=1, source_target_pairs={{0,28},{2,30},{4,24},{6,26},{8,20},{10,22},{12,16},{14,18},{1,29},... | collective-permute-start | bytes 786440 | tf_op jit(solution)/shard_map/ppermute | solution.py:400
  62.7 18.8 %collective-permute-start.4 = (bf16[1024,128]{1,0:T(8,128)(2,1)S(1)}, bf16[1024,128]{1,0:T(8,128)(2,1)S(1)}, u32[]{:S(2)}, u32[]{:S(2)}) collective-permute-start(bf16[1024,128]{1,0:T(8,128)(2,1)S(1)} %get-tuple-element.58), channel_id=1, source_target_pairs={{0,8},{2,10},{4,12},{6,14},{16,24},{18,26},{20,28},{22,30},{1,9},{... | collective-permute-start | bytes 786440 | tf_op jit(solution)/shard_map/ppermute | solution.py:400
  64.0 27.9 %collective-permute-start.5 = (bf16[1024,128]{1,0:T(8,128)(2,1)S(1)}, bf16[1024,128]{1,0:T(8,128)(2,1)S(1)}, u32[]{:S(2)}, u32[]{:S(2)}) collective-permute-start(bf16[1024,128]{1,0:T(8,128)(2,1)S(1)} %get-tuple-element.59), channel_id=1, source_target_pairs={{0,10},{2,8},{4,14},{6,12},{16,26},{18,24},{20,30},{22,28},{1,11},... | collective-permute-start | bytes 786440 | tf_op jit(solution)/shard_map/ppermute | solution.py:400
  65.4 28.5 %collective-permute-start.18 = (bf16[3072,128]{1,0:T(8,128)(2,1)S(1)}, bf16[3072,128]{1,0:T(8,128)(2,1)S(1)}, u32[]{:S(2)}, u32[]{:S(2)}) collective-permute-start(bf16[3072,128]{1,0:T(8,128)(2,1)S(1)} %get-tuple-element.85), channel_id=1, source_target_pairs={{0,1},{1,0},{2,3},{3,2},{4,5},{5,4},{6,7},{7,6},{8,9},{9,8},{10,11... | collective-permute-start | bytes 2359304 | tf_op jit(solution)/shard_map/ppermute | solution.py:415
  78.9 24.9 %collective-permute-start.15 = (bf16[1024,128]{1,0:T(8,128)(2,1)S(1)}, bf16[1024,128]{1,0:T(8,128)(2,1)S(1)}, u32[]{:S(2)}, u32[]{:S(2)}) collective-permute-start(bf16[1024,128]{1,0:T(8,128)(2,1)S(1)} %get-tuple-element.82), channel_id=1, source_target_pairs={{0,22},{2,20},{4,18},{6,16},{8,30},{10,28},{12,26},{14,24},{1,23},... | collective-permute-start | bytes 786440 | tf_op jit(solution)/shard_map/ppermute | solution.py:400
  80.2 23.6 %collective-permute-start.16 = (bf16[1024,128]{1,0:T(8,128)(2,1)S(1)}, bf16[1024,128]{1,0:T(8,128)(2,1)S(1)}, u32[]{:S(2)}, u32[]{:S(2)}) collective-permute-start(bf16[1024,128]{1,0:T(8,128)(2,1)S(1)} %get-tuple-element.83), channel_id=1, source_target_pairs={{0,12},{2,14},{4,8},{6,10},{16,28},{18,30},{20,24},{22,26},{1,13},... | collective-permute-start | bytes 786440 | tf_op jit(solution)/shard_map/ppermute | solution.py:400
  81.5 30.5 %collective-permute-start.17 = (bf16[1024,128]{1,0:T(8,128)(2,1)S(1)}, bf16[1024,128]{1,0:T(8,128)(2,1)S(1)}, u32[]{:S(2)}, u32[]{:S(2)}) collective-permute-start(bf16[1024,128]{1,0:T(8,128)(2,1)S(1)} %get-tuple-element.84), channel_id=1, source_target_pairs={{0,14},{2,12},{4,10},{6,8},{16,30},{18,28},{20,26},{22,24},{1,15},... | collective-permute-start | bytes 786440 | tf_op jit(solution)/shard_map/ppermute | solution.py:400
  92.6 29.8 %collective-permute-start.14 = (bf16[1024,128]{1,0:T(8,128)(2,1)S(1)}, bf16[1024,128]{1,0:T(8,128)(2,1)S(1)}, u32[]{:S(2)}, u32[]{:S(2)}) collective-permute-start(bf16[1024,128]{1,0:T(8,128)(2,1)S(1)} %get-tuple-element.81), channel_id=1, source_target_pairs={{0,30},{2,28},{4,26},{6,24},{8,22},{10,20},{12,18},{14,16},{1,31},... | collective-permute-start | bytes 786440 | tf_op jit(solution)/shard_map/ppermute | solution.py:400
  93.9 18.3 %collective-permute-start.20 = (bf16[4096,128]{1,0:T(8,128)(2,1)S(1)}, bf16[4096,128]{1,0:T(8,128)(2,1)S(1)}, u32[]{:S(2)}, u32[]{:S(2)}) collective-permute-start(bf16[4096,128]{1,0:T(8,128)(2,1)S(1)} %get-tuple-element.91), channel_id=1, source_target_pairs={{0,1},{1,0},{2,3},{3,2},{4,5},{5,4},{6,7},{7,6},{8,9},{9,8},{10,11... | collective-permute-start | bytes 3145736 | tf_op jit(solution)/shard_map/ppermute | solution.py:415
  112.1 6.2 %collective-permute-start.19 = (bf16[3072,128]{1,0:T(8,128)(2,1)S(1)}, bf16[3072,128]{1,0:T(8,128)(2,1)S(1)}, u32[]{:S(2)}, u32[]{:S(2)}) collective-permute-start(bf16[3072,128]{1,0:T(8,128)(2,1)S(1)} %get-tuple-element.90), channel_id=1, source_target_pairs={{0,1},{1,0},{2,3},{3,2},{4,5},{5,4},{6,7},{7,6},{8,9},{9,8},{10,11... | collective-permute-start | bytes 2359304 | tf_op jit(solution)/shard_map/ppermute | solution.py:415
  122.5 9.4 %collective-permute-start.21 = (bf16[1024,128]{1,0:T(8,128)(2,1)S(1)}, bf16[1024,128]{1,0:T(8,128)(2,1)S(1)}, u32[]{:S(2)}, u32[]{:S(2)}) collective-permute-start(bf16[1024,128]{1,0:T(8,128)(2,1)S(1)} %get-tuple-element.99), channel_id=1, source_target_pairs={{0,1},{1,0},{2,3},{3,2},{4,5},{5,4},{6,7},{7,6},{8,9},{9,8},{10,11... | collective-permute-start | bytes 786440 | tf_op jit(solution)/shard_map/ppermute | solution.py:415

commit v5 on v4

--- a/solution.py
+++ b/solution.py
@@ -28,6 +28,9 @@
 ANY = pl.ANY
 
 
+PAIR_TILES = [t for t in ALL_TILES if t[0] < 2]
+
+
 def patterns(peers):
     fast = 4 if peers % 4 == 0 else 1
     slow = peers // fast
@@ -42,9 +45,9 @@
         order = [permute(two, 0), permute(level, 1), permute(level, 2), permute(level, 3)]
         order += [permute(one, 0), permute(two, 1), permute(one, 1)]
         order += [permute(two, 2), permute(one, 2), permute(zero, 0), permute(zero, 1)]
-        order += [permute(two, 3), permute(zero, 2), permute(zero, 3)]
-        order += [permute(one, 3)]
-        edges = [0, 4, 7, 11, 14, 15]
+        order += [permute(two, 3), permute(zero, 2)]
+        order += [permute(zero, 3), permute(one, 3)]
+        edges = [0, 4, 7, 11, 13, 15]
     else:
         order = []
         for m in range(fast):
@@ -99,7 +102,7 @@
         later[g] = later[g] + meta[local_at + g]
     tiles = []
     for lo in range(0, BLK, SPAN):
-        for j in range(GROUP):
+        for j in range(2):
             for r in range(lo // TILE, BLK // TILE):
                 hi = min(lo + SPAN, (r + 1) * TILE)
                 tiles.append((j, r, lo, hi, hi == (r + 1) * TILE, lo == 0))
@@ -110,7 +113,12 @@
     def head(g, carry):
         cols = pl.ds(pl.multiple_of(g * HD, HD), HD)
         vt[...] = v[:, cols].T
-        fold(tiles, g, q, k.at[:, cols], vt, acc_out, stat_out)
+
+        def pair(h, carry):
+            fold(tiles, g, q, k.at[:, cols], vt, acc_out, stat_out, 2 * h)
+            return carry
+
+        lax.fori_loop(0, GROUP // 2, pair, 0)
 
         @pl.when(later[g] == 0)
         def _():
@@ -148,7 +156,12 @@
         def _():
             cols = pl.ds(pl.multiple_of(g * HD, HD), HD)
             vt[...] = ov[:, cols].T
-            fold(ALL_TILES, g, q, ok.at[:, cols], vt, acc_out, stat_out)
+
+            def pair(h, carry):
+                fold(PAIR_TILES, g, q, ok.at[:, cols], vt, acc_out, stat_out, 2 * h)
+                return carry
+
+            lax.fori_loop(0, GROUP // 2, pair, 0)
 
             @pl.when(later[g] == 0)
             def _():
@@ -190,21 +203,24 @@
 
 
 def write_out(g, acc, stat, outs):
-    for j in range(GROUP):
-        total = stat[g, GROUP + j : GROUP + j + 1, :]
-        outs[g, :, j * HD : (j + 1) * HD] = (acc[g, j] / total).astype(jnp.bfloat16).T
-
-
-def fold(tiles, g, q, k, vt, acc, stat):
+    def head(j, carry):
+        total = stat[g, GROUP + j]
+        outs[g, :, pl.ds(pl.multiple_of(j * HD, HD), HD)] = (acc[g, j] / total).astype(jnp.bfloat16).T
+        return carry
+
+    lax.fori_loop(0, GROUP, head, 0)
+
+
+def fold(tiles, g, q, k, vt, acc, stat, base=0):
     low = lax.broadcasted_iota(jnp.int32, (TILE, TILE), 1) >= lax.broadcasted_iota(jnp.int32, (TILE, TILE), 0)
     peaks, sums, scores, weights = {}, {}, {}, {}
     fresh = {t[:2] for t in tiles if t[5]}
     for j, r in {t[:2]: None for t in tiles if t[:2] not in fresh}:
         at = slice(r * TILE, (r + 1) * TILE)
-        peaks[j, r], sums[j, r] = stat[g, j : j + 1, at], stat[g, GROUP + j : GROUP + j + 1, at]
+        peaks[j, r], sums[j, r] = stat[g, base + j, :, at], stat[g, base + GROUP + j, :, at]
 
     def score(j, r, lo, hi, diagonal, first):
-        s = scores_of(k[lo:hi, :], q[r * TILE : (r + 1) * TILE, part(g, j)])
+        s = scores_of(k[lo:hi, :], q[r * TILE : (r + 1) * TILE, part(g, base + j)])
         if diagonal:
             last = jnp.where(low, s[hi - lo - TILE :], -1e30)
             s = jnp.concatenate([s[: hi - lo - TILE], last], axis=0) if hi - lo > TILE else last
@@ -226,7 +242,7 @@
         w, alpha = pair
         at = slice(r * TILE, (r + 1) * TILE)
         new = total_of(vt[:, lo:hi], w)
-        acc[g, j, :, at] = new if first else acc[g, j, :, at] * alpha + new
+        acc[g, base + j, :, at] = new if first else acc[g, base + j, :, at] * alpha + new
 
     count = len(tiles)
     for t in range(count + 3):
@@ -238,8 +254,8 @@
             gather(weights.pop(t - 3), *tiles[t - 3])
     for (j, r), m in peaks.items():
         at = slice(r * TILE, (r + 1) * TILE)
-        stat[g, j : j + 1, at] = m
-        stat[g, GROUP + j : GROUP + j + 1, at] = sums[j, r]
+        stat[g, base + j, :, at] = m
+        stat[g, base + GROUP + j, :, at] = sums[j, r]
 
 
 def far_kernel(n_here, n_swap, here_at, here_later, swap_at, swap_later, meta, *refs):
@@ -278,7 +294,12 @@
 
             pltpu.make_async_copy(kv.at[i], kv.at[i], kv_sem.at[i]).wait()
             vt[...] = kv[i, BLK:, :].T
-            fold(ALL_TILES, g, q, kv.at[i, pl.ds(0, BLK), :], vt, acc_out, stat_out)
+
+            def pair(h, carry):
+                fold(PAIR_TILES, g, q, kv.at[i, pl.ds(0, BLK), :], vt, acc_out, stat_out, 2 * h)
+                return carry
+
+            lax.fori_loop(0, GROUP // 2, pair, 0)
             seen[g] = seen[g] + 1
 
             @pl.when(jnp.logical_and(seen[g] == here[g], later[g] == 0))
@@ -337,7 +358,7 @@
     any_spec, vmem_spec = pl.BlockSpec(memory_space=ANY), pl.BlockSpec(memory_space=VMEM)
     state = (
         jax.ShapeDtypeStruct((KVH, GROUP, HD, BLK), jnp.float32),
-        jax.ShapeDtypeStruct((KVH, 2 * GROUP, BLK), jnp.float32),
+        jax.ShapeDtypeStruct((KVH, 2 * GROUP, 1, BLK), jnp.float32),
         jax.ShapeDtypeStruct((BLK, QH * HD), jnp.bfloat16),
     )
     params = pltpu.CompilerParams(vmem_limit_bytes=16 << 20)
@@ -419,7 +440,7 @@
         a, b = groups[here] if here is not None else (0, 0)
         a0, b0 = groups[swaps] if swaps is not None else (0, 0)
         here_end = max(b, b0)
-        swap_end = b0 if swaps is not None else (groups[here - 1][1] if here else 0)
+        swap_end = b0 if swaps is not None else a
         n_here = b - a
         pieces = n_here + b0 - a0
         others = [swapped[swaps]] if swaps is not None else []
@@ -462,18 +483,16 @@
     send(3)
     last = len(groups) - 1
     acc, stat, out = far(0, None, acc, stat, out)
-    for n in range(1, last):
+    acc, stat, out = far(None, 0, acc, stat, out)
+    for n in range(1, last + 1):
         stat = pack(n, stat)
         if n == last - 2:
             a, b = groups[last]
             stat, *final = cut(a, b - a, stat)
             sent += final
             send(last)
-        acc, stat, out = far(n, n - 1, acc, stat, out)
-    acc, stat, out = far(None, last - 1, acc, stat, out)
-    stat = pack(last, stat)
-    acc, stat, out = far(last, None, acc, stat, out)
-    acc, stat, out = far(None, last, acc, stat, out)
+        acc, stat, out = far(n, None, acc, stat, out)
+        acc, stat, out = far(None, n, acc, stat, out)
     return out
 
 

time: 135 us -> 138 us (1.022)
  the two profiles are of different devices: /device:TPU:28 before, /device:TPU:30 now
where the time goes in v5:
time: 138 us; the launch traced here: 136 us
  Pallas kernels  84.6 us (61%)
  starting transfers between devices  29.6 us (21%)
  waiting for transfers between devices  14.3 us (10%)
  local copies, waits for them, and re-layouts  6.4 us (5%)
    pallas_call x10, Pallas kernels, far(): pl.pallas_call(functools.partial(far_kernel, n_here, len(others), here_at...  64.1 us
    ppermute x15, starting transfers between devices, send(): landed[j] = lax.ppermute(sent[j], 'ctx', order[j])  19.4 us
    pallas_call x2, Pallas kernels, inner(): pl.pallas_call(functools.partial(kernel, local_at, (here_at, end), first)...  18.2 us
    ppermute x15, waiting for transfers between devices, send(): landed[j] = lax.ppermute(sent[j], 'ctx', order[j])  13.1 us
    ppermute x5, starting transfers between devices, pack(): swapped.append(lax.ppermute(joined, 'head', swap))  9.67 us
    unnamed x12, local copies, waits for them, and re-layouts  4.64 us
  transfers between devices with their start and end apart: 22, of which 2 were waited for; matrix products, arithmetic and copies ran while one was open for 2% of the time, Pallas kernels for 56%

profile of v5, /device:TPU:30, one launch (start us, length us, event | category | flops | bytes accessed | tf_op | source)
XLA Modules:
  0.0 136.4 jit_solution(5416101047129217389)
XLA Ops:
  0.0 0.5 collective-permute-start.1
  0.5 0.7 slice.12
  1.2 0.3 compare_reduce_fusion
  1.6 0.1 copy.49
  1.7 0.1 select_reduce_fusion.1
  1.8 0.1 reduce_max.44
  1.8 0.1 reduce_max.45
  2.0 0.7 constant_dynamic-slice_fusion
  2.7 0.1 slice_bitcast_fusion
  2.8 0.2 select_reduce_fusion
  2.9 0.1 compare_reduce_fusion.1
  3.0 0.1 select_reduce_fusion.2
  3.1 0.1 concatenate.3.meta
  3.2 0.0 collective-permute-done.ok.okey
  3.2 1.2 collective-permute-done.1.ov.ovalue
  4.4 1.2 copy-done
  5.6 1.2 copy-done.2
  6.8 1.1 cut.2
  7.9 1.3 collective-permute-start.9
  9.2 1.3 collective-permute-start.10
  10.5 1.3 collective-permute-start.11
  11.8 1.3 collective-permute-start.12
  13.1 1.3 collective-permute-start.6
  14.4 0.0 copy-start.4
  14.4 2.2 %copy-done.4 = bf16[512,4096]{1,0:T(8,128)(2,1)S(1)} copy-done((bf16[512,4096]{1,0:T(8,128)(2,1)S(1)}, bf16[512,4096]{1,0:T(8,128)(2,1)}, u32[]{:S(2)}) %copy-start.4) | copy-done | bytes 4194328
  16.6 16.0 %own.1 = (f32[8,4,128,512]{3,2,1,0:T(8,128)S(1)}, f32[8,8,1,512]{3,2,1,0:T(1,128)S(1)}, bf16[512,4096]{1,0:T(8,128)(2,1)}, bf16[1024,128]{1,0:T(8,128)(2,1)S(1)}...) custom-call(s32[54]{0:T(128)S(1)} %concatenate.3.meta, ...), custom_call_target="tpu_custom_call" | custom-call | bytes 1024 | tf_op jit(solution)/shard_map/own/pallas_call | solution.py:388
  32.6 0.0 collective-permute-done.9.refs_0_
  32.6 1.3 collective-permute-start.7
  33.9 1.3 collective-permute-start.8
  35.2 0.0 collective-permute-done.11.refs_2_
  35.2 1.3 collective-permute-start.2
  36.5 0.0 collective-permute-done.12.refs_3_
  36.5 0.1 pack.5
  36.6 0.2 collective-permute-start.13
  36.8 2.3 %near.1 = (f32[8,4,128,512]{3,2,1,0:T(8,128)S(1)}, f32[8,8,1,512]{3,2,1,0:T(1,128)S(1)}, bf16[512,4096]{1,0:T(8,128)(2,1)}, bf16[1024,128]{1,0:T(8,128)(2,1)S(1)}, bf16[1024,128]{1,0:T(8,128)(2,1)S(1)}) custom-call(s32[54]{0:T(128)S(1)} %concatenate.3.meta, ...), custom_call_target="tpu_custom_call", output_to_operand_aliasing={{0}: (6, {}), {1}: (7, {}), {2}: (8, {})} | custom-call | bytes 1024 | tf_op jit(solution)/shard_map/near/pallas_call | solution.py:388
  39.1 6.3 %far.10 = (f32[8,4,128,512]{3,2,1,0:T(8,128)S(1)}, f32[8,8,1,512]{3,2,1,0:T(1,128)S(1)}, bf16[512,4096]{1,0:T(8,128)(2,1)}) custom-call(s32[54]{0:T(128)S(1)} %concatenate.3.meta, bf16[1024,128]{1,0:T(8,128)(2,1)S(1)} %collective-permute-done.9.refs_0_, ...), custom_call_target="tpu_custom_call", output_to_operand_aliasing={{0}: (6, {}), {1}: (7, {}), {2}: (8, {})} | custom-call | flops 17179869184 | bytes 8388608 | tf_op jit(solution)/shard_map/far/pallas_call | solution.py:448
  45.5 0.0 collective-permute-done.13.refs_0_
  45.5 1.3 collective-permute-start.3
  46.8 5.4 %far.11 = (f32[8,4,128,512]{3,2,1,0:T(8,128)S(1)}, f32[8,8,1,512]{3,2,1,0:T(1,128)S(1)}, bf16[512,4096]{1,0:T(8,128)(2,1)}) custom-call(s32[54]{0:T(128)S(1)} %concatenate.3.meta, bf16[4096,128]{1,0:T(8,128)(2,1)S(1)} %collective-permute-done.13.refs_0_, bf16[512,4096]{1,0:T(8,128)(2,1)S(1)} %copy-done.5, ...), custom_call_target="tpu_custom_call", output_to_operand_aliasing={{0}: (3, {}), {1}: (4, {}), {2}: (5, {})} | custom-call | flops 17179869184 | bytes 8388608 | tf_op jit(solution)/shard_map/far/pallas_call | solution.py:448
  52.2 0.0 collective-permute-done.6.refs_0_
  52.2 1.3 collective-permute-start.4
  53.5 13.1 %collective-permute-done.7.refs_1_ = bf16[1024,128]{1,0:T(8,128)(2,1)S(1)} collective-permute-done((bf16[1024,128]{1,0:T(8,128)(2,1)S(1)}, bf16[1024,128]{1,0:T(8,128)(2,1)S(1)}, u32[]{:S(2)}, u32[]{:S(2)}) %collective-permute-start.7) | collective-permute-done | bytes 262176 | tf_op jit(solution)/shard_map/ppermute | solution.py:421
  66.6 1.3 collective-permute-start.5
  67.9 0.1 pack.6
  68.0 6.9 %collective-permute-start.14 = (bf16[3072,128]{1,0:T(8,128)(2,1)S(1)}, bf16[3072,128]{1,0:T(8,128)(2,1)S(1)}, u32[]{:S(2)}, u32[]{:S(2)}) collective-permute-start(bf16[3072,128]{1,0:T(8,128)(2,1)S(1)} %get-tuple-element.88), channel_id=1, source_target_pairs={{0,1},{1,0},{2,3},{3,2},{4,5},{5,4},{6,7},{7,6},{8,9},{9,8},{10,11... | collective-permute-start | bytes 2359304 | tf_op jit(solution)/shard_map/ppermute | solution.py:436
  74.9 4.2 %far.12 = (f32[8,4,128,512]{3,2,1,0:T(8,128)S(1)}, f32[8,8,1,512]{3,2,1,0:T(1,128)S(1)}, bf16[512,4096]{1,0:T(8,128)(2,1)}) custom-call(s32[54]{0:T(128)S(1)} %concatenate.3.meta, bf16[1024,128]{1,0:T(8,128)(2,1)S(1)} %collective-permute-done.6.refs_0_, ...), custom_call_target="tpu_custom_call", output_to_operand_aliasing={{0}: (5, {}), {1}: (6, {}), {2}: (7, {})} | custom-call | flops 12884901888 | bytes 6291456 | tf_op jit(solution)/shard_map/far/pallas_call | solution.py:448
  79.1 1.3 collective-permute-start.17
  80.4 8.1 %far.13 = (f32[8,4,128,512]{3,2,1,0:T(8,128)S(1)}, f32[8,8,1,512]{3,2,1,0:T(1,128)S(1)}, bf16[512,4096]{1,0:T(8,128)(2,1)}) custom-call(s32[54]{0:T(128)S(1)} %concatenate.3.meta, bf16[3072,128]{1,0:T(8,128)(2,1)S(1)} %collective-permute-done.14.refs_0_, bf16[512,4096]{1,0:T(8,128)(2,1)S(1)} %copy-done.5, ...), custom_call_target="tpu_custom_call", output_to_operand_aliasing={{0}: (3, {}), {1}: (4, {}), {2}: (5, {})} | custom-call | flops 12884901888 | bytes 6291456 | tf_op jit(solution)/shard_map/far/pallas_call | solution.py:448
  88.5 1.3 collective-permute-start.18
  89.9 0.1 pack.7
  90.0 0.7 cut.3
  90.7 1.3 collective-permute-start.15
  92.0 1.3 collective-permute-start.16
  93.3 2.4 %collective-permute-start.19 = (bf16[4096,128]{1,0:T(8,128)(2,1)S(1)}, bf16[4096,128]{1,0:T(8,128)(2,1)S(1)}, u32[]{:S(2)}, u32[]{:S(2)}) collective-permute-start(bf16[4096,128]{1,0:T(8,128)(2,1)S(1)} %get-tuple-element.101), channel_id=1, source_target_pairs={{0,1},{1,0},{2,3},{3,2},{4,5},{5,4},{6,7},{7,6},{8,9},{9,8},{10,11... | collective-permute-start | bytes 3145736 | tf_op jit(solution)/shard_map/ppermute | solution.py:436
  95.7 8.1 %far.14 = (f32[8,4,128,512]{3,2,1,0:T(8,128)S(1)}, f32[8,8,1,512]{3,2,1,0:T(1,128)S(1)}, bf16[512,4096]{1,0:T(8,128)(2,1)}) custom-call(s32[54]{0:T(128)S(1)} %concatenate.3.meta, bf16[1024,128]{1,0:T(8,128)(2,1)S(1)} %collective-permute-done.2.refs_0_, ...), custom_call_target="tpu_custom_call", output_to_operand_aliasing={{0}: (6, {}), {1}: (7, {}), {2}: (8, {})} | custom-call | flops 17179869184 | bytes 8388608 | tf_op jit(solution)/shard_map/far/pallas_call | solution.py:448
  103.8 6.0 %far.15 = (f32[8,4,128,512]{3,2,1,0:T(8,128)S(1)}, f32[8,8,1,512]{3,2,1,0:T(1,128)S(1)}, bf16[512,4096]{1,0:T(8,128)(2,1)}) custom-call(s32[54]{0:T(128)S(1)} %concatenate.3.meta, bf16[4096,128]{1,0:T(8,128)(2,1)S(1)} %collective-permute-done.19.refs_0_, bf16[512,4096]{1,0:T(8,128)(2,1)S(1)} %copy-done.5, ...), custom_call_target="tpu_custom_call", output_to_operand_aliasing={{0}: (3, {}), {1}: (4, {}), {2}: (5, {})} | custom-call | flops 17179869184 | bytes 8388608 | tf_op jit(solution)/shard_map/far/pallas_call | solution.py:448
  109.8 0.1 pack.8
  109.9 0.1 collective-permute-start.20
  110.0 7.6 %far.16 = (f32[8,4,128,512]{3,2,1,0:T(8,128)S(1)}, f32[8,8,1,512]{3,2,1,0:T(1,128)S(1)}, bf16[512,4096]{1,0:T(8,128)(2,1)}) custom-call(s32[54]{0:T(128)S(1)} %concatenate.3.meta, bf16[1024,128]{1,0:T(8,128)(2,1)S(1)} %collective-permute-done.17.refs_0_, ...), custom_call_target="tpu_custom_call", output_to_operand_aliasing={{0}: (4, {}), {1}: (5, {}), {2}: (6, {})} | custom-call | flops 8589934592 | bytes 4194304 | tf_op jit(solution)/shard_map/far/pallas_call | solution.py:448
  117.7 4.7 %far.17 = (f32[8,4,128,512]{3,2,1,0:T(8,128)S(1)}, f32[8,8,1,512]{3,2,1,0:T(1,128)S(1)}, bf16[512,4096]{1,0:T(8,128)(2,1)}) custom-call(s32[54]{0:T(128)S(1)} %concatenate.3.meta, bf16[2048,128]{1,0:T(8,128)(2,1)S(1)} %collective-permute-done.20.refs_0_, bf16[512,4096]{1,0:T(8,128)(2,1)S(1)} %copy-done.5, ...), custom_call_target="tpu_custom_call", output_to_operand_aliasing={{0}: (3, {}), {1}: (4, {}), {2}: (5, {})} | custom-call | flops 8589934592 | bytes 4194304 | tf_op jit(solution)/shard_map/far/pallas_call | solution.py:448
  122.4 0.1 pack.9
  122.5 0.1 collective-permute-start.21
  122.6 7.0 %far.18 = (f32[8,4,128,512]{3,2,1,0:T(8,128)S(1)}, f32[8,8,1,512]{3,2,1,0:T(1,128)S(1)}, bf16[512,4096]{1,0:T(8,128)(2,1)}) custom-call(s32[54]{0:T(128)S(1)} %concatenate.3.meta, bf16[1024,128]{1,0:T(8,128)(2,1)S(1)} %collective-permute-done.15.refs_0_, ...), custom_call_target="tpu_custom_call", output_to_operand_aliasing={{0}: (4, {}), {1}: (5, {}), {2}: (6, {})} | custom-call | flops 8589934592 | bytes 4194304 | tf_op jit(solution)/shard_map/far/pallas_call | solution.py:448
  129.6 6.7 %far.19 = (f32[8,4,128,512]{3,2,1,0:T(8,128)S(1)}, f32[8,8,1,512]{3,2,1,0:T(1,128)S(1)}, bf16[512,4096]{1,0:T(8,128)(2,1)}) custom-call(s32[54]{0:T(128)S(1)} %concatenate.3.meta, bf16[2048,128]{1,0:T(8,128)(2,1)S(1)} %collective-permute-done.21.refs_0_, bf16[512,4096]{1,0:T(8,128)(2,1)S(1)} %copy-done.5, ...), custom_call_target="tpu_custom_call", output_to_operand_aliasing={{0}: (3, {}), {1}: (4, {}), {2}: (5, {})} | custom-call | flops 8589934592 | bytes 4194304 | tf_op jit(solution)/shard_map/far/pallas_call | solution.py:448
  (26 shorter events, 0.1 us)
Async XLA Ops:
  0.0 3.2 %collective-permute-start = (bf16[512,1024]{1,0:T(8,128)(2,1)}, bf16[512,1024]{1,0:T(8,128)(2,1)S(1)}, u32[]{:S(2)}, u32[]{:S(2)}) collective-permute-start(bf16[512,1024]{1,0:T(8,128)(2,1)} %key.3), channel_id=1, source_target_pairs={{0,1},{1,0},{2,3},{3,2},{4,5},{5,4},{6,7},{7,6},{8,9},{9,8},{10,11... | collective-permute-start | bytes 3145736 | tf_op jit(solution)/shard_map/ppermute | solution.py:330
  0.0 4.4 %collective-permute-start.1 = (bf16[512,1024]{1,0:T(8,128)(2,1)}, bf16[512,1024]{1,0:T(8,128)(2,1)S(1)}, u32[]{:S(2)}, u32[]{:S(2)}) collective-permute-start(bf16[512,1024]{1,0:T(8,128)(2,1)} %value.3), channel_id=1, source_target_pairs={{0,1},{1,0},{2,3},{3,2},{4,5},{5,4},{6,7},{7,6},{8,9},{9,8},{10,11... | collective-permute-start | bytes 3145736 | tf_op jit(solution)/shard_map/ppermute | solution.py:330
  4.4 1.2 copy-start
  5.6 1.2 copy-start.2
  6.8 7.6 %copy-start.1 = (bf16[512,1024]{1,0:T(8,128)(2,1)S(1)}, bf16[512,1024]{1,0:T(8,128)(2,1)}, u32[]{:S(2)}) copy-start(bf16[512,1024]{1,0:T(8,128)(2,1)} %key.3) | copy-start | bytes 3145732
  6.8 7.6 %copy-start.3 = (bf16[512,1024]{1,0:T(8,128)(2,1)S(1)}, bf16[512,1024]{1,0:T(8,128)(2,1)}, u32[]{:S(2)}) copy-start(bf16[512,1024]{1,0:T(8,128)(2,1)} %value.3) | copy-start | bytes 3145732
  7.9 24.7 %collective-permute-start.9 = (bf16[1024,128]{1,0:T(8,128)(2,1)S(1)}, bf16[1024,128]{1,0:T(8,128)(2,1)S(1)}, u32[]{:S(2)}, u32[]{:S(2)}) collective-permute-start(bf16[1024,128]{1,0:T(8,128)(2,1)S(1)} %get-tuple-element.72), channel_id=1, source_target_pairs={{0,16},{2,18},{4,20},{6,22},{8,24},{10,26},{12,28},{14,30},{1,17},... | collective-permute-start | bytes 786440 | tf_op jit(solution)/shard_map/ppermute | solution.py:421
  9.2 24.7 %collective-permute-start.10 = (bf16[1024,128]{1,0:T(8,128)(2,1)S(1)}, bf16[1024,128]{1,0:T(8,128)(2,1)S(1)}, u32[]{:S(2)}, u32[]{:S(2)}) collective-permute-start(bf16[1024,128]{1,0:T(8,128)(2,1)S(1)} %get-tuple-element.73), channel_id=1, source_target_pairs={{0,2},{4,6},{8,10},{12,14},{16,18},{20,22},{24,26},{28,30},{1,3},{... | collective-permute-start | bytes 786440 | tf_op jit(solution)/shard_map/ppermute | solution.py:421
  10.5 24.7 %collective-permute-start.11 = (bf16[1024,128]{1,0:T(8,128)(2,1)S(1)}, bf16[1024,128]{1,0:T(8,128)(2,1)S(1)}, u32[]{:S(2)}, u32[]{:S(2)}) collective-permute-start(bf16[1024,128]{1,0:T(8,128)(2,1)S(1)} %get-tuple-element.74), channel_id=1, source_target_pairs={{0,4},{2,6},{8,12},{10,14},{16,20},{18,22},{24,28},{26,30},{1,5},{... | collective-permute-start | bytes 786440 | tf_op jit(solution)/shard_map/ppermute | solution.py:421
  11.8 24.7 %collective-permute-start.12 = (bf16[1024,128]{1,0:T(8,128)(2,1)S(1)}, bf16[1024,128]{1,0:T(8,128)(2,1)S(1)}, u32[]{:S(2)}, u32[]{:S(2)}) collective-permute-start(bf16[1024,128]{1,0:T(8,128)(2,1)S(1)} %get-tuple-element.75), channel_id=1, source_target_pairs={{0,6},{2,4},{8,14},{10,12},{16,22},{18,20},{24,30},{26,28},{1,7},{... | collective-permute-start | bytes 786440 | tf_op jit(solution)/shard_map/ppermute | solution.py:421
  13.1 39.1 %collective-permute-start.6 = (bf16[1024,128]{1,0:T(8,128)(2,1)S(1)}, bf16[1024,128]{1,0:T(8,128)(2,1)S(1)}, u32[]{:S(2)}, u32[]{:S(2)}) collective-permute-start(bf16[1024,128]{1,0:T(8,128)(2,1)S(1)} %get-tuple-element.69), channel_id=1, source_target_pairs={{0,24},{2,26},{4,28},{6,30},{8,16},{10,18},{12,20},{14,22},{1,25},... | collective-permute-start | bytes 786440 | tf_op jit(solution)/shard_map/ppermute | solution.py:421
  14.4 2.2 %copy-start.4 = (bf16[512,4096]{1,0:T(8,128)(2,1)S(1)}, bf16[512,4096]{1,0:T(8,128)(2,1)}, u32[]{:S(2)}) copy-start(bf16[512,4096]{1,0:T(8,128)(2,1)} %refs_1_.9) | copy-start | bytes 12582916
  16.6 20.2 %copy-start.5 = (bf16[512,4096]{1,0:T(8,128)(2,1)S(1)}, bf16[512,4096]{1,0:T(8,128)(2,1)}, u32[]{:S(2)}) copy-start(bf16[512,4096]{1,0:T(8,128)(2,1)} %refs_1_.9) | copy-start | bytes 12582916
  32.6 34.0 %collective-permute-start.7 = (bf16[1024,128]{1,0:T(8,128)(2,1)S(1)}, bf16[1024,128]{1,0:T(8,128)(2,1)S(1)}, u32[]{:S(2)}, u32[]{:S(2)}) collective-permute-start(bf16[1024,128]{1,0:T(8,128)(2,1)S(1)} %get-tuple-element.70), channel_id=1, source_target_pairs={{0,18},{2,16},{4,22},{6,20},{8,26},{10,24},{12,30},{14,28},{1,19},... | collective-permute-start | bytes 786440 | tf_op jit(solution)/shard_map/ppermute | solution.py:421
  33.9 34.0 %collective-permute-start.8 = (bf16[1024,128]{1,0:T(8,128)(2,1)S(1)}, bf16[1024,128]{1,0:T(8,128)(2,1)S(1)}, u32[]{:S(2)}, u32[]{:S(2)}) collective-permute-start(bf16[1024,128]{1,0:T(8,128)(2,1)S(1)} %get-tuple-element.71), channel_id=1, source_target_pairs={{0,26},{2,24},{4,30},{6,28},{8,18},{10,16},{12,22},{14,20},{1,27},... | collective-permute-start | bytes 786440 | tf_op jit(solution)/shard_map/ppermute | solution.py:421
  35.2 53.3 %collective-permute-start.2 = (bf16[1024,128]{1,0:T(8,128)(2,1)S(1)}, bf16[1024,128]{1,0:T(8,128)(2,1)S(1)}, u32[]{:S(2)}, u32[]{:S(2)}) collective-permute-start(bf16[1024,128]{1,0:T(8,128)(2,1)S(1)} %get-tuple-element.65), channel_id=1, source_target_pairs={{0,20},{2,22},{4,16},{6,18},{8,28},{10,30},{12,24},{14,26},{1,21},... | collective-permute-start | bytes 786440 | tf_op jit(solution)/shard_map/ppermute | solution.py:421
  36.6 8.8 %collective-permute-start.13 = (bf16[4096,128]{1,0:T(8,128)(2,1)S(1)}, bf16[4096,128]{1,0:T(8,128)(2,1)S(1)}, u32[]{:S(2)}, u32[]{:S(2)}) collective-permute-start(bf16[4096,128]{1,0:T(8,128)(2,1)S(1)} %get-tuple-element.77), channel_id=1, source_target_pairs={{0,1},{1,0},{2,3},{3,2},{4,5},{5,4},{6,7},{7,6},{8,9},{9,8},{10,11... | collective-permute-start | bytes 3145736 | tf_op jit(solution)/shard_map/ppermute | solution.py:436
  45.5 44.4 %collective-permute-start.3 = (bf16[1024,128]{1,0:T(8,128)(2,1)S(1)}, bf16[1024,128]{1,0:T(8,128)(2,1)S(1)}, u32[]{:S(2)}, u32[]{:S(2)}) collective-permute-start(bf16[1024,128]{1,0:T(8,128)(2,1)S(1)} %get-tuple-element.66), channel_id=1, source_target_pairs={{0,28},{2,30},{4,24},{6,26},{8,20},{10,22},{12,16},{14,18},{1,29},... | collective-permute-start | bytes 786440 | tf_op jit(solution)/shard_map/ppermute | solution.py:421
  52.2 37.7 %collective-permute-start.4 = (bf16[1024,128]{1,0:T(8,128)(2,1)S(1)}, bf16[1024,128]{1,0:T(8,128)(2,1)S(1)}, u32[]{:S(2)}, u32[]{:S(2)}) collective-permute-start(bf16[1024,128]{1,0:T(8,128)(2,1)S(1)} %get-tuple-element.67), channel_id=1, source_target_pairs={{0,8},{2,10},{4,12},{6,14},{16,24},{18,26},{20,28},{22,30},{1,9},{... | collective-permute-start | bytes 786440 | tf_op jit(solution)/shard_map/ppermute | solution.py:421
  66.6 23.3 %collective-permute-start.5 = (bf16[1024,128]{1,0:T(8,128)(2,1)S(1)}, bf16[1024,128]{1,0:T(8,128)(2,1)S(1)}, u32[]{:S(2)}, u32[]{:S(2)}) collective-permute-start(bf16[1024,128]{1,0:T(8,128)(2,1)S(1)} %get-tuple-element.68), channel_id=1, source_target_pairs={{0,10},{2,8},{4,14},{6,12},{16,26},{18,24},{20,30},{22,28},{1,11},... | collective-permute-start | bytes 786440 | tf_op jit(solution)/shard_map/ppermute | solution.py:421
  68.0 11.2 %collective-permute-start.14 = (bf16[3072,128]{1,0:T(8,128)(2,1)S(1)}, bf16[3072,128]{1,0:T(8,128)(2,1)S(1)}, u32[]{:S(2)}, u32[]{:S(2)}) collective-permute-start(bf16[3072,128]{1,0:T(8,128)(2,1)S(1)} %get-tuple-element.88), channel_id=1, source_target_pairs={{0,1},{1,0},{2,3},{3,2},{4,5},{5,4},{6,7},{7,6},{8,9},{9,8},{10,11... | collective-permute-start | bytes 2359304 | tf_op jit(solution)/shard_map/ppermute | solution.py:436
  79.1 30.7 %collective-permute-start.17 = (bf16[1024,128]{1,0:T(8,128)(2,1)S(1)}, bf16[1024,128]{1,0:T(8,128)(2,1)S(1)}, u32[]{:S(2)}, u32[]{:S(2)}) collective-permute-start(bf16[1024,128]{1,0:T(8,128)(2,1)S(1)} %get-tuple-element.99), channel_id=1, source_target_pairs={{0,22},{2,20},{4,18},{6,16},{8,30},{10,28},{12,26},{14,24},{1,23},... | collective-permute-start | bytes 786440 | tf_op jit(solution)/shard_map/ppermute | solution.py:421
  88.5 21.3 %collective-permute-start.18 = (bf16[1024,128]{1,0:T(8,128)(2,1)S(1)}, bf16[1024,128]{1,0:T(8,128)(2,1)S(1)}, u32[]{:S(2)}, u32[]{:S(2)}) collective-permute-start(bf16[1024,128]{1,0:T(8,128)(2,1)S(1)} %get-tuple-element.100), channel_id=1, source_target_pairs={{0,12},{2,14},{4,8},{6,10},{16,28},{18,30},{20,24},{22,26},{1,13},... | collective-permute-start | bytes 786440 | tf_op jit(solution)/shard_map/ppermute | solution.py:421
  90.7 31.7 %collective-permute-start.15 = (bf16[1024,128]{1,0:T(8,128)(2,1)S(1)}, bf16[1024,128]{1,0:T(8,128)(2,1)S(1)}, u32[]{:S(2)}, u32[]{:S(2)}) collective-permute-start(bf16[1024,128]{1,0:T(8,128)(2,1)S(1)} %get-tuple-element.97), channel_id=1, source_target_pairs={{0,14},{2,12},{4,10},{6,8},{16,30},{18,28},{20,26},{22,24},{1,15},... | collective-permute-start | bytes 786440 | tf_op jit(solution)/shard_map/ppermute | solution.py:421
  92.0 30.4 %collective-permute-start.16 = (bf16[1024,128]{1,0:T(8,128)(2,1)S(1)}, bf16[1024,128]{1,0:T(8,128)(2,1)S(1)}, u32[]{:S(2)}, u32[]{:S(2)}) collective-permute-start(bf16[1024,128]{1,0:T(8,128)(2,1)S(1)} %get-tuple-element.98), channel_id=1, source_target_pairs={{0,30},{2,28},{4,26},{6,24},{8,22},{10,20},{12,18},{14,16},{1,31},... | collective-permute-start | bytes 786440 | tf_op jit(solution)/shard_map/ppermute | solution.py:421
  93.3 10.5 %collective-permute-start.19 = (bf16[4096,128]{1,0:T(8,128)(2,1)S(1)}, bf16[4096,128]{1,0:T(8,128)(2,1)S(1)}, u32[]{:S(2)}, u32[]{:S(2)}) collective-permute-start(bf16[4096,128]{1,0:T(8,128)(2,1)S(1)} %get-tuple-element.101), channel_id=1, source_target_pairs={{0,1},{1,0},{2,3},{3,2},{4,5},{5,4},{6,7},{7,6},{8,9},{9,8},{10,11... | collective-permute-start | bytes 3145736 | tf_op jit(solution)/shard_map/ppermute | solution.py:436
  109.9 7.7 %collective-permute-start.20 = (bf16[2048,128]{1,0:T(8,128)(2,1)S(1)}, bf16[2048,128]{1,0:T(8,128)(2,1)S(1)}, u32[]{:S(2)}, u32[]{:S(2)}) collective-permute-start(bf16[2048,128]{1,0:T(8,128)(2,1)S(1)} %get-tuple-element.109), channel_id=1, source_target_pairs={{0,1},{1,0},{2,3},{3,2},{4,5},{5,4},{6,7},{7,6},{8,9},{9,8},{10,11... | collective-permute-start | bytes 1572872 | tf_op jit(solution)/shard_map/ppermute | solution.py:436
  122.5 7.1 %collective-permute-start.21 = (bf16[2048,128]{1,0:T(8,128)(2,1)S(1)}, bf16[2048,128]{1,0:T(8,128)(2,1)S(1)}, u32[]{:S(2)}, u32[]{:S(2)}) collective-permute-start(bf16[2048,128]{1,0:T(8,128)(2,1)S(1)} %get-tuple-element.117), channel_id=1, source_target_pairs={{0,1},{1,0},{2,3},{3,2},{4,5},{5,4},{6,7},{7,6},{8,9},{9,8},{10,11... | collective-permute-start | bytes 1572872 | tf_op jit(solution)/shard_map/ppermute | solution.py:436

commit v6 on v4

--- a/solution.py
+++ b/solution.py
@@ -39,12 +39,12 @@
     level = [(a, a) for a in range(slow)]
     if (fast, slow) == (4, 4):
         two, one, zero = [(0, 2), (1, 3)], [(0, 3), (1, 2)], [(0, 1), (2, 3)]
-        order = [permute(two, 0), permute(level, 1), permute(level, 2), permute(level, 3)]
-        order += [permute(one, 0), permute(two, 1), permute(one, 1)]
-        order += [permute(two, 2), permute(one, 2), permute(zero, 0), permute(zero, 1)]
+        order = [permute(two, 0), permute(one, 0), permute(level, 1)]
+        order += [permute(two, 1), permute(one, 1), permute(zero, 0), permute(level, 2)]
+        order += [permute(two, 2), permute(one, 2), permute(zero, 1), permute(level, 3)]
         order += [permute(two, 3), permute(zero, 2), permute(zero, 3)]
         order += [permute(one, 3)]
-        edges = [0, 4, 7, 11, 14, 15]
+        edges = [0, 3, 7, 11, 14, 15]
     else:
         order = []
         for m in range(fast):
@@ -342,7 +342,7 @@
     )
     params = pltpu.CompilerParams(vmem_limit_bytes=16 << 20)
 
-    firsts = [0, groups[1][1], groups[2][1], groups[3][1]]
+    firsts = [0, groups[0][1], groups[1][1], groups[3][1]]
     counts = [b - a for a, b in zip(firsts[:-1], firsts[1:])]
     def cut(first, count, *through):
         return pl.pallas_call(
@@ -454,12 +454,13 @@
             name="far",
         )(meta, *landed[a:b], *others, queries, acc, stat, out)
 
-    for n in range(3):
-        send(n)
-    stat = pack(0, stat)
+    send(0)
+    send(1)
     acc, stat, out, *third = inner(near_kernel, "near", firsts[2], counts[2], acc, stat, out)
     sent += third
+    send(2)
     send(3)
+    stat = pack(0, stat)
     last = len(groups) - 1
     acc, stat, out = far(0, None, acc, stat, out)
     for n in range(1, last):

time: 135 us -> 142 us (1.052)
  starting transfers between devices: 28.1 us -> 42.5 us
  waiting for transfers between devices: 39.1 us -> 33.3 us
  Pallas kernels: 62.5 us -> 59.8 us
    ppermute x5, starting transfers between devices: 6.07 us -> 20.6 us  [pack(): swapped.append(lax.ppermute(joined, 'head', swap))]
    ppermute x15, waiting for transfers between devices: 37.9 us -> 32.1 us  [send(): landed[j] = lax.ppermute(sent[j], 'ctx', order[j])]
    pallas_call x7, Pallas kernels: 43.6 us -> 40.8 us  [far(): pl.pallas_call(functools.partial(far_kernel, n_here, len(others), here_at...]
  transfers between devices with their start and end apart: 22 -> 22, of which waited for: 5 -> 5; matrix products, arithmetic and copies ran while one was open for 2% -> 2% of each run, Pallas kernels for 43% -> 39%
where the time goes in v6:
time: 142 us; the launch traced here: 141 us
  Pallas kernels  59.8 us (42%)
  starting transfers between devices  42.5 us (30%)
  waiting for transfers between devices  33.3 us (23%)
  local copies, waits for them, and re-layouts  4.3 us (3%)
    pallas_call x7, Pallas kernels, far(): pl.pallas_call(functools.partial(far_kernel, n_here, len(others), here_at...  40.8 us
    ppermute x15, waiting for transfers between devices, send(): landed[j] = lax.ppermute(sent[j], 'ctx', order[j])  32.1 us
    ppermute x15, starting transfers between devices, send(): landed[j] = lax.ppermute(sent[j], 'ctx', order[j])  21.4 us
    ppermute x5, starting transfers between devices, pack(): swapped.append(lax.ppermute(joined, 'head', swap))  20.6 us
    pallas_call x2, Pallas kernels, inner(): pl.pallas_call(functools.partial(kernel, local_at, (here_at, end), first)...  17.1 us
  transfers between devices with their start and end apart: 22, of which 5 were waited for; matrix products, arithmetic and copies ran while one was open for 2% of the time, Pallas kernels for 39%

profile of v6, /device:TPU:28, one launch (start us, length us, event | category | flops | bytes accessed | tf_op | source)
XLA Modules:
  0.0 141.4 jit_solution(10691551603331302651)
XLA Ops:
  0.0 0.0 collective-permute-start
  0.0 0.5 collective-permute-start.1
  0.5 0.7 slice.12
  1.2 0.3 compare_reduce_fusion
  1.6 0.1 copy.40
  1.7 0.1 select_reduce_fusion.1
  1.8 0.1 reduce_max.44
  1.8 0.1 reduce_max.45
  2.0 0.7 constant_dynamic-slice_fusion
  2.7 0.1 slice_bitcast_fusion
  2.8 0.2 select_reduce_fusion
  2.9 0.1 compare_reduce_fusion.1
  3.0 0.1 select_reduce_fusion.2
  3.1 0.1 concatenate.3.meta
  3.2 0.0 collective-permute-done.ok.okey
  3.2 1.2 collective-permute-done.1.ov.ovalue
  4.4 1.3 copy-done.1
  5.7 1.2 copy-done.3
  6.9 0.8 cut.2
  7.7 1.3 collective-permute-start.10
  9.0 1.3 collective-permute-start.11
  10.3 3.3 %collective-permute-start.12 = (bf16[1024,128]{1,0:T(8,128)(2,1)S(1)}, bf16[1024,128]{1,0:T(8,128)(2,1)S(1)}, u32[]{:S(2)}, u32[]{:S(2)}) collective-permute-start(bf16[1024,128]{1,0:T(8,128)(2,1)S(1)} %get-tuple-element.69), channel_id=1, source_target_pairs={{0,2},{4,6},{8,10},{12,14},{16,18},{20,22},{24,26},{28,30},{1,3},{... | collective-permute-start | bytes 786440 | tf_op jit(solution)/shard_map/ppermute | solution.py:400
  13.7 14.4 %own.1 = (f32[8,4,128,512]{3,2,1,0:T(8,128)S(1)}, f32[8,8,512]{2,1,0:T(8,128)S(1)}, bf16[512,4096]{1,0:T(8,128)(2,1)}, bf16[1024,128]{1,0:T(8,128)(2,1)S(1)}, bf...) custom-call(s32[54]{0:T(128)S(1)} %concatenate.3.meta, ...), custom_call_target="tpu_custom_call" | custom-call | bytes 1024 | tf_op jit(solution)/shard_map/own/pallas_call | solution.py:367
  28.2 1.3 collective-permute-start.6
  29.5 1.3 collective-permute-start.7
  30.8 2.7 %near.1 = (f32[8,4,128,512]{3,2,1,0:T(8,128)S(1)}, f32[8,8,512]{2,1,0:T(8,128)S(1)}, bf16[512,4096]{1,0:T(8,128)(2,1)}, bf16[1024,128]{1,0:T(8,128)(2,1)S(1)}, b...) custom-call(s32[54]{0:T(128)S(1)} %concatenate.3.meta, ...), custom_call_target="tpu_custom_call", output_to_operand_aliasing={{0}: (6, {}), {1}: (7, {}), {2}: (8, {})} | custom-call | bytes 1024 | tf_op jit(solution)/shard_map/near/pallas_call | solution.py:367
  33.4 0.0 collective-permute-done.10.refs_0_
  33.4 1.3 collective-permute-start.8
  34.7 1.3 collective-permute-start.9
  36.0 0.0 collective-permute-done.12.refs_2_
  36.1 0.1 pack.5
  36.1 12.4 %collective-permute-start.13 = (bf16[3072,128]{1,0:T(8,128)(2,1)S(1)}, bf16[3072,128]{1,0:T(8,128)(2,1)S(1)}, u32[]{:S(2)}, u32[]{:S(2)}) collective-permute-start(bf16[3072,128]{1,0:T(8,128)(2,1)S(1)} %get-tuple-element.71), channel_id=1, source_target_pairs={{0,1},{1,0},{2,3},{3,2},{4,5},{5,4},{6,7},{7,6},{8,9},{9,8},{10,11... | collective-permute-start | bytes 2359304 | tf_op jit(solution)/shard_map/ppermute | solution.py:415
  48.5 3.9 %far.7 = (f32[8,4,128,512]{3,2,1,0:T(8,128)S(1)}, f32[8,8,512]{2,1,0:T(8,128)S(1)}, bf16[512,4096]{1,0:T(8,128)(2,1)}) custom-call(s32[54]{0:T(128)S(1)} %concatenate.3.meta, bf16[1024,128]{1,0:T(8,128)(2,1)S(1)} %collective-permute-done.10.refs_0_, ...), custom_call_target="tpu_custom_call", output_to_operand_aliasing={{0}: (5, {}), {1}: (6, {}), {2}: (7, {})} | custom-call | flops 12884901888 | bytes 6291456 | tf_op jit(solution)/shard_map/far/pallas_call | solution.py:427
  52.4 1.0 collective-permute-done.6.refs_0_
  53.4 1.3 collective-permute-start.2
  54.7 0.0 collective-permute-done.7.refs_1_
  54.7 1.3 collective-permute-start.3
  56.0 0.0 collective-permute-done.8.refs_2_
  56.0 1.3 collective-permute-start.4
  57.3 1.3 collective-permute-start.5
  58.6 0.1 pack.6
  58.7 0.0 collective-permute-done.13.refs_4_
  58.7 0.1 collective-permute-start.18
  58.8 0.0 copy-start.2
  58.8 0.0 copy-start.4
  58.8 8.5 %far.8 = (f32[8,4,128,512]{3,2,1,0:T(8,128)S(1)}, f32[8,8,512]{2,1,0:T(8,128)S(1)}, bf16[512,4096]{1,0:T(8,128)(2,1)}) custom-call(s32[54]{0:T(128)S(1)} %concatenate.3.meta, bf16[1024,128]{1,0:T(8,128)(2,1)S(1)} %collective-permute-done.6.refs_0_, ...), custom_call_target="tpu_custom_call", output_to_operand_aliasing={{0}: (7, {}), {1}: (8, {}), {2}: (9, {})} | custom-call | flops 30064771072 | bytes 14680064 | tf_op jit(solution)/shard_map/far/pallas_call | solution.py:427
  67.3 16.9 %collective-permute-done.2.refs_0_ = bf16[1024,128]{1,0:T(8,128)(2,1)S(1)} collective-permute-done((bf16[1024,128]{1,0:T(8,128)(2,1)S(1)}, bf16[1024,128]{1,0:T(8,128)(2,1)S(1)}, u32[]{:S(2)}, u32[]{:S(2)}) %collective-permute-start.2) | collective-permute-done | bytes 262176 | tf_op jit(solution)/shard_map/ppermute | solution.py:400
  84.2 1.3 collective-permute-start.15
  85.5 1.3 collective-permute-start.16
  86.8 1.3 collective-permute-start.17
  88.2 0.1 pack.7
  88.3 0.6 cut.3
  88.9 1.3 collective-permute-start.14
  90.2 0.1 collective-permute-start.20
  90.3 11.4 %far.9 = (f32[8,4,128,512]{3,2,1,0:T(8,128)S(1)}, f32[8,8,512]{2,1,0:T(8,128)S(1)}, bf16[512,4096]{1,0:T(8,128)(2,1)}) custom-call(s32[54]{0:T(128)S(1)} %concatenate.3.meta, bf16[1024,128]{1,0:T(8,128)(2,1)S(1)} %collective-permute-done.2.refs_0_, ...), custom_call_target="tpu_custom_call", output_to_operand_aliasing={{0}: (7, {}), {1}: (8, {}), {2}: (9, {})} | custom-call | flops 34359738368 | bytes 16777216 | tf_op jit(solution)/shard_map/far/pallas_call | solution.py:427
  101.7 4.3 %collective-permute-done.16.refs_1_ = bf16[1024,128]{1,0:T(8,128)(2,1)S(1)} collective-permute-done((bf16[1024,128]{1,0:T(8,128)(2,1)S(1)}, bf16[1024,128]{1,0:T(8,128)(2,1)S(1)}, u32[]{:S(2)}, u32[]{:S(2)}) %collective-permute-start.16) | collective-permute-done | bytes 262176 | tf_op jit(solution)/shard_map/ppermute | solution.py:400
  106.0 9.9 %collective-permute-done.17.refs_2_ = bf16[1024,128]{1,0:T(8,128)(2,1)S(1)} collective-permute-done((bf16[1024,128]{1,0:T(8,128)(2,1)S(1)}, bf16[1024,128]{1,0:T(8,128)(2,1)S(1)}, u32[]{:S(2)}, u32[]{:S(2)}) %collective-permute-start.17) | collective-permute-done | bytes 262176 | tf_op jit(solution)/shard_map/ppermute | solution.py:400
  115.8 0.1 pack.8
  115.9 0.5 collective-permute-start.19
  116.4 8.7 %far.10 = (f32[8,4,128,512]{3,2,1,0:T(8,128)S(1)}, f32[8,8,512]{2,1,0:T(8,128)S(1)}, bf16[512,4096]{1,0:T(8,128)(2,1)}) custom-call(s32[54]{0:T(128)S(1)} %concatenate.3.meta, bf16[1024,128]{1,0:T(8,128)(2,1)S(1)} %collective-permute-done.15.refs_0_, ...), custom_call_target="tpu_custom_call", output_to_operand_aliasing={{0}: (6, {}), {1}: (7, {}), {2}: (8, {})} | custom-call | flops 30064771072 | bytes 14680064 | tf_op jit(solution)/shard_map/far/pallas_call | solution.py:427
  125.0 1.4 far.11
  126.5 7.6 %collective-permute-start.21 = (bf16[1024,128]{1,0:T(8,128)(2,1)S(1)}, bf16[1024,128]{1,0:T(8,128)(2,1)S(1)}, u32[]{:S(2)}, u32[]{:S(2)}) collective-permute-start(bf16[1024,128]{1,0:T(8,128)(2,1)S(1)} %get-tuple-element.99), channel_id=1, source_target_pairs={{0,1},{1,0},{2,3},{3,2},{4,5},{5,4},{6,7},{7,6},{8,9},{9,8},{10,11... | collective-permute-start | bytes 786440 | tf_op jit(solution)/shard_map/ppermute | solution.py:415
  134.1 3.6 %far.12 = (f32[8,4,128,512]{3,2,1,0:T(8,128)S(1)}, f32[8,8,512]{2,1,0:T(8,128)S(1)}, bf16[512,4096]{1,0:T(8,128)(2,1)}) custom-call(s32[54]{0:T(128)S(1)} %concatenate.3.meta, bf16[1024,128]{1,0:T(8,128)(2,1)S(1)} %collective-permute-done.14.refs_0_, bf16[512,4096]{1,0:T(8,128)(2,1)S(1)} %copy-done, ...), custom_call_target="tpu_custom_call", output_to_operand_aliasing={{0}: (3, {}), {1}: (4, {}), {2}: (5, {})} | custom-call | flops 4294967296 | bytes 2097152 | tf_op jit(solution)/shard_map/far/pallas_call | solution.py:427
  137.7 3.5 %far.13 = (f32[8,4,128,512]{3,2,1,0:T(8,128)S(1)}, f32[8,8,512]{2,1,0:T(8,128)S(1)}, bf16[512,4096]{1,0:T(8,128)(2,1)}) custom-call(s32[54]{0:T(128)S(1)} %concatenate.3.meta, bf16[1024,128]{1,0:T(8,128)(2,1)S(1)} %collective-permute-done.21.refs_0_, bf16[512,4096]{1,0:T(8,128)(2,1)S(1)} %copy-done, ...), custom_call_target="tpu_custom_call", output_to_operand_aliasing={{0}: (3, {}), {1}: (4, {}), {2}: (5, {})} | custom-call | flops 4294967296 | bytes 2097152 | tf_op jit(solution)/shard_map/far/pallas_call | solution.py:427
  (21 shorter events, 0.1 us)
Async XLA Ops:
  0.0 3.2 %collective-permute-start = (bf16[512,1024]{1,0:T(8,128)(2,1)}, bf16[512,1024]{1,0:T(8,128)(2,1)S(1)}, u32[]{:S(2)}, u32[]{:S(2)}) collective-permute-start(bf16[512,1024]{1,0:T(8,128)(2,1)} %key.3), channel_id=1, source_target_pairs={{0,1},{1,0},{2,3},{3,2},{4,5},{5,4},{6,7},{7,6},{8,9},{9,8},{10,11... | collective-permute-start | bytes 3145736 | tf_op jit(solution)/shard_map/ppermute | solution.py:309
  0.0 4.4 %collective-permute-start.1 = (bf16[512,1024]{1,0:T(8,128)(2,1)}, bf16[512,1024]{1,0:T(8,128)(2,1)S(1)}, u32[]{:S(2)}, u32[]{:S(2)}) collective-permute-start(bf16[512,1024]{1,0:T(8,128)(2,1)} %value.3), channel_id=1, source_target_pairs={{0,1},{1,0},{2,3},{3,2},{4,5},{5,4},{6,7},{7,6},{8,9},{9,8},{10,11... | collective-permute-start | bytes 3145736 | tf_op jit(solution)/shard_map/ppermute | solution.py:309
  3.2 10.5 %copy-start = (bf16[512,4096]{1,0:T(8,128)(2,1)S(1)}, bf16[512,4096]{1,0:T(8,128)(2,1)}, u32[]{:S(2)}) copy-start(bf16[512,4096]{1,0:T(8,128)(2,1)} %refs_1_.5) | copy-start | bytes 12582916
  4.4 1.3 copy-start.1
  5.7 1.2 copy-start.3
  7.7 25.7 %collective-permute-start.10 = (bf16[1024,128]{1,0:T(8,128)(2,1)S(1)}, bf16[1024,128]{1,0:T(8,128)(2,1)S(1)}, u32[]{:S(2)}, u32[]{:S(2)}) collective-permute-start(bf16[1024,128]{1,0:T(8,128)(2,1)S(1)} %get-tuple-element.67), channel_id=1, source_target_pairs={{0,16},{2,18},{4,20},{6,22},{8,24},{10,26},{12,28},{14,30},{1,17},... | collective-permute-start | bytes 786440 | tf_op jit(solution)/shard_map/ppermute | solution.py:400
  9.0 25.7 %collective-permute-start.11 = (bf16[1024,128]{1,0:T(8,128)(2,1)S(1)}, bf16[1024,128]{1,0:T(8,128)(2,1)S(1)}, u32[]{:S(2)}, u32[]{:S(2)}) collective-permute-start(bf16[1024,128]{1,0:T(8,128)(2,1)S(1)} %get-tuple-element.68), channel_id=1, source_target_pairs={{0,24},{2,26},{4,28},{6,30},{8,16},{10,18},{12,20},{14,22},{1,25},... | collective-permute-start | bytes 786440 | tf_op jit(solution)/shard_map/ppermute | solution.py:400
  10.3 25.7 %collective-permute-start.12 = (bf16[1024,128]{1,0:T(8,128)(2,1)S(1)}, bf16[1024,128]{1,0:T(8,128)(2,1)S(1)}, u32[]{:S(2)}, u32[]{:S(2)}) collective-permute-start(bf16[1024,128]{1,0:T(8,128)(2,1)S(1)} %get-tuple-element.69), channel_id=1, source_target_pairs={{0,2},{4,6},{8,10},{12,14},{16,18},{20,22},{24,26},{28,30},{1,3},{... | collective-permute-start | bytes 786440 | tf_op jit(solution)/shard_map/ppermute | solution.py:400
  28.2 25.2 %collective-permute-start.6 = (bf16[1024,128]{1,0:T(8,128)(2,1)S(1)}, bf16[1024,128]{1,0:T(8,128)(2,1)S(1)}, u32[]{:S(2)}, u32[]{:S(2)}) collective-permute-start(bf16[1024,128]{1,0:T(8,128)(2,1)S(1)} %get-tuple-element.63), channel_id=1, source_target_pairs={{0,18},{2,16},{4,22},{6,20},{8,26},{10,24},{12,30},{14,28},{1,19},... | collective-permute-start | bytes 786440 | tf_op jit(solution)/shard_map/ppermute | solution.py:400
  29.5 25.2 %collective-permute-start.7 = (bf16[1024,128]{1,0:T(8,128)(2,1)S(1)}, bf16[1024,128]{1,0:T(8,128)(2,1)S(1)}, u32[]{:S(2)}, u32[]{:S(2)}) collective-permute-start(bf16[1024,128]{1,0:T(8,128)(2,1)S(1)} %get-tuple-element.64), channel_id=1, source_target_pairs={{0,26},{2,24},{4,30},{6,28},{8,18},{10,16},{12,22},{14,20},{1,27},... | collective-permute-start | bytes 786440 | tf_op jit(solution)/shard_map/ppermute | solution.py:400
  33.4 22.5 %collective-permute-start.8 = (bf16[1024,128]{1,0:T(8,128)(2,1)S(1)}, bf16[1024,128]{1,0:T(8,128)(2,1)S(1)}, u32[]{:S(2)}, u32[]{:S(2)}) collective-permute-start(bf16[1024,128]{1,0:T(8,128)(2,1)S(1)} %get-tuple-element.65), channel_id=1, source_target_pairs={{0,8},{2,10},{4,12},{6,14},{16,24},{18,26},{20,28},{22,30},{1,9},{... | collective-permute-start | bytes 786440 | tf_op jit(solution)/shard_map/ppermute | solution.py:400
  34.7 22.5 %collective-permute-start.9 = (bf16[1024,128]{1,0:T(8,128)(2,1)S(1)}, bf16[1024,128]{1,0:T(8,128)(2,1)S(1)}, u32[]{:S(2)}, u32[]{:S(2)}) collective-permute-start(bf16[1024,128]{1,0:T(8,128)(2,1)S(1)} %get-tuple-element.66), channel_id=1, source_target_pairs={{0,4},{2,6},{8,12},{10,14},{16,20},{18,22},{24,28},{26,30},{1,5},{... | collective-permute-start | bytes 786440 | tf_op jit(solution)/shard_map/ppermute | solution.py:400
  36.1 22.6 %collective-permute-start.13 = (bf16[3072,128]{1,0:T(8,128)(2,1)S(1)}, bf16[3072,128]{1,0:T(8,128)(2,1)S(1)}, u32[]{:S(2)}, u32[]{:S(2)}) collective-permute-start(bf16[3072,128]{1,0:T(8,128)(2,1)S(1)} %get-tuple-element.71), channel_id=1, source_target_pairs={{0,1},{1,0},{2,3},{3,2},{4,5},{5,4},{6,7},{7,6},{8,9},{9,8},{10,11... | collective-permute-start | bytes 2359304 | tf_op jit(solution)/shard_map/ppermute | solution.py:415
  53.4 30.9 %collective-permute-start.2 = (bf16[1024,128]{1,0:T(8,128)(2,1)S(1)}, bf16[1024,128]{1,0:T(8,128)(2,1)S(1)}, u32[]{:S(2)}, u32[]{:S(2)}) collective-permute-start(bf16[1024,128]{1,0:T(8,128)(2,1)S(1)} %get-tuple-element.59), channel_id=1, source_target_pairs={{0,20},{2,22},{4,16},{6,18},{8,28},{10,30},{12,24},{14,26},{1,21},... | collective-permute-start | bytes 786440 | tf_op jit(solution)/shard_map/ppermute | solution.py:400
  54.7 30.8 %collective-permute-start.3 = (bf16[1024,128]{1,0:T(8,128)(2,1)S(1)}, bf16[1024,128]{1,0:T(8,128)(2,1)S(1)}, u32[]{:S(2)}, u32[]{:S(2)}) collective-permute-start(bf16[1024,128]{1,0:T(8,128)(2,1)S(1)} %get-tuple-element.60), channel_id=1, source_target_pairs={{0,28},{2,30},{4,24},{6,26},{8,20},{10,22},{12,16},{14,18},{1,29},... | collective-permute-start | bytes 786440 | tf_op jit(solution)/shard_map/ppermute | solution.py:400
  56.0 30.8 %collective-permute-start.4 = (bf16[1024,128]{1,0:T(8,128)(2,1)S(1)}, bf16[1024,128]{1,0:T(8,128)(2,1)S(1)}, u32[]{:S(2)}, u32[]{:S(2)}) collective-permute-start(bf16[1024,128]{1,0:T(8,128)(2,1)S(1)} %get-tuple-element.61), channel_id=1, source_target_pairs={{0,10},{2,8},{4,14},{6,12},{16,26},{18,24},{20,30},{22,28},{1,11},... | collective-permute-start | bytes 786440 | tf_op jit(solution)/shard_map/ppermute | solution.py:400
  57.3 30.8 %collective-permute-start.5 = (bf16[1024,128]{1,0:T(8,128)(2,1)S(1)}, bf16[1024,128]{1,0:T(8,128)(2,1)S(1)}, u32[]{:S(2)}, u32[]{:S(2)}) collective-permute-start(bf16[1024,128]{1,0:T(8,128)(2,1)S(1)} %get-tuple-element.62), channel_id=1, source_target_pairs={{0,6},{2,4},{8,14},{10,12},{16,22},{18,20},{24,30},{26,28},{1,7},{... | collective-permute-start | bytes 786440 | tf_op jit(solution)/shard_map/ppermute | solution.py:400
  58.7 31.5 %collective-permute-start.18 = (bf16[4096,128]{1,0:T(8,128)(2,1)S(1)}, bf16[4096,128]{1,0:T(8,128)(2,1)S(1)}, u32[]{:S(2)}, u32[]{:S(2)}) collective-permute-start(bf16[4096,128]{1,0:T(8,128)(2,1)S(1)} %get-tuple-element.85), channel_id=1, source_target_pairs={{0,1},{1,0},{2,3},{3,2},{4,5},{5,4},{6,7},{7,6},{8,9},{9,8},{10,11... | collective-permute-start | bytes 3145736 | tf_op jit(solution)/shard_map/ppermute | solution.py:415
  58.8 29.5 %copy-start.2 = (bf16[512,1024]{1,0:T(8,128)(2,1)S(1)}, bf16[512,1024]{1,0:T(8,128)(2,1)}, u32[]{:S(2)}) copy-start(bf16[512,1024]{1,0:T(8,128)(2,1)} %key.3) | copy-start | bytes 3145732
  58.8 29.5 %copy-start.4 = (bf16[512,1024]{1,0:T(8,128)(2,1)S(1)}, bf16[512,1024]{1,0:T(8,128)(2,1)}, u32[]{:S(2)}) copy-start(bf16[512,1024]{1,0:T(8,128)(2,1)} %value.3) | copy-start | bytes 3145732
  84.2 17.4 %collective-permute-start.15 = (bf16[1024,128]{1,0:T(8,128)(2,1)S(1)}, bf16[1024,128]{1,0:T(8,128)(2,1)S(1)}, u32[]{:S(2)}, u32[]{:S(2)}) collective-permute-start(bf16[1024,128]{1,0:T(8,128)(2,1)S(1)} %get-tuple-element.82), channel_id=1, source_target_pairs={{0,22},{2,20},{4,18},{6,16},{8,30},{10,28},{12,26},{14,24},{1,23},... | collective-permute-start | bytes 786440 | tf_op jit(solution)/shard_map/ppermute | solution.py:400
  85.5 20.4 %collective-permute-start.16 = (bf16[1024,128]{1,0:T(8,128)(2,1)S(1)}, bf16[1024,128]{1,0:T(8,128)(2,1)S(1)}, u32[]{:S(2)}, u32[]{:S(2)}) collective-permute-start(bf16[1024,128]{1,0:T(8,128)(2,1)S(1)} %get-tuple-element.83), channel_id=1, source_target_pairs={{0,12},{2,14},{4,8},{6,10},{16,28},{18,30},{20,24},{22,26},{1,13},... | collective-permute-start | bytes 786440 | tf_op jit(solution)/shard_map/ppermute | solution.py:400
  86.8 29.0 %collective-permute-start.17 = (bf16[1024,128]{1,0:T(8,128)(2,1)S(1)}, bf16[1024,128]{1,0:T(8,128)(2,1)S(1)}, u32[]{:S(2)}, u32[]{:S(2)}) collective-permute-start(bf16[1024,128]{1,0:T(8,128)(2,1)S(1)} %get-tuple-element.84), channel_id=1, source_target_pairs={{0,14},{2,12},{4,10},{6,8},{16,30},{18,28},{20,26},{22,24},{1,15},... | collective-permute-start | bytes 786440 | tf_op jit(solution)/shard_map/ppermute | solution.py:400
  88.9 37.5 %collective-permute-start.14 = (bf16[1024,128]{1,0:T(8,128)(2,1)S(1)}, bf16[1024,128]{1,0:T(8,128)(2,1)S(1)}, u32[]{:S(2)}, u32[]{:S(2)}) collective-permute-start(bf16[1024,128]{1,0:T(8,128)(2,1)S(1)} %get-tuple-element.81), channel_id=1, source_target_pairs={{0,30},{2,28},{4,26},{6,24},{8,22},{10,20},{12,18},{14,16},{1,31},... | collective-permute-start | bytes 786440 | tf_op jit(solution)/shard_map/ppermute | solution.py:400
  90.2 26.1 %collective-permute-start.20 = (bf16[4096,128]{1,0:T(8,128)(2,1)S(1)}, bf16[4096,128]{1,0:T(8,128)(2,1)S(1)}, u32[]{:S(2)}, u32[]{:S(2)}) collective-permute-start(bf16[4096,128]{1,0:T(8,128)(2,1)S(1)} %get-tuple-element.91), channel_id=1, source_target_pairs={{0,1},{1,0},{2,3},{3,2},{4,5},{5,4},{6,7},{7,6},{8,9},{9,8},{10,11... | collective-permute-start | bytes 3145736 | tf_op jit(solution)/shard_map/ppermute | solution.py:415
  115.9 9.2 %collective-permute-start.19 = (bf16[3072,128]{1,0:T(8,128)(2,1)S(1)}, bf16[3072,128]{1,0:T(8,128)(2,1)S(1)}, u32[]{:S(2)}, u32[]{:S(2)}) collective-permute-start(bf16[3072,128]{1,0:T(8,128)(2,1)S(1)} %get-tuple-element.90), channel_id=1, source_target_pairs={{0,1},{1,0},{2,3},{3,2},{4,5},{5,4},{6,7},{7,6},{8,9},{9,8},{10,11... | collective-permute-start | bytes 2359304 | tf_op jit(solution)/shard_map/ppermute | solution.py:415
  126.5 11.2 %collective-permute-start.21 = (bf16[1024,128]{1,0:T(8,128)(2,1)S(1)}, bf16[1024,128]{1,0:T(8,128)(2,1)S(1)}, u32[]{:S(2)}, u32[]{:S(2)}) collective-permute-start(bf16[1024,128]{1,0:T(8,128)(2,1)S(1)} %get-tuple-element.99), channel_id=1, source_target_pairs={{0,1},{1,0},{2,3},{3,2},{4,5},{5,4},{6,7},{7,6},{8,9},{9,8},{10,11... | collective-permute-start | bytes 786440 | tf_op jit(solution)/shard_map/ppermute | solution.py:415
